TPU v7x, 512 devices: a whole 4x4x16 slice. The times are simulated.
512 devices in a mesh: ens: 4 (over x), lat: 8 (over z_lo), lon: 16 (over z_hi, y, core).
Axes of the slice: x: 4, y: 4, z: 16 (z_hi: 2, z_lo: 8; z = z_hi * 8 + z_lo), core: 2. Of those that a mesh axis runs over, the one named last changes fastest.
Arguments:
- features: bfloat16 [4, 128, 128, 2048], P('ens', None, 'lat', 'lon'), may hold values from -21 to 21
- conv_weight: bfloat16 [128, 9, 128], replicated, may hold values from -0.1875 to 0.1875
- conv_bias: float32 [128], replicated, may hold values from -3 to 3
- out_weight: bfloat16 [69, 128], replicated, may hold values from -0.5 to 0.5
- out_bias: float32 [69], replicated, may hold values from -3 to 3
- var_weight: float32 [69], replicated, may hold values from 0.2 to 2
- target: float32 [69, 128, 2048], P(None, 'lat', 'lon'), may hold values from -6 to 6
Outputs:
- grad_features: bfloat16 [4, 128, 128, 2048], P('ens', None, 'lat', 'lon')
- grad_weight: float32 [128, 9, 128], P('lon')
All inputs are finite; a program needn't handle non-finite values.
Results may differ from a plain program's by a relative error of at most 0.038.
Values may be sent and summed in bfloat16 or wider, within the bound.
No kernel may reach another device: no remote copies, remote signals or barrier semaphores. Data moves between devices by JAX's collectives and lax.ppermute only.
A program may use at most 64 MiB of HBM per device.

v0:
```python
import math

import jax
import jax.numpy as jnp
from jax import lax
from jax.sharding import PartitionSpec as P

smoothing = 0.1


def padded_2(x, sides, width, wrap):
    for axis, dim in sides:
        peers, length = (lax.axis_size(axis), x.shape[dim])
        up = [(i, (i + 1) % peers) for i in range(peers if wrap else peers - 1)]
        down = [(j, i) for i, j in up]
        last = lax.slice_in_dim(x, length - width, length, axis=dim)
        initial = lax.slice_in_dim(x, 0, width, axis=dim)
        before = lax.ppermute(last, axis, up)
        after = lax.ppermute(initial, axis, down)
        x = jnp.concatenate([before, x, after], axis=dim)
    return x


def swapped(x, axis, bit):
    return lax.ppermute(x, axis, [(i, i ^ 1 << bit) for i in range(lax.axis_size(axis))])


def tap_offsets():
    return [(tap_index, tap_index // 3 - 1, tap_index % 3 - 1) for tap_index in range(9)]


def member_grad(own_values, others, truth_rows, var_weight, members):
    differences = own_values[None] - others
    pair_term = jnp.sum(
        differences / jnp.sqrt(differences * differences + smoothing * smoothing), axis=0
    )
    misfit = own_values - truth_rows
    fit_term = misfit / jnp.sqrt(misfit * misfit + smoothing * smoothing)
    scaled = var_weight[:, None, None] * (
        fit_term / members - pair_term / (members * (members - 1))
    )
    return scaled.astype(jnp.bfloat16)


def on_device(features, conv_weight, conv_bias, out_weight, out_bias, var_weight, target):
    hidden_field = features[0]
    channels, row_count, col_count = hidden_field.shape
    variables = out_weight.shape[0]
    members = lax.axis_size("ens")
    band_index = lax.axis_index("lat")
    band_total = lax.axis_size("lat")
    swap_bit = lax.axis_size("lon").bit_length() - 2
    widened = padded_2(hidden_field, (("lon", 2),), 1, True)
    padded = padded_2(widened, (("lat", 1),), 1, False)
    edge_rows = jnp.stack([padded[:, 1], padded[:, row_count]], axis=1)
    partner = swapped(edge_rows, "lon", swap_bit)
    north_row = jnp.where(band_index == 0, partner[:, 0], padded[:, 0])
    south_row = jnp.where(band_index == band_total - 1, partner[:, 1], padded[:, row_count + 1])
    padded = jnp.concatenate(
        [north_row[:, None], padded[:, 1 : row_count + 1], south_row[:, None]], axis=1
    )
    pre_act = jnp.zeros((channels, row_count, col_count), jnp.float32) + conv_bias[:, None, None]
    for tap_index, shift_row, shift_col in tap_offsets():
        tap_slice = padded[
            :, 1 + shift_row : 1 + shift_row + row_count, 1 + shift_col : 1 + shift_col + col_count
        ]
        pre_act = pre_act + jnp.einsum(
            "io,irc->orc",
            conv_weight[:, tap_index, :],
            tap_slice,
            preferred_element_type=jnp.float32,
        )
    sigmoid_z = jax.nn.sigmoid(pre_act)
    active = (pre_act * sigmoid_z).astype(jnp.bfloat16)
    result = jnp.dot(out_weight, active.reshape(channels, -1), preferred_element_type=jnp.float32)
    outputs = (result.reshape(variables, row_count, col_count) + out_bias[:, None, None]).astype(
        jnp.bfloat16
    )
    ensemble = lax.all_gather(outputs[None], "ens", axis=0, tiled=True).astype(jnp.float32)
    grad_out = member_grad(outputs.astype(jnp.float32), ensemble, target, var_weight, members)
    grad_act = jnp.einsum("vc,vrw->crw", out_weight, grad_out, preferred_element_type=jnp.float32)
    grad_pre = (grad_act * sigmoid_z * (1.0 + pre_act * (1.0 - sigmoid_z))).astype(jnp.bfloat16)
    grad_pad = jnp.zeros((channels, row_count + 2, col_count + 2), jnp.float32)
    weight_terms = []
    for tap_index, shift_row, shift_col in tap_offsets():
        tap_slice = padded[
            :, 1 + shift_row : 1 + shift_row + row_count, 1 + shift_col : 1 + shift_col + col_count
        ]
        weight_terms.append(
            jnp.einsum("irc,orc->io", tap_slice, grad_pre, preferred_element_type=jnp.float32)
        )
        contrib = jnp.einsum(
            "io,orc->irc",
            conv_weight[:, tap_index, :],
            grad_pre,
            preferred_element_type=jnp.float32,
        )
        grad_pad = grad_pad.at[
            :, 1 + shift_row : 1 + shift_row + row_count, 1 + shift_col : 1 + shift_col + col_count
        ].add(contrib)
    weight_term = jnp.stack(weight_terms, axis=1)
    rim_grads = jnp.stack([grad_pad[:, :, 0], grad_pad[:, :, -1]], axis=2)
    neighbours = padded_2(rim_grads, (("lon", 2),), 1, True)
    inner_grad = grad_pad[:, :, 1:-1]
    inner_grad = inner_grad.at[:, :, 0].add(neighbours[:, :, 0])
    inner_grad = inner_grad.at[:, :, -1].add(neighbours[:, :, 3])
    band_rims = jnp.stack([inner_grad[:, 0], inner_grad[:, -1]], axis=1)
    band_neighbours = padded_2(band_rims.astype(jnp.bfloat16), (("lat", 1),), 1, False).astype(
        band_rims.dtype
    )
    core_grad = inner_grad[:, 1:-1]
    core_grad = core_grad.at[:, 0].add(band_neighbours[:, 0])
    core_grad = core_grad.at[:, -1].add(band_neighbours[:, 3])
    north_send = jnp.where(band_index == 0, inner_grad[:, 0], 0.0)
    south_send = jnp.where(band_index == band_total - 1, inner_grad[:, -1], 0.0)
    returned = swapped(
        jnp.stack([north_send, south_send], axis=1).astype(jnp.bfloat16), "lon", swap_bit
    ).astype(jnp.float32)
    core_grad = core_grad.at[:, 0].add(returned[:, 0])
    core_grad = core_grad.at[:, -1].add(returned[:, 1])
    summed = lax.psum(weight_term.astype(jnp.bfloat16), ("ens", "lat"))
    share = lax.psum_scatter(summed, "lon", scatter_dimension=0, tiled=True).astype(jnp.float32)
    total_cells = members * row_count * band_total * col_count * lax.axis_size("lon")
    grad_weight = share / math.sqrt(total_cells)
    return (core_grad.astype(jnp.bfloat16)[None], grad_weight)


def solution(mesh):
    return jax.shard_map(
        on_device,
        mesh=mesh,
        in_specs=(P("ens", None, "lat", "lon"), P(), P(), P(), P(), P(), P(None, "lat", "lon")),
        out_specs=(P("ens", None, "lat", "lon"), P("lon", None, None)),
        check_vma=False,
    )
```

profile of v0, /device:TPU:0, one launch (start us, length us, event | category | flops | bytes accessed | tf_op | source)
XLA Modules:
  0.0 625.4 jit_solution(1539024863433689526)
XLA Ops:
  7.2 1.5 copy.31
  8.8 1.9 collective-permute-start
  10.7 14.5 %collective-permute-start.1 = (bf16[128,16,1]{0,2,1:T(2,128)(2,1)S(1)}, bf16[128,16,1]{0,2,1:T(2,128)(2,1)S(1)}, u32[]{:S(2)}, u32[]{:S(2)}) collective-permute-start(bf16[128,16,1]{0,2,1:T(2,128)(2,1)S(1)} %get-tuple-element.197), channel_id=1, source_target_pairs={{1,0},{2,1},{3,2},{4,3},{5,4},{6,5},{7,6},{8,7},{9,8},{10,9},{11,1... | collective-permute-start | bytes 12296 | tf_op jit(solution)/shard_map/ppermute | solution.py:19
  29.2 12.0 %collective-permute-start.2 = (bf16[128,2,130]{0,2,1:T(8,128)(2,1)S(1)}, bf16[128,2,130]{0,2,1:T(8,128)(2,1)S(1)}, u32[]{:S(2)}, u32[]{:S(2)}) collective-permute-start(bf16[128,2,130]{0,2,1:T(8,128)(2,1)S(1)} %pad_maximum_fusion.7), channel_id=1, source_target_pairs={{0,8},{1,9},{2,10},{3,11},{4,12},{5,13},{6,14},{7,15},{8,0},{9,1},... | collective-permute-start | bytes 199688 | tf_op jit(solution)/shard_map/ppermute | solution.py:25
  41.5 3.6 collective-permute-done.2
  47.6 1.5 multiply_convert_fusion
  50.7 1.3 dynamic-slice.133
  54.9 31.8 %all-gather.2.cloned.1.call-done = bf16[4,69,16,128]{3,2,1,0:T(8,128)(2,1)} async-done(((bf16[1,69,16,128]{3,2,1,0:T(8,128)(2,1)}), bf16[4,69,16,128]{3,2,1,0:T(8,128)(2,1)}) %all-gather.2.cloned.1.call-update) | async-done | bytes 1130512 | tf_op jit(solution)/shard_map/all_gather | solution.py:79
  86.7 1.9 multiply_reduce_fusion
  99.2 2.4 fusion.6
  101.6 3.5 scatter-add.51
  105.1 3.0 add_select_fusion
  108.1 3.3 scatter-add.54
  113.5 2.1 scatter-add.56
  116.7 2.1 scatter-add.59
  120.9 2.1 scatter-add.61
  124.1 2.1 scatter-add.64
  126.3 1.9 collective-permute-start.5
  129.3 14.5 %collective-permute-start.6 = (f32[128,18,1]{0,2,1:T(1,128)S(1)}, f32[128,18,1]{0,2,1:T(1,128)S(1)}, u32[]{:S(2)}, u32[]{:S(2)}) collective-permute-start(f32[128,18,1]{0,2,1:T(1,128)S(1)} %get-tuple-element.186), channel_id=1, source_target_pairs={{1,0},{2,1},{3,2},{4,3},{5,4},{6,5},{7,6},{8,7},{9,8},{10,9},{11,1... | collective-permute-start | bytes 27656 | tf_op jit(solution)/shard_map/ppermute | solution.py:19
  145.3 3.4 collective-permute-start.7
  150.1 11.9 %collective-permute-start.9 = (bf16[128,2,128]{0,2,1:T(8,128)(2,1)S(1)}, bf16[128,2,128]{0,2,1:T(8,128)(2,1)S(1)}, u32[]{:S(2)}, u32[]{:S(2)}) collective-permute-start(bf16[128,2,128]{0,2,1:T(8,128)(2,1)S(1)} %pad_maximum_fusion.8), channel_id=1, source_target_pairs={{0,8},{1,9},{2,10},{3,11},{4,12},{5,13},{6,14},{7,15},{8,0},{9,1},... | collective-permute-start | bytes 196616 | tf_op jit(solution)/shard_map/ppermute | solution.py:25
  162.1 3.2 collective-permute-done.9
  166.7 216.0 %all-reduce.4.cloned.1.call-done = bf16[128,9,128]{2,0,1:T(8,128)(2,1)} async-done(((bf16[128,9,128]{2,0,1:T(8,128)(2,1)}), bf16[128,9,128]{2,0,1:T(8,128)(2,1)}) %all-reduce.4.cloned.1.call-update) | async-done | bytes 294928
  383.4 234.5 %psum.8 = bf16[8,9,128]{2,0,1:T(8,128)(2,1)S(1)} all-reduce(bf16[8,9,128]{2,0,1:T(8,128)(2,1)S(1)} %constant_dynamic-slice_fusion), channel_id=1, replica_groups=mesh['ens'=4,'lat'=8,'lon'=16] {'ens','lat'}, use_global_device_ids=true, to_apply=%region_2.3 | all-reduce | flops 9216 | bytes 36864 | tf_op jit(solution)/shard_map/psum | solution.py:121
  (100 shorter events, 34.1 us)
Async XLA Ops:
  7.2 42.0 %copy-start = (bf16[69,128]{1,0:T(8,128)(2,1)S(1)}, bf16[69,128]{1,0:T(8,128)(2,1)}, u32[]{:S(2)}) copy-start(bf16[69,128]{1,0:T(8,128)(2,1)} %param.40) | copy-start | bytes 52996
  7.2 34.0 %copy-start.1 = (bf16[128,9,128]{2,0,1:T(8,128)(2,1)S(1)}, bf16[128,9,128]{2,0,1:T(8,128)(2,1)}, u32[]{:S(2)}) copy-start(bf16[128,9,128]{2,0,1:T(8,128)(2,1)} %param.38) | copy-start | bytes 884740
  7.2 79.5 %all-gather.2.cloned.1.call-start = ((), (), s32[]{:S(2)}) async-start(), calls=%async_computation | async-start | bytes 1413120 | tf_op jit(solution)/shard_map/all_gather | solution.py:79
  8.8 16.4 %collective-permute-start = (bf16[128,16,1]{0,2,1:T(2,128)(2,1)S(1)}, bf16[128,16,1]{0,2,1:T(2,128)(2,1)S(1)}, u32[]{:S(2)}, u32[]{:S(2)}) collective-permute-start(bf16[128,16,1]{0,2,1:T(2,128)(2,1)S(1)} %get-tuple-element.196), channel_id=1, source_target_pairs={{0,1},{1,2},{2,3},{3,4},{4,5},{5,6},{6,7},{7,8},{8,9},{9,10},{10,1... | collective-permute-start | bytes 12296 | tf_op jit(solution)/shard_map/ppermute | solution.py:18
  10.7 15.8 %collective-permute-start.1 = (bf16[128,16,1]{0,2,1:T(2,128)(2,1)S(1)}, bf16[128,16,1]{0,2,1:T(2,128)(2,1)S(1)}, u32[]{:S(2)}, u32[]{:S(2)}) collective-permute-start(bf16[128,16,1]{0,2,1:T(2,128)(2,1)S(1)} %get-tuple-element.197), channel_id=1, source_target_pairs={{1,0},{2,1},{3,2},{4,3},{5,4},{6,5},{7,6},{8,7},{9,8},{10,9},{11,1... | collective-permute-start | bytes 12296 | tf_op jit(solution)/shard_map/ppermute | solution.py:19
  25.2 22.1 %copy-start.4 = (bf16[128,16,1]{0,2,1:T(2,128)(2,1)}, bf16[128,16,1]{0,2,1:T(2,128)(2,1)S(1)}, u32[]{:S(2)}) copy-start(bf16[128,16,1]{0,2,1:T(2,128)(2,1)S(1)} %collective-permute-done) | copy-start | bytes 12292
  26.5 21.1 %copy-start.6 = (bf16[128,16,1]{0,2,1:T(2,128)(2,1)}, bf16[128,16,1]{0,2,1:T(2,128)(2,1)S(1)}, u32[]{:S(2)}) copy-start(bf16[128,16,1]{0,2,1:T(2,128)(2,1)S(1)} %collective-permute-done.1) | copy-start | bytes 12292
  26.5 14.9 %collective-permute-start.3 = (bf16[128,1,130]{0,2,1:T(8,128)(2,1)S(1)}, bf16[128,1,130]{0,2,1:T(8,128)(2,1)S(1)}, u32[]{:S(2)}, u32[]{:S(2)}) collective-permute-start(bf16[128,1,130]{0,2,1:T(8,128)(2,1)S(1)} %get-tuple-element.194), channel_id=1, source_target_pairs={{0,16},{16,32},{32,48},{48,64},{64,80},{80,96},{96,112},{1,17},{17... | collective-permute-start | bytes 99848 | tf_op jit(solution)/shard_map/ppermute | solution.py:18
  27.9 13.6 %collective-permute-start.4 = (bf16[128,1,130]{0,2,1:T(8,128)(2,1)S(1)}, bf16[128,1,130]{0,2,1:T(8,128)(2,1)S(1)}, u32[]{:S(2)}, u32[]{:S(2)}) collective-permute-start(bf16[128,1,130]{0,2,1:T(8,128)(2,1)S(1)} %get-tuple-element.195), channel_id=1, source_target_pairs={{16,0},{32,16},{48,32},{64,48},{80,64},{96,80},{112,96},{17,1},{33... | collective-permute-start | bytes 99848 | tf_op jit(solution)/shard_map/ppermute | solution.py:19
  29.2 15.9 %collective-permute-start.2 = (bf16[128,2,130]{0,2,1:T(8,128)(2,1)S(1)}, bf16[128,2,130]{0,2,1:T(8,128)(2,1)S(1)}, u32[]{:S(2)}, u32[]{:S(2)}) collective-permute-start(bf16[128,2,130]{0,2,1:T(8,128)(2,1)S(1)} %pad_maximum_fusion.7), channel_id=1, source_target_pairs={{0,8},{1,9},{2,10},{3,11},{4,12},{5,13},{6,14},{7,15},{8,0},{9,1},... | collective-permute-start | bytes 199688 | tf_op jit(solution)/shard_map/ppermute | solution.py:25
  45.7 0.7 copy-start.9
  49.6 4.4 copy-start.11
  50.6 332.0 %all-reduce.4.cloned.1.call-start = ((), (), s32[]{:S(2)}) async-start(), calls=%async_computation.1 | async-start | bytes 589824
  54.9 33.7 %copy-start.10 = (f32[69]{0:T(128)S(1)}, f32[69]{0:T(128)}, u32[]{:S(2)}) copy-start(f32[69]{0:T(128)} %param.42) | copy-start | bytes 832
  86.7 1.9 copy-start.2
  88.6 1.2 copy-start.12
  92.4 1.9 copy-start.5
  93.4 1.9 copy-start.3
  94.3 1.9 copy-start.7
  126.3 17.5 %collective-permute-start.5 = (f32[128,18,1]{0,2,1:T(1,128)S(1)}, f32[128,18,1]{0,2,1:T(1,128)S(1)}, u32[]{:S(2)}, u32[]{:S(2)}) collective-permute-start(f32[128,18,1]{0,2,1:T(1,128)S(1)} %get-tuple-element.187), channel_id=1, source_target_pairs={{0,1},{1,2},{2,3},{3,4},{4,5},{5,6},{6,7},{7,8},{8,9},{9,10},{10,1... | collective-permute-start | bytes 27656 | tf_op jit(solution)/shard_map/ppermute | solution.py:18
  129.3 15.8 %collective-permute-start.6 = (f32[128,18,1]{0,2,1:T(1,128)S(1)}, f32[128,18,1]{0,2,1:T(1,128)S(1)}, u32[]{:S(2)}, u32[]{:S(2)}) collective-permute-start(f32[128,18,1]{0,2,1:T(1,128)S(1)} %get-tuple-element.186), channel_id=1, source_target_pairs={{1,0},{2,1},{3,2},{4,3},{5,4},{6,5},{7,6},{8,7},{9,8},{10,9},{11,1... | collective-permute-start | bytes 27656 | tf_op jit(solution)/shard_map/ppermute | solution.py:19
  145.3 16.8 %collective-permute-start.7 = (bf16[128,1,128]{0,2,1:T(8,128)(2,1)S(1)}, bf16[128,1,128]{0,2,1:T(8,128)(2,1)S(1)}, u32[]{:S(2)}, u32[]{:S(2)}) collective-permute-start(bf16[128,1,128]{0,2,1:T(8,128)(2,1)S(1)} %get-tuple-element.191), channel_id=1, source_target_pairs={{0,16},{16,32},{32,48},{48,64},{64,80},{80,96},{96,112},{1,17},{17... | collective-permute-start | bytes 98312 | tf_op jit(solution)/shard_map/ppermute | solution.py:18
  148.7 13.3 %collective-permute-start.8 = (bf16[128,1,128]{0,2,1:T(8,128)(2,1)S(1)}, bf16[128,1,128]{0,2,1:T(8,128)(2,1)S(1)}, u32[]{:S(2)}, u32[]{:S(2)}) collective-permute-start(bf16[128,1,128]{0,2,1:T(8,128)(2,1)S(1)} %get-tuple-element.190), channel_id=1, source_target_pairs={{16,0},{32,16},{48,32},{64,48},{80,64},{96,80},{112,96},{17,1},{33... | collective-permute-start | bytes 98312 | tf_op jit(solution)/shard_map/ppermute | solution.py:19
  150.1 15.2 %collective-permute-start.9 = (bf16[128,2,128]{0,2,1:T(8,128)(2,1)S(1)}, bf16[128,2,128]{0,2,1:T(8,128)(2,1)S(1)}, u32[]{:S(2)}, u32[]{:S(2)}) collective-permute-start(bf16[128,2,128]{0,2,1:T(8,128)(2,1)S(1)} %pad_maximum_fusion.8), channel_id=1, source_target_pairs={{0,8},{1,9},{2,10},{3,11},{4,12},{5,13},{6,14},{7,15},{8,0},{9,1},... | collective-permute-start | bytes 196616 | tf_op jit(solution)/shard_map/ppermute | solution.py:25
  (1 other events, 0.7 us)
Sparse Core Ops, SparseCore 0:
  50.8 35.8 all-gather.1
  129.4 253.2 all-reduce.3
where the time goes:
time: 627 us; the launch traced here: 625 us
  waiting for transfers between devices  257 us (41%)
  blocking collectives  235 us (37%)
  starting transfers between devices  64.1 us (10%)
  matrix products  26.3 us (4%)
  local copies, waits for them, and re-layouts  22.9 us (4%)
  between operations  15.2 us (2%)
    psum x1, blocking collectives, on_device(): summed = lax.psum(weight_term.astype(jnp.bfloat16), ('ens', 'lat'))  235 us
    unnamed x3, waiting for transfers between devices  216 us
    all_gather x1, waiting for transfers between devices, on_device(): lax.all_gather(outputs[None], 'ens', axis=0, tiled=True).astype(jnp.float32)  31.8 us
    ppermute x4, starting transfers between devices, padded_2(): after = lax.ppermute(initial, axis, down)  31.5 us
    ppermute x2, starting transfers between devices, swapped(): lax.ppermute(x, axis, [(i, i ^ 1 << bit) for i in range(lax.axis_size(axi...  23.9 us
    scatter-add x7, local copies, waits for them, and re-layouts, on_device(): grad_pad = grad_pad.at[:, 1 + shift_row:1 + shift_row + row_count, 1 + sh...  15.3 us
    dot_general x9, matrix products, on_device(): jnp.einsum('io,orc->irc', conv_weight[:, tap_index, :], grad_pre, preferr...  12.8 us
  transfers between devices with their start and end apart: 12, of which 6 were waited for; matrix products, arithmetic and copies ran while one was open for 1% of the time, Pallas kernels for 0%

commit v1 on v0

v1 whole, which is shorter than its diff:
```python
import functools
import math

import jax
import jax.numpy as jnp
from jax import lax
from jax.experimental import pallas as pl
from jax.experimental.pallas import tpu as pltpu
from jax.sharding import PartitionSpec as P

smoothing = 0.1
LANES = 128


def dot(a, b, dims=(((1,), (0,)), ((), ()))):
    return lax.dot_general(a, b, dims, preferred_element_type=jnp.float32)


def forward_kernel(rows, x_ref, north_ref, south_ref, left_ref, right_ref, w_ref, b_ref, ow_ref, ob_ref,
                   out_ref, slope_ref, x3_ref):
    channels = x_ref.shape[0]
    lane = lax.broadcasted_iota(jnp.int32, (channels, LANES), 1)
    left_cols = left_ref[...].astype(jnp.float32)
    right_cols = right_ref[...].astype(jnp.float32)
    north = north_ref[...].astype(jnp.float32)
    south = south_ref[...].astype(jnp.float32)
    for row in range(rows + 2):
        if row == 0:
            block, before, after = north[:, :LANES], north[:, LANES : LANES + 1], north[:, LANES + 1 :]
        elif row == rows + 1:
            block, before, after = south[:, :LANES], south[:, LANES : LANES + 1], south[:, LANES + 1 :]
        else:
            block = x_ref[:, (row - 1) * LANES : row * LANES].astype(jnp.float32)
            before, after = left_cols[:, row - 1 : row], right_cols[:, row - 1 : row]
        west = jnp.where(lane == 0, before, pltpu.roll(block, 1, 1))
        east = jnp.where(lane == LANES - 1, after, pltpu.roll(block, LANES - 1, 1))
        cells = slice(row * LANES, (row + 1) * LANES)
        x3_ref[:channels, cells] = west.astype(jnp.bfloat16)
        x3_ref[channels : 2 * channels, cells] = block.astype(jnp.bfloat16)
        x3_ref[2 * channels :, cells] = east.astype(jnp.bfloat16)
    for pair in range(rows // 2):
        start = 2 * pair * LANES
        pre = b_ref[...] + jnp.zeros((channels, 2 * LANES), jnp.float32)
        for tap_row in range(3):
            begin = start + tap_row * LANES
            pre = pre + dot(w_ref[tap_row], x3_ref[:, begin : begin + 2 * LANES])
        sigmoid = 1.0 / (1.0 + jnp.exp(-pre))
        active = (pre * sigmoid).astype(jnp.bfloat16)
        slope_ref[:, start : start + 2 * LANES] = sigmoid * (1.0 + pre * (1.0 - sigmoid))
        result = dot(ow_ref[...], active) + ob_ref[...]
        out_ref[:, start : start + 2 * LANES] = result.astype(jnp.bfloat16)


def backward_kernel(rows, shares, members, own_ref, peer_refs, target_ref, vw_ref, owt_ref, slope_ref, x3_ref, wb_ref,
                    grad_ref, right_ref, left_ref, even_ref, odd_ref, g_ref):
    channels = slope_ref.shape[0]
    cells = rows * LANES
    eps = smoothing * smoothing

    def signed(d):
        return d * lax.rsqrt(d * d + eps)

    g_ref[:, : 2 * LANES] = jnp.zeros((channels, 2 * LANES), jnp.bfloat16)
    g_ref[:, 2 * LANES + cells :] = jnp.zeros((channels, 2 * LANES), jnp.bfloat16)
    for pair in range(rows // 2):
        here = slice(2 * pair * LANES, 2 * (pair + 1) * LANES)
        own = own_ref[:, here].astype(jnp.float32)
        total = jnp.zeros_like(own)
        for peer_ref in peer_refs:
            total = total + signed(own - peer_ref[:, here].astype(jnp.float32))
        fit = signed(own - target_ref[:, here])
        grad_out = vw_ref[...] * (fit / members - total / (members * (members - 1)))
        grad_act = dot(owt_ref[...], grad_out.astype(jnp.bfloat16))
        g_ref[:, 2 * LANES + here.start : 2 * LANES + here.stop] = (grad_act * slope_ref[:, here]).astype(jnp.bfloat16)

    grad_pre = g_ref[:, 2 * LANES : 2 * LANES + cells]
    terms = []
    for tap_row in range(3):
        terms.append(dot(x3_ref[:, tap_row * LANES : tap_row * LANES + cells], grad_pre, (((1,), (1,)), ((), ()))))
    size = channels // shares
    for parity, ref in ((0, even_ref), (1, odd_ref)):
        pieces = []
        for share in range(parity, shares, 2):
            for tap in range(9):
                begin = (tap % 3) * channels + share * size
                pieces.append(terms[tap // 3][begin : begin + size])
        ref[...] = jnp.concatenate(pieces, axis=0).astype(jnp.bfloat16)

    lane = lax.broadcasted_iota(jnp.int32, (channels, LANES), 1)
    right = jnp.zeros((channels, LANES), jnp.float32)
    left = jnp.zeros((channels, LANES), jnp.float32)
    for pair in range((rows + 2) // 2):
        start = 2 * pair * LANES
        spread = jnp.zeros((3 * channels, 2 * LANES), jnp.float32)
        for tap_row in range(3):
            begin = start + (2 - tap_row) * LANES
            spread = spread + dot(wb_ref[tap_row], g_ref[:, begin : begin + 2 * LANES])
        for half in range(2):
            row = 2 * pair + half
            part = slice(half * LANES, (half + 1) * LANES)
            to_west = spread[:channels, part]
            to_east = spread[2 * channels :, part]
            moved_west = pltpu.roll(to_west, LANES - 1, 1)
            moved_east = pltpu.roll(to_east, 1, 1)
            total = spread[channels : 2 * channels, part]
            total = total + jnp.where(lane == LANES - 1, 0.0, moved_west) + jnp.where(lane == 0, 0.0, moved_east)
            grad_ref[:, row * LANES : (row + 1) * LANES] = total
            left = jnp.where(lane == row, pltpu.roll(to_west, row, 1) if row else to_west, left)
            right = jnp.where(lane == row, pltpu.roll(to_east, row + 1, 1), right)
    left_ref[...] = left[:, : rows + 2]
    right_ref[...] = right[:, : rows + 2]


def ring_pairs(bands, loops):
    half = loops // 2
    pairs = []
    for band in range(bands):
        for loop in range(loops):
            if loop < half:
                goal = (band + 1, loop) if band + 1 < bands else (band, loop + half)
            else:
                goal = (band - 1, loop) if band > 0 else (band, loop - half)
            pairs.append((band * loops + loop, goal[0] * loops + goal[1]))
    return pairs, [(j, i) for i, j in pairs]


def flipped(size, bit):
    return [(i, i ^ bit) for i in range(size)]


def total_of(value, axis, bits):
    size = lax.axis_size(axis)
    parts = [value]
    for k in range(1, bits):
        parts.append(lax.ppermute(value, axis, flipped(size, k)))
    return parts


def butterfly(values):
    values = [v.astype(jnp.float32) for v in values]
    while len(values) > 1:
        values = [values[i] + values[i + 1] for i in range(0, len(values), 2)]
    return values[0]


def pallas(kernel, out_shape, scratch=(), flops=0, nbytes=0):
    return pl.pallas_call(
        kernel,
        out_shape=out_shape,
        scratch_shapes=list(scratch),
        compiler_params=pltpu.CompilerParams(vmem_limit_bytes=48 * 1024 * 1024),
        cost_estimate=pl.CostEstimate(flops=flops, bytes_accessed=nbytes, transcendentals=0),
    )


def on_device(features, conv_weight, conv_bias, out_weight, out_bias, var_weight, target):
    field = features[0]
    channels, rows, cols = field.shape
    variables = out_weight.shape[0]
    members = lax.axis_size("ens")
    bands, loops = lax.axis_size("lat"), lax.axis_size("lon")
    loop = lax.axis_index("lon")
    cells = rows * cols
    f32, bf16 = jnp.float32, jnp.bfloat16
    east_way = [(i, (i + 1) % loops) for i in range(loops)]
    west_way = [(j, i) for i, j in east_way]
    onward, back = ring_pairs(bands, loops)
    near = loop < loops // 2

    flat = field.reshape(channels, cells)
    left = lax.ppermute(field[:, :, cols - 1], "lon", east_way)
    right = lax.ppermute(field[:, :, 0], "lon", west_way)
    first = jnp.concatenate([field[:, 0], left[:, :1], right[:, :1]], axis=1)
    last = jnp.concatenate([field[:, rows - 1], left[:, rows - 1 :], right[:, rows - 1 :]], axis=1)
    got_on = lax.ppermute(jnp.where(near, last, first), ("lat", "lon"), onward)
    got_back = lax.ppermute(jnp.where(near, first, last), ("lat", "lon"), back)
    north = jnp.where(near, got_on, got_back)
    south = jnp.where(near, got_back, got_on)

    taps = conv_weight.reshape(channels, 3, 3, channels)
    w_forward = taps.transpose(1, 3, 2, 0).reshape(3, channels, 3 * channels)
    w_backward = taps.transpose(1, 2, 0, 3).reshape(3, 3 * channels, channels)
    truth = target.reshape(variables, cells)

    own, slope, x3 = pallas(
        functools.partial(forward_kernel, rows),
        (
            jax.ShapeDtypeStruct((variables, cells), bf16),
            jax.ShapeDtypeStruct((channels, cells), f32),
            jax.ShapeDtypeStruct((3 * channels, cells + 2 * cols), bf16),
        ),
        flops=2 * cells * channels * (9 * channels + variables),
    )(flat, north, south, left, right, w_forward, conv_bias[:, None], out_weight, out_bias[:, None])

    peers = total_of(own, "ens", members)[1:]

    def kernel(own_ref, p1, p2, p3, *rest):
        backward_kernel(rows, loops, members, own_ref, (p1, p2, p3), *rest)

    share_rows = 9 * channels // 2
    grad, rim_right, rim_left, even, odd = pallas(
        kernel,
        (
            jax.ShapeDtypeStruct((channels, cells + 2 * cols), f32),
            jax.ShapeDtypeStruct((channels, rows + 2), f32),
            jax.ShapeDtypeStruct((channels, rows + 2), f32),
            jax.ShapeDtypeStruct((share_rows, channels), bf16),
            jax.ShapeDtypeStruct((share_rows, channels), bf16),
        ),
        scratch=[pltpu.VMEM((channels, cells + 4 * cols), bf16)],
        flops=2 * cells * channels * (18 * channels + variables),
    )(own, *peers, truth, var_weight[:, None], out_weight.T, slope, x3, w_backward)

    is_odd = (loop % 2) == 1
    got = lax.ppermute(jnp.where(is_odd, even, odd), "lon", flipped(loops, 1))
    kept = jnp.where(is_odd, odd, even).astype(f32) + got.astype(f32)
    block = 9 * channels // loops

    from_left = lax.ppermute(rim_right.astype(bf16), "lon", east_way).astype(f32)
    from_right = lax.ppermute(rim_left.astype(bf16), "lon", west_way).astype(f32)
    grad3 = grad.reshape(channels, rows + 2, cols)
    grad3 = grad3 + jnp.pad(from_left[:, :, None], ((0, 0), (0, 0), (0, cols - 1)))
    grad3 = grad3 + jnp.pad(from_right[:, :, None], ((0, 0), (0, 0), (cols - 1, 0)))
    top, bottom = grad3[:, 0].astype(bf16), grad3[:, rows + 1].astype(bf16)
    got_back = lax.ppermute(jnp.where(near, top, bottom), ("lat", "lon"), back)
    got_on = lax.ppermute(jnp.where(near, bottom, top), ("lat", "lon"), onward)
    to_first = jnp.where(near, got_on, got_back).astype(f32)
    to_last = jnp.where(near, got_back, got_on).astype(f32)
    core = grad3[:, 1 : rows + 1]
    core = core + jnp.pad(to_first[:, None], ((0, 0), (0, rows - 1), (0, 0)))
    core = core + jnp.pad(to_last[:, None], ((0, 0), (rows - 1, 0), (0, 0)))
    grad_features = core.astype(bf16)[None]

    bit = loops // 2
    kept = kept.astype(bf16).reshape(loops // 2, block, channels)
    while bit > 1:
        mine = (loop // bit) % 2
        half = kept.shape[0] // 2
        send = jnp.where(mine == 1, kept[:half], kept[half:])
        hold = jnp.where(mine == 1, kept[half:], kept[:half])
        got = lax.ppermute(send, "lon", flipped(loops, bit))
        kept = (hold.astype(f32) + got.astype(f32)).astype(bf16)
        bit //= 2
    share = kept[0]
    share = butterfly(total_of(share, "ens", members)).astype(bf16)
    bit = 1
    while bit < bands:
        share = butterfly([share, lax.ppermute(share, "lat", flipped(bands, bit))]).astype(bf16 if 2 * bit < bands else f32)
        bit *= 2
    total_cells = members * cells * bands * loops
    grad_weight = (share / math.sqrt(total_cells)).reshape(9, channels // loops, channels).transpose(1, 0, 2)
    return grad_features, grad_weight


def solution(mesh):
    return jax.shard_map(
        on_device,
        mesh=mesh,
        in_specs=(P("ens", None, "lat", "lon"), P(), P(), P(), P(), P(), P(None, "lat", "lon")),
        out_specs=(P("ens", None, "lat", "lon"), P("lon", None, None)),
        check_vma=False,
    )
```

time: 627 us -> 234 us (0.37)
  the two profiles are of different devices: /device:TPU:0 before, /device:TPU:25 now
where the time goes in v1:
time: 234 us; the launch traced here: 233 us
  starting transfers between devices  85.7 us (37%)
  local copies, waits for them, and re-layouts  72.7 us (31%)
  waiting for transfers between devices  44.2 us (19%)
  other arithmetic  20.4 us (9%)
  Pallas kernels  8.33 us (4%)
    unnamed x32, local copies, waits for them, and re-layouts  20.2 us
    ppermute x6, starting transfers between devices, total_of(): parts.append(lax.ppermute(value, axis, flipped(size, k)))  17.9 us
    ppermute x1, starting transfers between devices, on_device(): left = lax.ppermute(field[:, :, cols - 1], 'lon', east_way)  15.7 us
    ppermute x3, waiting for transfers between devices, on_device(): got = lax.ppermute(send, 'lon', flipped(loops, bit))  15.5 us
    slice x2, local copies, waits for them, and re-layouts, on_device(): field[:, rows - 1]  13.7 us
    ppermute x1, starting transfers between devices, on_device(): lax.ppermute(rim_right.astype(bf16), 'lon', east_way).astype(f32)  11.8 us
    ppermute x1, waiting for transfers between devices, on_device(): got_on = lax.ppermute(jnp.where(near, last, first), ('lat', 'lon'), onward)  11.2 us
    ppermute x3, starting transfers between devices, on_device(): got = lax.ppermute(send, 'lon', flipped(loops, bit))  11.1 us
  transfers between devices with their start and end apart: 21, of which 7 were waited for; matrix products, arithmetic and copies ran while one was open for 34% of the time, Pallas kernels for 0%

profile of v1, /device:TPU:25, one launch (start us, length us, event | category | flops | bytes accessed | tf_op | source)
XLA Modules:
  0.0 232.5 jit_solution(6465376354350809125)
XLA Ops:
  0.6 7.3 %copy.81 = bf16[1,128,16,128]{2,1,3,0:T(8,128)(2,1)} copy(bf16[1,128,16,128]{3,2,1,0:T(8,128)(2,1)} %param.7) | data formatting | bytes 1048576 | tf_op args[0]
  8.7 15.7 %collective-permute-start = (bf16[128,16]{1,0:T(8,128)(2,1)S(1)}, bf16[128,16]{1,0:T(8,128)(2,1)S(1)}, u32[]{:S(2)}, u32[]{:S(2)}) collective-permute-start(bf16[128,16]{1,0:T(8,128)(2,1)S(1)} %get-tuple-element.34), channel_id=1, source_target_pairs={{0,1},{1,2},{2,3},{3,4},{4,5},{5,6},{6,7},{7,8},{8,9},{9,10},{10,1... | collective-permute-start | bytes 12296 | tf_op jit(solution)/shard_map/ppermute | solution.py:171
  26.3 7.5 %fusion.6 = (bf16[128,1,128]{1,0,2:T(8,128)(2,1)}, bf16[128,1,128]{1,0,2:T(8,128)(2,1)}) fusion(bf16[128,16,128]{1,0,2:T(8,128)(2,1)} %bitcast.54), kind=kLoop, calls=%fused_computation.34 | loop fusion | bytes 131072 | tf_op jit(solution)/shard_map/slice | solution.py:174
  33.8 6.2 %copy.82 = bf16[128,1,128]{2,0,1:T(8,128)(2,1)S(1)} copy(bf16[128,1,128]{1,0,2:T(8,128)(2,1)} %get-tuple-element.32) | data formatting | bytes 65536 | tf_op jit(solution)/shard_map/slice | solution.py:174
  40.0 6.2 %copy.83 = bf16[128,1,128]{2,0,1:T(8,128)(2,1)S(1)} copy(bf16[128,1,128]{1,0,2:T(8,128)(2,1)} %get-tuple-element.33) | data formatting | bytes 65536 | tf_op jit(solution)/shard_map/slice | solution.py:173
  53.0 11.2 %collective-permute-done.2 = bf16[128,130]{1,0:T(8,128)(2,1)S(1)} collective-permute-done((bf16[128,130]{1,0:T(8,128)(2,1)S(1)}, bf16[128,130]{1,0:T(8,128)(2,1)S(1)}, u32[]{:S(2)}, u32[]{:S(2)}) %collective-permute-start.2) | collective-permute-done | bytes 33312 | tf_op jit(solution)/shard_map/ppermute | solution.py:175
  82.8 4.5 %collective-permute-done.4.p1 = bf16[69,2048]{1,0:T(8,128)(2,1)S(1)} collective-permute-done((bf16[69,2048]{1,0:T(8,128)(2,1)S(1)}, bf16[69,2048]{1,0:T(8,128)(2,1)S(1)}, u32[]{:S(2)}, u32[]{:S(2)}) %collective-permute-start.4) | collective-permute-done | bytes 282656 | tf_op jit(solution)/shard_map/ppermute | solution.py:135
  89.9 5.1 %shard_map.87 = (f32[128,2304]{1,0:T(8,128)S(1)}, f32[128,18]{1,0:T(8,128)S(1)}, f32[128,18]{1,0:T(8,128)S(1)}, bf16[576,128]{1,0:T(8,128)(2,1)S(1)}, bf16[576,128]{1,0:T(8,128)(2,1)S(1)}) custom-call(bf16[69,2048]{1,0:T(8,128)(2,1)S(1)} %get-tuple-element.10.own_ref, bf16[69,2048]{1,0:T(8,128)(2,1)S(1)} %copy-done.5, bf16[69,2048]{1,0:T(8,128)(2,1)S(1)} %copy-done.3, ...), custom_call_target="tpu_custom_call" | custom-call | flops 1244135424 | tf_op jit(solution)/shard_map/pallas_call | solution.py:201
  95.7 4.7 %collective-permute-start.11 = (bf16[576,128]{1,0:T(8,128)(2,1)S(1)}, bf16[576,128]{1,0:T(8,128)(2,1)S(1)}, u32[]{:S(2)}, u32[]{:S(2)}) collective-permute-start(bf16[576,128]{1,0:T(8,128)(2,1)S(1)} %broadcast_select_fusion.2), channel_id=1, source_target_pairs={{0,1},{1,0},{2,3},{3,2},{4,5},{5,4},{6,7},{7,6},{8,9},{9,8},{10,11... | collective-permute-start | bytes 442376 | tf_op jit(solution)/shard_map/ppermute | solution.py:215
  103.4 11.9 %collective-permute-done.12 = bf16[4,72,128]{2,1,0:T(8,128)(2,1)S(1)} collective-permute-done((bf16[4,72,128]{2,1,0:T(8,128)(2,1)S(1)}, bf16[4,72,128]{2,1,0:T(8,128)(2,1)S(1)}, u32[]{:S(2)}, u32[]{:S(2)}) %collective-permute-start.12) | collective-permute-done | bytes 73760 | tf_op jit(solution)/shard_map/ppermute | solution.py:241
  121.5 6.7 %collective-permute-start.14 = (bf16[1,72,128]{2,1,0:T(8,128)(2,1)S(1)}, bf16[1,72,128]{2,1,0:T(8,128)(2,1)S(1)}, u32[]{:S(2)}, u32[]{:S(2)}) collective-permute-start(bf16[1,72,128]{2,1,0:T(8,128)(2,1)S(1)} %broadcast_select_fusion.10), channel_id=1, source_target_pairs={{0,2},{1,3},{2,0},{3,1},{4,6},{5,7},{6,4},{7,5},{8,10},{9,11},{10,... | collective-permute-start | bytes 55304 | tf_op jit(solution)/shard_map/ppermute | solution.py:241
  128.6 4.6 %collective-permute-start.8 = (bf16[128,18]{1,0:T(8,128)(2,1)S(1)}, bf16[128,18]{1,0:T(8,128)(2,1)S(1)}, u32[]{:S(2)}, u32[]{:S(2)}) collective-permute-start(bf16[128,18]{1,0:T(8,128)(2,1)S(1)} %convert_element_type.104), channel_id=1, source_target_pairs={{1,0},{2,1},{3,2},{4,3},{5,4},{6,5},{7,6},{8,7},{9,8},{10,9},{11,1... | collective-permute-start | bytes 13832 | tf_op jit(solution)/shard_map/ppermute | solution.py:220
  133.2 11.8 %collective-permute-start.7 = (bf16[128,18]{1,0:T(8,128)(2,1)S(1)}, bf16[128,18]{1,0:T(8,128)(2,1)S(1)}, u32[]{:S(2)}, u32[]{:S(2)}) collective-permute-start(bf16[128,18]{1,0:T(8,128)(2,1)S(1)} %convert_element_type.103), channel_id=1, source_target_pairs={{0,1},{1,2},{2,3},{3,4},{4,5},{5,6},{6,7},{7,8},{8,9},{9,10},{10,1... | collective-permute-start | bytes 13832 | tf_op jit(solution)/shard_map/ppermute | solution.py:219
  145.0 4.8 %copy.90 = f32[128,18,128]{1,0,2:T(8,128)} copy(f32[128,18,128]{0,2,1:T(8,128)S(1)} %bitcast.55) | data formatting | bytes 2359296 | tf_op jit(solution)/shard_map/reshape | solution.py:221
  149.8 4.1 %collective-permute-start.17 = (bf16[72,128]{1,0:T(8,128)(2,1)S(1)}, bf16[72,128]{1,0:T(8,128)(2,1)S(1)}, u32[]{:S(2)}, u32[]{:S(2)}) collective-permute-start(bf16[72,128]{1,0:T(8,128)(2,1)S(1)} %fusion.4), channel_id=1, source_target_pairs={{0,384},{128,256},{256,128},{384,0},{1,385},{129,257},{257,129},{3... | collective-permute-start | bytes 55304 | tf_op jit(solution)/shard_map/ppermute | solution.py:135
  158.8 6.6 %fusion.5 = (bf16[128,18,128]{1,0,2:T(8,128)(2,1)S(1)}, f32[128,18,128]{1,0,2:T(8,128)}) fusion(bf16[128,18,1]{1,0,2:T(8,128)(2,1)S(1)} %bitcast.62, f32[128,18,128]{1,0,2:T(8,128)} %copy.90, bf16[128,18,1]{1,0,2:T(8,128)(2,1)S(1)} %bitcast.63), kind=kLoop, calls=%fused_computation.33 | loop fusion | flops 1474560 | bytes 2958336 | tf_op jit(solution)/shard_map/convert.14
  171.4 6.2 %copy.91 = bf16[128,1,128]{2,0,1:T(8,128)(2,1)S(1)} copy(bf16[128,1,128]{1,0,2:T(8,128)(2,1)} %get-tuple-element.30) | data formatting | bytes 65536 | tf_op jit(solution)/shard_map/jit(_where)/select_n | solution.py:226
  177.5 6.2 %copy.92 = bf16[128,1,128]{2,0,1:T(8,128)(2,1)S(1)} copy(bf16[128,1,128]{1,0,2:T(8,128)(2,1)} %get-tuple-element.31) | data formatting | bytes 65536 | tf_op jit(solution)/shard_map/jit(_where)/select_n | solution.py:225
  183.7 4.2 %collective-permute-start.10 = (bf16[128,128]{1,0:T(8,128)(2,1)S(1)}, bf16[128,128]{1,0:T(8,128)(2,1)S(1)}, u32[]{:S(2)}, u32[]{:S(2)}) collective-permute-start(bf16[128,128]{1,0:T(8,128)(2,1)S(1)} %bitcast.65), channel_id=1, source_target_pairs={{16,0},{17,1},{18,2},{19,3},{20,4},{21,5},{22,6},{23,7},{0,8},{1,9... | collective-permute-start | bytes 98312 | tf_op jit(solution)/shard_map/ppermute | solution.py:225
  192.1 9.1 %collective-permute-done.9 = bf16[128,128]{1,0:T(8,128)(2,1)S(1)} collective-permute-done((bf16[128,128]{1,0:T(8,128)(2,1)S(1)}, bf16[128,128]{1,0:T(8,128)(2,1)S(1)}, u32[]{:S(2)}, u32[]{:S(2)}) %collective-permute-start.9) | collective-permute-done | bytes 32800 | tf_op jit(solution)/shard_map/ppermute | solution.py:226
  201.3 6.9 %copy.93 = bf16[128,1,128]{1,0,2:T(8,128)(2,1)} copy(bf16[128,1,128]{2,0,1:T(8,128)(2,1)S(1)} %get-tuple-element.42) | data formatting | bytes 65536 | tf_op jit(solution)/shard_map/broadcast_in_dim | solution.py:230
  208.1 6.8 %copy.94 = bf16[128,1,128]{1,0,2:T(8,128)(2,1)} copy(bf16[128,1,128]{2,0,1:T(8,128)(2,1)S(1)} %get-tuple-element.43) | data formatting | bytes 65536 | tf_op jit(solution)/shard_map/broadcast_in_dim | solution.py:231
  216.9 8.9 %fusion.2 = bf16[1,128,16,128]{2,1,3,0:T(8,128)(2,1)} fusion(f32[128,18,128]{1,0,2:T(8,128)} %get-tuple-element.29, bf16[128,1,128]{1,0,2:T(8,128)(2,1)} %copy.94, bf16[128,1,128]{1,0,2:T(8,128)(2,1)} %copy.93), kind=kLoop, calls=%fused_computation.4 | loop fusion | flops 1310720 | bytes 1638400 | tf_op jit(solution)/shard_map/broadcast_in_dim | solution.py:232
  225.8 6.2 %copy.95 = bf16[1,128,16,128]{3,2,1,0:T(8,128)(2,1)} copy(bf16[1,128,16,128]{2,1,3,0:T(8,128)(2,1)} %fusion.2) | data formatting | bytes 1048576
  (88 shorter events, 58.3 us)
Async XLA Ops:
  8.7 37.6 %collective-permute-start = (bf16[128,16]{1,0:T(8,128)(2,1)S(1)}, bf16[128,16]{1,0:T(8,128)(2,1)S(1)}, u32[]{:S(2)}, u32[]{:S(2)}) collective-permute-start(bf16[128,16]{1,0:T(8,128)(2,1)S(1)} %get-tuple-element.34), channel_id=1, source_target_pairs={{0,1},{1,2},{2,3},{3,4},{4,5},{5,6},{6,7},{7,8},{8,9},{9,10},{10,1... | collective-permute-start | bytes 12296 | tf_op jit(solution)/shard_map/ppermute | solution.py:171
  24.3 21.9 %collective-permute-start.1 = (bf16[128,16]{1,0:T(8,128)(2,1)S(1)}, bf16[128,16]{1,0:T(8,128)(2,1)S(1)}, u32[]{:S(2)}, u32[]{:S(2)}) collective-permute-start(bf16[128,16]{1,0:T(8,128)(2,1)S(1)} %get-tuple-element.35), channel_id=1, source_target_pairs={{1,0},{2,1},{3,2},{4,3},{5,4},{6,5},{7,6},{8,7},{9,8},{10,9},{11,1... | collective-permute-start | bytes 12296 | tf_op jit(solution)/shard_map/ppermute | solution.py:172
  40.0 24.1 %copy-start.8 = (bf16[69,128]{1,0:T(8,128)(2,1)S(1)}, bf16[69,128]{1,0:T(8,128)(2,1)}, u32[]{:S(2)}) copy-start(bf16[69,128]{1,0:T(8,128)(2,1)} %ow_ref.1) | copy-start | bytes 52996
  40.0 37.8 %copy-start.12 = (f32[69]{0:T(128)S(1)}, f32[69]{0:T(128)}, u32[]{:S(2)}) copy-start(f32[69]{0:T(128)} %param.12) | copy-start | bytes 832
  46.5 6.5 %collective-permute-start.3 = (bf16[128,130]{1,0:T(8,128)(2,1)S(1)}, bf16[128,130]{1,0:T(8,128)(2,1)S(1)}, u32[]{:S(2)}, u32[]{:S(2)}) collective-permute-start(bf16[128,130]{1,0:T(8,128)(2,1)S(1)} %get-tuple-element.36), channel_id=1, source_target_pairs={{16,0},{17,1},{18,2},{19,3},{20,4},{21,5},{22,6},{23,7},{0,8},{1,9... | collective-permute-start | bytes 99848 | tf_op jit(solution)/shard_map/ppermute | solution.py:176
  50.4 13.7 %collective-permute-start.2 = (bf16[128,130]{1,0:T(8,128)(2,1)S(1)}, bf16[128,130]{1,0:T(8,128)(2,1)S(1)}, u32[]{:S(2)}, u32[]{:S(2)}) collective-permute-start(bf16[128,130]{1,0:T(8,128)(2,1)S(1)} %get-tuple-element.37), channel_id=1, source_target_pairs={{0,16},{1,17},{2,18},{3,19},{4,20},{5,21},{6,22},{7,23},{8,0},{9,1... | collective-permute-start | bytes 99848 | tf_op jit(solution)/shard_map/ppermute | solution.py:175
  68.6 13.4 %collective-permute-start.6 = (bf16[69,2048]{1,0:T(8,128)(2,1)S(1)}, bf16[69,2048]{1,0:T(8,128)(2,1)S(1)}, u32[]{:S(2)}, u32[]{:S(2)}) collective-permute-start(bf16[69,2048]{1,0:T(8,128)(2,1)S(1)} %get-tuple-element.10.own_ref), channel_id=1, source_target_pairs={{0,384},{128,256},{256,128},{384,0},{1,385},{129,257},{257,129},{3... | collective-permute-start | bytes 847880 | tf_op jit(solution)/shard_map/ppermute | solution.py:135
  71.5 10.6 %collective-permute-start.5 = (bf16[69,2048]{1,0:T(8,128)(2,1)S(1)}, bf16[69,2048]{1,0:T(8,128)(2,1)S(1)}, u32[]{:S(2)}, u32[]{:S(2)}) collective-permute-start(bf16[69,2048]{1,0:T(8,128)(2,1)S(1)} %get-tuple-element.10.own_ref), channel_id=1, source_target_pairs={{0,256},{128,384},{256,0},{384,128},{1,257},{129,385},{257,1},{385... | collective-permute-start | bytes 847880 | tf_op jit(solution)/shard_map/ppermute | solution.py:135
  73.9 13.4 %collective-permute-start.4 = (bf16[69,2048]{1,0:T(8,128)(2,1)S(1)}, bf16[69,2048]{1,0:T(8,128)(2,1)S(1)}, u32[]{:S(2)}, u32[]{:S(2)}) collective-permute-start(bf16[69,2048]{1,0:T(8,128)(2,1)S(1)} %get-tuple-element.10.own_ref), channel_id=1, source_target_pairs={{0,128},{128,0},{256,384},{384,256},{1,129},{129,1},{257,385},{385... | collective-permute-start | bytes 847880 | tf_op jit(solution)/shard_map/ppermute | solution.py:135
  95.6 32.9 %copy-start.7 = (f32[128,18]{1,0:T(8,128)S(1)}, f32[128,18]{1,0:T(8,128)}, u32[]{:S(2)}) copy-start(f32[128,18]{1,0:T(8,128)} %copy-done.6) | copy-start | bytes 27652
  95.7 5.7 %collective-permute-start.11 = (bf16[576,128]{1,0:T(8,128)(2,1)S(1)}, bf16[576,128]{1,0:T(8,128)(2,1)S(1)}, u32[]{:S(2)}, u32[]{:S(2)}) collective-permute-start(bf16[576,128]{1,0:T(8,128)(2,1)S(1)} %broadcast_select_fusion.2), channel_id=1, source_target_pairs={{0,1},{1,0},{2,3},{3,2},{4,5},{5,4},{6,7},{7,6},{8,9},{9,8},{10,11... | collective-permute-start | bytes 442376 | tf_op jit(solution)/shard_map/ppermute | solution.py:215
  101.4 13.8 %collective-permute-start.12 = (bf16[4,72,128]{2,1,0:T(8,128)(2,1)S(1)}, bf16[4,72,128]{2,1,0:T(8,128)(2,1)S(1)}, u32[]{:S(2)}, u32[]{:S(2)}) collective-permute-start(bf16[4,72,128]{2,1,0:T(8,128)(2,1)S(1)} %bitcast.61), channel_id=1, source_target_pairs={{0,8},{1,9},{2,10},{3,11},{4,12},{5,13},{6,14},{7,15},{8,0},{9,1},... | collective-permute-start | bytes 221192 | tf_op jit(solution)/shard_map/ppermute | solution.py:241
  115.3 6.2 %collective-permute-start.13 = (bf16[2,72,128]{2,1,0:T(8,128)(2,1)S(1)}, bf16[2,72,128]{2,1,0:T(8,128)(2,1)S(1)}, u32[]{:S(2)}, u32[]{:S(2)}) collective-permute-start(bf16[2,72,128]{2,1,0:T(8,128)(2,1)S(1)} %broadcast_select_fusion.9), channel_id=1, source_target_pairs={{0,4},{1,5},{2,6},{3,7},{4,0},{5,1},{6,2},{7,3},{8,12},{9,13},{10,... | collective-permute-start | bytes 110600 | tf_op jit(solution)/shard_map/ppermute | solution.py:241
  121.5 28.3 %collective-permute-start.14 = (bf16[1,72,128]{2,1,0:T(8,128)(2,1)S(1)}, bf16[1,72,128]{2,1,0:T(8,128)(2,1)S(1)}, u32[]{:S(2)}, u32[]{:S(2)}) collective-permute-start(bf16[1,72,128]{2,1,0:T(8,128)(2,1)S(1)} %broadcast_select_fusion.10), channel_id=1, source_target_pairs={{0,2},{1,3},{2,0},{3,1},{4,6},{5,7},{6,4},{7,5},{8,10},{9,11},{10,... | collective-permute-start | bytes 55304 | tf_op jit(solution)/shard_map/ppermute | solution.py:241
  128.6 30.2 %collective-permute-start.8 = (bf16[128,18]{1,0:T(8,128)(2,1)S(1)}, bf16[128,18]{1,0:T(8,128)(2,1)S(1)}, u32[]{:S(2)}, u32[]{:S(2)}) collective-permute-start(bf16[128,18]{1,0:T(8,128)(2,1)S(1)} %convert_element_type.104), channel_id=1, source_target_pairs={{1,0},{2,1},{3,2},{4,3},{5,4},{6,5},{7,6},{8,7},{9,8},{10,9},{11,1... | collective-permute-start | bytes 13832 | tf_op jit(solution)/shard_map/ppermute | solution.py:220
  133.2 25.6 %collective-permute-start.7 = (bf16[128,18]{1,0:T(8,128)(2,1)S(1)}, bf16[128,18]{1,0:T(8,128)(2,1)S(1)}, u32[]{:S(2)}, u32[]{:S(2)}) collective-permute-start(bf16[128,18]{1,0:T(8,128)(2,1)S(1)} %convert_element_type.103), channel_id=1, source_target_pairs={{0,1},{1,2},{2,3},{3,4},{4,5},{5,6},{6,7},{7,8},{8,9},{9,10},{10,1... | collective-permute-start | bytes 13832 | tf_op jit(solution)/shard_map/ppermute | solution.py:219
  149.8 15.6 %collective-permute-start.17 = (bf16[72,128]{1,0:T(8,128)(2,1)S(1)}, bf16[72,128]{1,0:T(8,128)(2,1)S(1)}, u32[]{:S(2)}, u32[]{:S(2)}) collective-permute-start(bf16[72,128]{1,0:T(8,128)(2,1)S(1)} %fusion.4), channel_id=1, source_target_pairs={{0,384},{128,256},{256,128},{384,0},{1,385},{129,257},{257,129},{3... | collective-permute-start | bytes 55304 | tf_op jit(solution)/shard_map/ppermute | solution.py:135
  154.0 11.5 %collective-permute-start.16 = (bf16[72,128]{1,0:T(8,128)(2,1)S(1)}, bf16[72,128]{1,0:T(8,128)(2,1)S(1)}, u32[]{:S(2)}, u32[]{:S(2)}) collective-permute-start(bf16[72,128]{1,0:T(8,128)(2,1)S(1)} %fusion.4), channel_id=1, source_target_pairs={{0,256},{128,384},{256,0},{384,128},{1,257},{129,385},{257,1},{385... | collective-permute-start | bytes 55304 | tf_op jit(solution)/shard_map/ppermute | solution.py:135
  156.4 9.1 %collective-permute-start.15 = (bf16[72,128]{1,0:T(8,128)(2,1)S(1)}, bf16[72,128]{1,0:T(8,128)(2,1)S(1)}, u32[]{:S(2)}, u32[]{:S(2)}) collective-permute-start(bf16[72,128]{1,0:T(8,128)(2,1)S(1)} %fusion.4), channel_id=1, source_target_pairs={{0,128},{128,0},{256,384},{384,256},{1,129},{129,1},{257,385},{385... | collective-permute-start | bytes 55304 | tf_op jit(solution)/shard_map/ppermute | solution.py:135
  165.5 24.4 %collective-permute-start.18 = (bf16[72,128]{1,0:T(8,128)(2,1)S(1)}, bf16[72,128]{1,0:T(8,128)(2,1)S(1)}, u32[]{:S(2)}, u32[]{:S(2)}) collective-permute-start(bf16[72,128]{1,0:T(8,128)(2,1)S(1)} %add_convert_fusion.4), channel_id=1, source_target_pairs={{0,16},{16,0},{32,48},{48,32},{64,80},{80,64},{96,112},{112,96},{1... | collective-permute-start | bytes 55304 | tf_op jit(solution)/shard_map/ppermute | solution.py:248
  183.7 8.4 %collective-permute-start.10 = (bf16[128,128]{1,0:T(8,128)(2,1)S(1)}, bf16[128,128]{1,0:T(8,128)(2,1)S(1)}, u32[]{:S(2)}, u32[]{:S(2)}) collective-permute-start(bf16[128,128]{1,0:T(8,128)(2,1)S(1)} %bitcast.65), channel_id=1, source_target_pairs={{16,0},{17,1},{18,2},{19,3},{20,4},{21,5},{22,6},{23,7},{0,8},{1,9... | collective-permute-start | bytes 98312 | tf_op jit(solution)/shard_map/ppermute | solution.py:225
  187.9 13.4 %collective-permute-start.9 = (bf16[128,128]{1,0:T(8,128)(2,1)S(1)}, bf16[128,128]{1,0:T(8,128)(2,1)S(1)}, u32[]{:S(2)}, u32[]{:S(2)}) collective-permute-start(bf16[128,128]{1,0:T(8,128)(2,1)S(1)} %bitcast.64), channel_id=1, source_target_pairs={{0,16},{1,17},{2,18},{3,19},{4,20},{5,21},{6,22},{7,23},{8,0},{9,1... | collective-permute-start | bytes 98312 | tf_op jit(solution)/shard_map/ppermute | solution.py:226
  189.9 25.1 %collective-permute-start.19 = (bf16[72,128]{1,0:T(8,128)(2,1)S(1)}, bf16[72,128]{1,0:T(8,128)(2,1)S(1)}, u32[]{:S(2)}, u32[]{:S(2)}) collective-permute-start(bf16[72,128]{1,0:T(8,128)(2,1)S(1)} %add_convert_fusion.3), channel_id=1, source_target_pairs={{0,32},{16,48},{32,0},{48,16},{64,96},{80,112},{96,64},{112,80},{1... | collective-permute-start | bytes 55304 | tf_op jit(solution)/shard_map/ppermute | solution.py:248
  215.0 17.0 %collective-permute-start.20 = (bf16[72,128]{1,0:T(8,128)(2,1)S(1)}, bf16[72,128]{1,0:T(8,128)(2,1)S(1)}, u32[]{:S(2)}, u32[]{:S(2)}) collective-permute-start(bf16[72,128]{1,0:T(8,128)(2,1)S(1)} %add_convert_fusion.2), channel_id=1, source_target_pairs={{0,64},{16,80},{32,96},{48,112},{64,0},{80,16},{96,32},{112,48},{1... | collective-permute-start | bytes 55304 | tf_op jit(solution)/shard_map/ppermute | solution.py:248
  (10 other events, 80.4 us)

commit v2 on v1

v2 whole, which is shorter than its diff:
```python
import functools
import math

import jax
import jax.numpy as jnp
from jax import lax
from jax.experimental import pallas as pl
from jax.experimental.pallas import tpu as pltpu
from jax.sharding import PartitionSpec as P

smoothing = 0.1
LANES = 128


def dot(a, b, dims=(((1,), (0,)), ((), ()))):
    return lax.dot_general(a, b, dims, preferred_element_type=jnp.float32)


def prepare_kernel(x_ref, flat_ref, east_ref, west_ref, wide_ref):
    channels, rows, cols = wide_ref.shape
    wide_ref[...] = x_ref[0].astype(jnp.float32)
    for row in range(rows):
        flat_ref[:, row * cols : (row + 1) * cols] = wide_ref[:, row, :].astype(jnp.bfloat16)
    cell = lax.broadcasted_iota(jnp.int32, (rows * cols, 2 * rows), 0)
    slot = lax.broadcasted_iota(jnp.int32, (rows * cols, 2 * rows), 1)
    wanted = jnp.where(slot < rows, slot * cols + (cols - 1), (slot - rows) * cols)
    pick = jnp.where(cell == wanted, 1.0, 0.0).astype(jnp.bfloat16)
    edges = dot(flat_ref[...], pick).astype(jnp.bfloat16)
    east_ref[...] = edges[:, :rows]
    west_ref[...] = edges[:, rows:]


def forward_kernel(rows, x_ref, north_ref, south_ref, left_ref, right_ref, w_ref, b_ref, ow_ref, ob_ref,
                   out_ref, slope_ref, x3_ref):
    channels = x_ref.shape[0]
    lane = lax.broadcasted_iota(jnp.int32, (channels, LANES), 1)
    left_cols = left_ref[...].astype(jnp.float32)
    right_cols = right_ref[...].astype(jnp.float32)
    north = north_ref[...].astype(jnp.float32)
    south = south_ref[...].astype(jnp.float32)
    weights = w_ref[...].T
    for row in range(rows + 2):
        if row == 0:
            block, before, after = north[:, :LANES], north[:, LANES : LANES + 1], north[:, LANES + 1 :]
        elif row == rows + 1:
            block, before, after = south[:, :LANES], south[:, LANES : LANES + 1], south[:, LANES + 1 :]
        else:
            block = x_ref[:, (row - 1) * LANES : row * LANES].astype(jnp.float32)
            before, after = left_cols[:, row - 1 : row], right_cols[:, row - 1 : row]
        west = jnp.where(lane == 0, before, pltpu.roll(block, 1, 1))
        east = jnp.where(lane == LANES - 1, after, pltpu.roll(block, LANES - 1, 1))
        cells = slice(row * LANES, (row + 1) * LANES)
        x3_ref[:channels, cells] = west.astype(jnp.bfloat16)
        x3_ref[channels : 2 * channels, cells] = block.astype(jnp.bfloat16)
        x3_ref[2 * channels :, cells] = east.astype(jnp.bfloat16)
    for pair in range(rows // 2):
        start = 2 * pair * LANES
        pre = b_ref[...] + jnp.zeros((channels, 2 * LANES), jnp.float32)
        for tap_row in range(3):
            begin = start + tap_row * LANES
            taps = weights[:, tap_row * 3 * channels : (tap_row + 1) * 3 * channels]
            pre = pre + dot(taps, x3_ref[:, begin : begin + 2 * LANES])
        sigmoid = 1.0 / (1.0 + jnp.exp(-pre))
        active = (pre * sigmoid).astype(jnp.bfloat16)
        slope_ref[:, start : start + 2 * LANES] = sigmoid * (1.0 + pre * (1.0 - sigmoid))
        result = dot(ow_ref[...], active) + ob_ref[...]
        out_ref[:, start : start + 2 * LANES] = result.astype(jnp.bfloat16)


def backward_kernel(rows, shares, members, own_ref, all_ref, target_ref, vw_ref, owt_ref, slope_ref, x3_ref, w_ref,
                    core_ref, rims_ref, right_ref, left_ref, term_ref, g_ref):
    channels = slope_ref.shape[0]
    cells = rows * LANES
    eps = smoothing * smoothing

    def signed(d):
        return d * lax.rsqrt(d * d + eps)

    g_ref[:, : 2 * LANES] = jnp.zeros((channels, 2 * LANES), jnp.bfloat16)
    g_ref[:, 2 * LANES + cells :] = jnp.zeros((channels, 2 * LANES), jnp.bfloat16)
    for pair in range(rows // 2):
        here = slice(2 * pair * LANES, 2 * (pair + 1) * LANES)
        own = own_ref[:, here].astype(jnp.float32)
        total = jnp.zeros_like(own)
        for member in range(members):
            total = total + signed(own - all_ref[member, :, here].astype(jnp.float32))
        truth = jnp.concatenate([target_ref[:, 2 * pair, :], target_ref[:, 2 * pair + 1, :]], axis=1)
        fit = signed(own - truth)
        grad_out = vw_ref[...] * (fit / members - total / (members * (members - 1)))
        grad_act = dot(owt_ref[...], grad_out.astype(jnp.bfloat16))
        g_ref[:, 2 * LANES + here.start : 2 * LANES + here.stop] = (grad_act * slope_ref[:, here]).astype(jnp.bfloat16)

    grad_pre = g_ref[:, 2 * LANES : 2 * LANES + cells]
    terms = []
    for tap_row in range(3):
        terms.append(dot(x3_ref[:, tap_row * LANES : tap_row * LANES + cells], grad_pre, (((1,), (1,)), ((), ()))))
    size = channels // shares
    pieces = []
    for loop_half in range(2):
        for taps in (range(5), range(5, 10)):
            for share in range(loop_half * shares // 2, (loop_half + 1) * shares // 2):
                for tap in taps:
                    if tap < 9:
                        begin = (tap % 3) * channels + share * size
                        pieces.append(terms[tap // 3][begin : begin + size])
                    else:
                        pieces.append(jnp.zeros((size, channels), jnp.float32))
    term_ref[...] = jnp.concatenate(pieces, axis=0).astype(jnp.bfloat16)

    lane = lax.broadcasted_iota(jnp.int32, (channels, LANES), 1)
    right = jnp.zeros((channels, LANES), jnp.float32)
    left = jnp.zeros((channels, LANES), jnp.float32)
    for pair in range((rows + 2) // 2):
        start = 2 * pair * LANES
        spread = jnp.zeros((3 * channels, 2 * LANES), jnp.float32)
        for tap_row in range(3):
            begin = start + (2 - tap_row) * LANES
            taps = w_ref[tap_row * 3 * channels : (tap_row + 1) * 3 * channels, :]
            spread = spread + dot(taps, g_ref[:, begin : begin + 2 * LANES])
        for half in range(2):
            row = 2 * pair + half
            part = slice(half * LANES, (half + 1) * LANES)
            to_west = spread[:channels, part]
            to_east = spread[2 * channels :, part]
            moved_west = pltpu.roll(to_west, LANES - 1, 1)
            moved_east = pltpu.roll(to_east, 1, 1)
            total = spread[channels : 2 * channels, part]
            total = total + jnp.where(lane == LANES - 1, 0.0, moved_west) + jnp.where(lane == 0, 0.0, moved_east)
            if row == 0:
                rims_ref[:, :LANES] = total
            elif row == rows + 1:
                rims_ref[:, LANES:] = total
            else:
                core_ref[:, (row - 1) * LANES : row * LANES] = total
            left = jnp.where(lane == row, pltpu.roll(to_west, row, 1) if row else to_west, left)
            right = jnp.where(lane == row, pltpu.roll(to_east, row + 1, 1), right)
    left_ref[...] = left[:, : rows + 2].astype(jnp.bfloat16)
    right_ref[...] = right[:, : rows + 2].astype(jnp.bfloat16)


def finish_kernel(core_ref, left_ref, right_ref, first_ref, last_ref, out_ref, wide_ref):
    channels, rows, cols = wide_ref.shape
    lane = lax.broadcasted_iota(jnp.int32, (channels, cols), 1)
    left_cols = left_ref[...].astype(jnp.float32)
    right_cols = right_ref[...].astype(jnp.float32)
    for row in range(rows):
        total = core_ref[:, row * cols : (row + 1) * cols]
        total = total + jnp.where(lane == 0, left_cols[:, row + 1 : row + 2], 0.0)
        total = total + jnp.where(lane == cols - 1, right_cols[:, row + 1 : row + 2], 0.0)
        if row == 0:
            total = total + first_ref[...].astype(jnp.float32)
        if row == rows - 1:
            total = total + last_ref[...].astype(jnp.float32)
        wide_ref[:, row, :] = total
    out_ref[0] = wide_ref[...].astype(jnp.bfloat16)


def ring_pairs(bands, loops):
    half = loops // 2
    pairs = []
    for band in range(bands):
        for loop in range(loops):
            if loop < half:
                goal = (band + 1, loop) if band + 1 < bands else (band, loop + half)
            else:
                goal = (band - 1, loop) if band > 0 else (band, loop - half)
            pairs.append((band * loops + loop, goal[0] * loops + goal[1]))
    return pairs, [(j, i) for i, j in pairs]


def exchange(pieces, groups):
    return lax.all_to_all(
        pieces, ("ens", "lat", "lon"), split_axis=0, concat_axis=0, axis_index_groups=groups, tiled=True
    )


def pallas(kernel, out_shape, scratch=(), flops=0, nbytes=0):
    return pl.pallas_call(
        kernel,
        out_shape=out_shape,
        scratch_shapes=list(scratch),
        compiler_params=pltpu.CompilerParams(vmem_limit_bytes=48 * 1024 * 1024),
        cost_estimate=pl.CostEstimate(flops=flops, bytes_accessed=nbytes, transcendentals=0),
    )


def on_device(features, conv_weight, conv_bias, out_weight, out_bias, var_weight, target):
    channels, rows, cols = features.shape[1:]
    variables = out_weight.shape[0]
    members = lax.axis_size("ens")
    bands, loops = lax.axis_size("lat"), lax.axis_size("lon")
    half = loops // 2
    loop = lax.axis_index("lon")
    cells = rows * cols
    f32, bf16 = jnp.float32, jnp.bfloat16
    shape = jax.ShapeDtypeStruct
    east_way = [(i, (i + 1) % loops) for i in range(loops)]
    west_way = [(j, i) for i, j in east_way]
    onward, back = ring_pairs(bands, loops)
    near = loop < half

    def place(member, band, spot):
        return (member * bands + band) * loops + spot

    level_groups = [
        [place(e, b, h * half + s) for e in range(members) for s in range(half)] for b in range(bands) for h in range(2)
    ]
    column_groups = [
        [place(e, b, h * half + s) for h in range(2) for b in range(bands)] for e in range(members) for s in range(half)
    ]
    member_groups = [[place(e, b, s) for e in range(members)] for b in range(bands) for s in range(loops)]

    flat, east, west = pallas(
        prepare_kernel,
        (shape((channels, cells), bf16), shape((channels, rows), bf16), shape((channels, rows), bf16)),
        scratch=[pltpu.VMEM((channels, rows, cols), f32)],
    )(features)
    left = lax.ppermute(east, "lon", east_way)
    right = lax.ppermute(west, "lon", west_way)
    first = jnp.concatenate([flat[:, :cols], left[:, :1], right[:, :1]], axis=1)
    last = jnp.concatenate([flat[:, cells - cols :], left[:, rows - 1 :], right[:, rows - 1 :]], axis=1)
    got_on = lax.ppermute(jnp.where(near, last, first), ("lat", "lon"), onward)
    got_back = lax.ppermute(jnp.where(near, first, last), ("lat", "lon"), back)
    north = jnp.where(near, got_on, got_back)
    south = jnp.where(near, got_back, got_on)

    weights = conv_weight.transpose(1, 0, 2).reshape(9 * channels, channels)

    own, slope, x3 = pallas(
        functools.partial(forward_kernel, rows),
        (
            shape((variables, cells), bf16),
            shape((channels, cells), f32),
            shape((3 * channels, cells + 2 * cols), bf16),
        ),
        flops=2 * cells * channels * (9 * channels + variables),
    )(flat, north, south, left, right, weights, conv_bias[:, None], out_weight, out_bias[:, None])

    everyone = exchange(jnp.broadcast_to(own, (members, variables, cells)), member_groups)

    core, rims, rim_right, rim_left, terms = pallas(
        functools.partial(backward_kernel, rows, loops, members),
        (
            shape((channels, cells), f32),
            shape((channels, 2 * cols), f32),
            shape((channels, rows + 2), bf16),
            shape((channels, rows + 2), bf16),
            shape((10 * channels, channels), bf16),
        ),
        scratch=[pltpu.VMEM((channels, cells + 4 * cols), bf16)],
        flops=2 * cells * channels * (18 * channels + variables),
    )(own, everyone, target, var_weight[:, None], out_weight.T, slope, x3, weights)

    from_left = lax.ppermute(rim_right, "lon", east_way)
    from_right = lax.ppermute(rim_left, "lon", west_way)

    size = 5 * channels // loops
    terms = exchange(terms.reshape(members * half, size, channels), level_groups)
    terms = jnp.sum(terms.astype(f32), axis=0).astype(bf16)

    lane = lax.broadcasted_iota(jnp.int32, (channels, cols), 1)
    wide = [
        jnp.where(lane == 0, from_left[:, r : r + 1].astype(f32), 0.0)
        + jnp.where(lane == cols - 1, from_right[:, r : r + 1].astype(f32), 0.0)
        for r in (0, rows + 1)
    ]
    top = (rims[:, :cols] + wide[0]).astype(bf16)
    bottom = (rims[:, cols:] + wide[1]).astype(bf16)
    got_back = lax.ppermute(jnp.where(near, top, bottom), ("lat", "lon"), back)
    got_on = lax.ppermute(jnp.where(near, bottom, top), ("lat", "lon"), onward)
    to_first = jnp.where(near, got_on, got_back)
    to_last = jnp.where(near, got_back, got_on)

    terms = exchange(jnp.broadcast_to(terms, (2 * bands, size, channels)), column_groups)
    terms = jnp.sum(terms.astype(f32), axis=0).astype(bf16)

    grad_features = pallas(
        finish_kernel,
        shape((1, channels, rows, cols), bf16),
        scratch=[pltpu.VMEM((channels, rows, cols), f32)],
    )(core, from_left, from_right, to_first, to_last)

    terms = exchange(jnp.broadcast_to(terms, (members, size, channels)), member_groups)
    share = jnp.where(near, terms[: members // 2], terms[members // 2 :]).reshape(2 * size, channels)
    share = share[: 9 * channels // loops].astype(f32)
    total_cells = members * cells * bands * loops
    grad_weight = (share / math.sqrt(total_cells)).reshape(9, channels // loops, channels).transpose(1, 0, 2)
    return grad_features, grad_weight


def solution(mesh):
    return jax.shard_map(
        on_device,
        mesh=mesh,
        in_specs=(P("ens", None, "lat", "lon"), P(), P(), P(), P(), P(), P(None, "lat", "lon")),
        out_specs=(P("ens", None, "lat", "lon"), P("lon", None, None)),
        check_vma=False,
    )
```

time: 234 us -> 160 us (0.68)
  local copies, waits for them, and re-layouts: 72.7 us -> 8.25 us
  other arithmetic: 20.4 us -> 1.34 us
  blocking collectives: 0 us -> 13 us
  starting transfers between devices: 85.7 us -> 80.6 us
  Pallas kernels: 8.33 us -> 11.9 us
    ppermute x17 -> x4, starting transfers between devices: 73.8 us -> 33.3 us  [the longest x1 15.7 us: on_device(): left = lax.ppermute(east, 'lon', east_way)]
    slice x3 -> x1, local copies, waits for them, and re-layouts: 19.9 us -> 0.01 us  [on_device(): flat[:, cells - cols:]]
    all_to_all x0 -> x3, starting transfers between devices: none -> 19.3 us  [exchange(): lax.all_to_all(pieces, ('ens', 'lat', 'lon'), split_axis=0, concat_axis=0...]
    unnamed x32 -> x25, local copies, waits for them, and re-layouts: 20.2 us -> 5.27 us
    all_to_all x0 -> x1, blocking collectives: none -> 13 us  [exchange(): lax.all_to_all(pieces, ('ens', 'lat', 'lon'), split_axis=0, concat_axis=0...]
    all_to_all x0 -> x3, waiting for transfers between devices: none -> 12.8 us  [exchange(): lax.all_to_all(pieces, ('ens', 'lat', 'lon'), split_axis=0, concat_axis=0...]
    select_n x2 -> x0, local copies, waits for them, and re-layouts: 12.3 us -> none  [the longest x1 6.16 us: on_device(): got_back = lax.ppermute(jnp.where(near, top, bottom), ('lat', 'lon'), back)]
    broadcast_in_dim x2 -> x3, local copies, waits for them, and re-layouts: 13.7 us -> 2.47 us  [the longest x1 1.16 us: on_device(): jnp.broadcast_to(own, (members, variables, cells))]
  transfers between devices with their start and end apart: 21 -> 11, of which waited for: 7 -> 5; matrix products, arithmetic and copies ran while one was open for 34% -> 1% of each run, Pallas kernels for 0% -> 1%
where the time goes in v2:
time: 160 us; the launch traced here: 159 us
  starting transfers between devices  80.6 us (50%)
  waiting for transfers between devices  42.9 us (27%)
  blocking collectives  13 us (8%)
  Pallas kernels  11.9 us (7%)
  local copies, waits for them, and re-layouts  8.25 us (5%)
    all_to_all x3, starting transfers between devices, exchange(): lax.all_to_all(pieces, ('ens', 'lat', 'lon'), split_axis=0, concat_axis=0...  19.3 us
    ppermute x1, starting transfers between devices, on_device(): left = lax.ppermute(east, 'lon', east_way)  15.7 us
    ppermute x1, waiting for transfers between devices, on_device(): from_right = lax.ppermute(rim_left, 'lon', west_way)  15 us
    ppermute x1, waiting for transfers between devices, on_device(): right = lax.ppermute(west, 'lon', west_way)  14 us
    ppermute x1, starting transfers between devices, on_device(): from_left = lax.ppermute(rim_right, 'lon', east_way)  13.8 us
    all_to_all x1, blocking collectives, exchange(): lax.all_to_all(pieces, ('ens', 'lat', 'lon'), split_axis=0, concat_axis=0...  13 us
    all_to_all x3, waiting for transfers between devices, exchange(): lax.all_to_all(pieces, ('ens', 'lat', 'lon'), split_axis=0, concat_axis=0...  12.8 us
    ppermute x1, starting transfers between devices, on_device(): got_back = lax.ppermute(jnp.where(near, top, bottom), ('lat', 'lon'), back)  12 us
  transfers between devices with their start and end apart: 11, of which 5 were waited for; matrix products, arithmetic and copies ran while one was open for 1% of the time, Pallas kernels for 1%

profile of v2, /device:TPU:25, one launch (start us, length us, event | category | flops | bytes accessed | tf_op | source)
XLA Modules:
  0.0 158.9 jit_solution(16595781671476946433)
XLA Ops:
  1.7 1.5 shard_map.86
  3.2 15.7 %collective-permute-start = (bf16[128,16]{1,0:T(8,128)(2,1)S(1)}, bf16[128,16]{1,0:T(8,128)(2,1)S(1)}, u32[]{:S(2)}, u32[]{:S(2)}) collective-permute-start(bf16[128,16]{1,0:T(8,128)(2,1)S(1)} %get-tuple-element.14), channel_id=1, source_target_pairs={{0,1},{1,2},{2,3},{3,4},{4,5},{5,6},{6,7},{7,8},{8,9},{9,10},{10,1... | collective-permute-start | bytes 12296 | tf_op jit(solution)/shard_map/ppermute | solution.py:218
  18.9 1.9 %collective-permute-start.1 = (bf16[128,16]{1,0:T(8,128)(2,1)S(1)}, bf16[128,16]{1,0:T(8,128)(2,1)S(1)}, u32[]{:S(2)}, u32[]{:S(2)}) collective-permute-start(bf16[128,16]{1,0:T(8,128)(2,1)S(1)} %get-tuple-element.15), channel_id=1, source_target_pairs={{1,0},{2,1},{3,2},{4,3},{5,4},{6,5},{7,6},{8,7},{9,8},{10,9},{11,1... | collective-permute-start | bytes 12296 | tf_op jit(solution)/shard_map/ppermute | solution.py:219
  20.9 14.0 %collective-permute-done.1.right_ref = bf16[128,16]{1,0:T(8,128)(2,1)S(1)} collective-permute-done((bf16[128,16]{1,0:T(8,128)(2,1)S(1)}, bf16[128,16]{1,0:T(8,128)(2,1)S(1)}, u32[]{:S(2)}, u32[]{:S(2)}) %collective-permute-start.1) | collective-permute-done | bytes 4128 | tf_op jit(solution)/shard_map/ppermute | solution.py:219
  35.1 2.6 %collective-permute-start.2 = (bf16[128,130]{1,0:T(8,128)(2,1)S(1)}, bf16[128,130]{1,0:T(8,128)(2,1)S(1)}, u32[]{:S(2)}, u32[]{:S(2)}) collective-permute-start(bf16[128,130]{1,0:T(8,128)(2,1)S(1)} %get-tuple-element.31), channel_id=1, source_target_pairs={{0,16},{1,17},{2,18},{3,19},{4,20},{5,21},{6,22},{7,23},{8,0},{9,1... | collective-permute-start | bytes 99848 | tf_op jit(solution)/shard_map/ppermute | solution.py:222
  37.8 11.3 %collective-permute-start.3 = (bf16[128,130]{1,0:T(8,128)(2,1)S(1)}, bf16[128,130]{1,0:T(8,128)(2,1)S(1)}, u32[]{:S(2)}, u32[]{:S(2)}) collective-permute-start(bf16[128,130]{1,0:T(8,128)(2,1)S(1)} %get-tuple-element.30), channel_id=1, source_target_pairs={{16,0},{17,1},{18,2},{19,3},{20,4},{21,5},{22,6},{23,7},{0,8},{1,9... | collective-permute-start | bytes 99848 | tf_op jit(solution)/shard_map/ppermute | solution.py:223
  49.4 1.1 collective-permute-done.3
  50.5 3.2 %shard_map.87 = (bf16[69,2048]{1,0:T(8,128)(2,1)S(1)}, f32[128,2048]{1,0:T(8,128)S(1)}, bf16[384,2304]{1,0:T(8,128)(2,1)S(1)}) custom-call(bf16[128,2048]{1,0:T(8,128)(2,1)S(1)} %get-tuple-element.13.x_ref, bf16[128,130]{1,0:T(8,128)(2,1)S(1)} %get-tuple-element.35.north_ref, bf16[128,130]{1,0:T(8,128)(2,1)S(1)} %get-tuple-element.34.south_ref, ...), custom_call_target="tpu_custom_call" | custom-call | flops 640155648 | tf_op jit(solution)/shard_map/pallas_call | solution.py:229
  53.7 1.2 copy-done
  55.9 1.2 broadcast_in_dim.70
  57.1 4.1 %all-to-all-start = ((bf16[4,69,2048]{2,1,0:T(8,128)(2,1)}), bf16[4,69,2048]{2,1,0:T(8,128)(2,1)S(1)}, u32[]{:S(2)}, u32[]{:S(2)}) async-start(bf16[4,69,2048]{2,1,0:T(8,128)(2,1)} %broadcast_in_dim.70), calls=%async_computation | async-start | bytes 2359296 | tf_op jit(solution)/shard_map/all_to_all | solution.py:172
  61.5 10.2 %all-to-all-done.all_ref = bf16[4,69,2048]{2,1,0:T(8,128)(2,1)S(1)} async-done(((bf16[4,69,2048]{2,1,0:T(8,128)(2,1)}), bf16[4,69,2048]{2,1,0:T(8,128)(2,1)S(1)}, u32[]{:S(2)}, u32[]{:S(2)}) %all-to-all-start) | async-done | bytes 1130528 | tf_op jit(solution)/shard_map/all_to_all | solution.py:172
  71.7 1.2 copy-done.2
  72.9 5.4 %shard_map.88 = (f32[128,2048]{1,0:T(8,128)S(1)}, f32[128,256]{1,0:T(8,128)S(1)}, bf16[128,18]{1,0:T(8,128)(2,1)S(1)}, bf16[128,18]{1,0:T(8,128)(2,1)S(1)}, bf16[1280,128]{1,0:T(8,128)(2,1)S(1)}) custom-call(bf16[69,2048]{1,0:T(8,128)(2,1)S(1)} %get-tuple-element.16.own_ref, bf16[4,69,2048]{2,1,0:T(8,128)(2,1)S(1)} %all-to-all-done.all_ref, ...), custom_call_target="tpu_custom_call" | custom-call | flops 1244135424 | tf_op jit(solution)/shard_map/pallas_call | solution.py:241
  79.0 13.0 %all_to_all.20 = bf16[32,40,128]{2,1,0:T(8,128)(2,1)S(1)} all-to-all(bf16[32,40,128]{2,1,0:T(8,128)(2,1)S(1)} %bitcast.13), channel_id=1, replica_groups={{0,1,2,3,4,5,6,7,128,129,130,131,132,133,134,135,256,257,258,259,260,26..., dimensions={0} | all-to-all | bytes 655360 | tf_op jit(solution)/shard_map/all_to_all | solution.py:172
  92.8 11.9 %all-to-all-start.2 = ((bf16[16,40,128]{2,1,0:T(8,128)(2,1)}), bf16[16,40,128]{2,1,0:T(8,128)(2,1)S(1)}, u32[]{:S(2)}, u32[]{:S(2)}) async-start(bf16[16,40,128]{2,1,0:T(8,128)(2,1)} %broadcast_in_dim.85), calls=%async_computation.2 | async-start | bytes 327680 | tf_op jit(solution)/shard_map/all_to_all | solution.py:172
  104.7 13.8 %collective-permute-start.4 = (bf16[128,18]{1,0:T(8,128)(2,1)S(1)}, bf16[128,18]{1,0:T(8,128)(2,1)S(1)}, u32[]{:S(2)}, u32[]{:S(2)}) collective-permute-start(bf16[128,18]{1,0:T(8,128)(2,1)S(1)} %get-tuple-element.20), channel_id=1, source_target_pairs={{0,1},{1,2},{2,3},{3,4},{4,5},{5,6},{6,7},{7,8},{8,9},{9,10},{10,1... | collective-permute-start | bytes 13832 | tf_op jit(solution)/shard_map/ppermute | solution.py:254
  118.5 1.9 %collective-permute-start.5 = (bf16[128,18]{1,0:T(8,128)(2,1)S(1)}, bf16[128,18]{1,0:T(8,128)(2,1)S(1)}, u32[]{:S(2)}, u32[]{:S(2)}) collective-permute-start(bf16[128,18]{1,0:T(8,128)(2,1)S(1)} %get-tuple-element.21), channel_id=1, source_target_pairs={{1,0},{2,1},{3,2},{4,3},{5,4},{6,5},{7,6},{8,7},{9,8},{10,9},{11,1... | collective-permute-start | bytes 13832 | tf_op jit(solution)/shard_map/ppermute | solution.py:255
  120.6 15.0 %collective-permute-done.5.right_ref = bf16[128,18]{1,0:T(8,128)(2,1)S(1)} collective-permute-done((bf16[128,18]{1,0:T(8,128)(2,1)S(1)}, bf16[128,18]{1,0:T(8,128)(2,1)S(1)}, u32[]{:S(2)}, u32[]{:S(2)}) %collective-permute-start.5) | collective-permute-done | bytes 4640 | tf_op jit(solution)/shard_map/ppermute | solution.py:255
  136.0 2.0 %collective-permute-start.6 = (bf16[128,128]{1,0:T(8,128)(2,1)S(1)}, bf16[128,128]{1,0:T(8,128)(2,1)S(1)}, u32[]{:S(2)}, u32[]{:S(2)}) collective-permute-start(bf16[128,128]{1,0:T(8,128)(2,1)S(1)} %get-tuple-element.33), channel_id=1, source_target_pairs={{0,16},{1,17},{2,18},{3,19},{4,20},{5,21},{6,22},{7,23},{8,0},{9,1... | collective-permute-start | bytes 98312 | tf_op jit(solution)/shard_map/ppermute | solution.py:270
  138.0 12.0 %collective-permute-start.7 = (bf16[128,128]{1,0:T(8,128)(2,1)S(1)}, bf16[128,128]{1,0:T(8,128)(2,1)S(1)}, u32[]{:S(2)}, u32[]{:S(2)}) collective-permute-start(bf16[128,128]{1,0:T(8,128)(2,1)S(1)} %get-tuple-element.32), channel_id=1, source_target_pairs={{16,0},{17,1},{18,2},{19,3},{20,4},{21,5},{22,6},{23,7},{0,8},{1,9... | collective-permute-start | bytes 98312 | tf_op jit(solution)/shard_map/ppermute | solution.py:269
  150.6 3.3 %all-to-all-start.3 = ((bf16[4,40,128]{2,1,0:T(8,128)(2,1)}), bf16[4,40,128]{2,1,0:T(8,128)(2,1)S(1)}, u32[]{:S(2)}, u32[]{:S(2)}) async-start(bf16[4,40,128]{2,1,0:T(8,128)(2,1)} %broadcast_in_dim.86), calls=%async_computation.3 | async-start | bytes 81920 | tf_op jit(solution)/shard_map/all_to_all | solution.py:172
  154.0 1.7 %shard_map.89 = bf16[1,128,16,128]{3,2,1,0:T(8,128)(2,1)} custom-call(f32[128,2048]{1,0:T(8,128)S(1)} %get-tuple-element.19.core_ref, bf16[128,18]{1,0:T(8,128)(2,1)S(1)} %collective-permute-done.4.left_ref, bf16[128,18]{1,0:T(8,128)(2,1)S(1)} %collective-permute-done.5.right_ref, bf16[128,128]{1,0:T(8,128)(2,1)S(1)} %get-tuple-element.37.first_ref, ...), custom_call_target="tpu_custom_call" | custom-call | tf_op jit(solution)/shard_map/pallas_call | solution.py:277
  155.7 2.6 %all-to-all-done.3 = bf16[4,40,128]{2,1,0:T(8,128)(2,1)S(1)} async-done(((bf16[4,40,128]{2,1,0:T(8,128)(2,1)}), bf16[4,40,128]{2,1,0:T(8,128)(2,1)S(1)}, u32[]{:S(2)}, u32[]{:S(2)}) %all-to-all-start.3) | async-done | bytes 40992 | tf_op jit(solution)/shard_map/all_to_all | solution.py:172
  (48 shorter events, 6.0 us)
Async XLA Ops:
  0.6 1.0 copy-start.4
  1.7 47.4 %copy-start.9 = (f32[128]{0:T(128)S(1)}, f32[128]{0:T(128)}, u32[]{:S(2)}) copy-start(f32[128]{0:T(128)} %param.9) | copy-start | bytes 1540
  1.7 47.6 %copy-start.10 = (f32[69]{0:T(128)S(1)}, f32[69]{0:T(128)}, u32[]{:S(2)}) copy-start(f32[69]{0:T(128)} %param.11) | copy-start | bytes 832
  1.7 48.8 %copy-start.5 = (bf16[128,9,128]{2,0,1:T(8,128)(2,1)S(1)}, bf16[128,9,128]{2,0,1:T(8,128)(2,1)}, u32[]{:S(2)}) copy-start(bf16[128,9,128]{2,0,1:T(8,128)(2,1)} %param.8) | copy-start | bytes 884740
  1.7 48.8 %copy-start.8 = (bf16[69,128]{1,0:T(8,128)(2,1)S(1)}, bf16[69,128]{1,0:T(8,128)(2,1)}, u32[]{:S(2)}) copy-start(bf16[69,128]{1,0:T(8,128)(2,1)} %ow_ref.1) | copy-start | bytes 52996
  3.2 17.6 %collective-permute-start = (bf16[128,16]{1,0:T(8,128)(2,1)S(1)}, bf16[128,16]{1,0:T(8,128)(2,1)S(1)}, u32[]{:S(2)}, u32[]{:S(2)}) collective-permute-start(bf16[128,16]{1,0:T(8,128)(2,1)S(1)} %get-tuple-element.14), channel_id=1, source_target_pairs={{0,1},{1,2},{2,3},{3,4},{4,5},{5,6},{6,7},{7,8},{8,9},{9,10},{10,1... | collective-permute-start | bytes 12296 | tf_op jit(solution)/shard_map/ppermute | solution.py:218
  18.9 16.1 %collective-permute-start.1 = (bf16[128,16]{1,0:T(8,128)(2,1)S(1)}, bf16[128,16]{1,0:T(8,128)(2,1)S(1)}, u32[]{:S(2)}, u32[]{:S(2)}) collective-permute-start(bf16[128,16]{1,0:T(8,128)(2,1)S(1)} %get-tuple-element.15), channel_id=1, source_target_pairs={{1,0},{2,1},{3,2},{4,3},{5,4},{6,5},{7,6},{8,7},{9,8},{10,9},{11,1... | collective-permute-start | bytes 12296 | tf_op jit(solution)/shard_map/ppermute | solution.py:219
  35.1 14.3 %collective-permute-start.2 = (bf16[128,130]{1,0:T(8,128)(2,1)S(1)}, bf16[128,130]{1,0:T(8,128)(2,1)S(1)}, u32[]{:S(2)}, u32[]{:S(2)}) collective-permute-start(bf16[128,130]{1,0:T(8,128)(2,1)S(1)} %get-tuple-element.31), channel_id=1, source_target_pairs={{0,16},{1,17},{2,18},{3,19},{4,20},{5,21},{6,22},{7,23},{8,0},{9,1... | collective-permute-start | bytes 99848 | tf_op jit(solution)/shard_map/ppermute | solution.py:222
  37.8 12.7 %collective-permute-start.3 = (bf16[128,130]{1,0:T(8,128)(2,1)S(1)}, bf16[128,130]{1,0:T(8,128)(2,1)S(1)}, u32[]{:S(2)}, u32[]{:S(2)}) collective-permute-start(bf16[128,130]{1,0:T(8,128)(2,1)S(1)} %get-tuple-element.30), channel_id=1, source_target_pairs={{16,0},{17,1},{18,2},{19,3},{20,4},{21,5},{22,6},{23,7},{0,8},{1,9... | collective-permute-start | bytes 99848 | tf_op jit(solution)/shard_map/ppermute | solution.py:223
  53.7 1.2 copy-start
  55.0 1.0 copy-start.1
  57.1 4.3 %copy-start.11 = (f32[69]{0:T(128)S(1)}, f32[69]{0:T(128)}, u32[]{:S(2)}) copy-start(f32[69]{0:T(128)} %param.12) | copy-start | bytes 832
  57.1 14.6 %copy-start.3 = (f32[69,16,128]{2,1,0:T(8,128)S(1)}, f32[69,16,128]{2,1,0:T(8,128)}, u32[]{:S(2)}) copy-start(f32[69,16,128]{2,1,0:T(8,128)} %target_ref.1) | copy-start | bytes 1695748
  57.1 14.6 %all-to-all-start = ((bf16[4,69,2048]{2,1,0:T(8,128)(2,1)}), bf16[4,69,2048]{2,1,0:T(8,128)(2,1)S(1)}, u32[]{:S(2)}, u32[]{:S(2)}) async-start(bf16[4,69,2048]{2,1,0:T(8,128)(2,1)} %broadcast_in_dim.70), calls=%async_computation | async-start | bytes 2359296 | tf_op jit(solution)/shard_map/all_to_all | solution.py:172
  71.7 1.2 copy-start.2
  78.4 0.6 copy-start.6
  79.0 56.8 %copy-start.7 = (f32[128,256]{1,0:T(8,128)S(1)}, f32[128,256]{1,0:T(8,128)}, u32[]{:S(2)}) copy-start(f32[128,256]{1,0:T(8,128)} %copy-done.6) | copy-start | bytes 393220
  92.8 57.2 %all-to-all-start.2 = ((bf16[16,40,128]{2,1,0:T(8,128)(2,1)}), bf16[16,40,128]{2,1,0:T(8,128)(2,1)S(1)}, u32[]{:S(2)}, u32[]{:S(2)}) async-start(bf16[16,40,128]{2,1,0:T(8,128)(2,1)} %broadcast_in_dim.85), calls=%async_computation.2 | async-start | bytes 327680 | tf_op jit(solution)/shard_map/all_to_all | solution.py:172
  104.7 15.8 %collective-permute-start.4 = (bf16[128,18]{1,0:T(8,128)(2,1)S(1)}, bf16[128,18]{1,0:T(8,128)(2,1)S(1)}, u32[]{:S(2)}, u32[]{:S(2)}) collective-permute-start(bf16[128,18]{1,0:T(8,128)(2,1)S(1)} %get-tuple-element.20), channel_id=1, source_target_pairs={{0,1},{1,2},{2,3},{3,4},{4,5},{5,6},{6,7},{7,8},{8,9},{9,10},{10,1... | collective-permute-start | bytes 13832 | tf_op jit(solution)/shard_map/ppermute | solution.py:254
  118.5 17.1 %collective-permute-start.5 = (bf16[128,18]{1,0:T(8,128)(2,1)S(1)}, bf16[128,18]{1,0:T(8,128)(2,1)S(1)}, u32[]{:S(2)}, u32[]{:S(2)}) collective-permute-start(bf16[128,18]{1,0:T(8,128)(2,1)S(1)} %get-tuple-element.21), channel_id=1, source_target_pairs={{1,0},{2,1},{3,2},{4,3},{5,4},{6,5},{7,6},{8,7},{9,8},{10,9},{11,1... | collective-permute-start | bytes 13832 | tf_op jit(solution)/shard_map/ppermute | solution.py:255
  136.0 18.0 %collective-permute-start.6 = (bf16[128,128]{1,0:T(8,128)(2,1)S(1)}, bf16[128,128]{1,0:T(8,128)(2,1)S(1)}, u32[]{:S(2)}, u32[]{:S(2)}) collective-permute-start(bf16[128,128]{1,0:T(8,128)(2,1)S(1)} %get-tuple-element.33), channel_id=1, source_target_pairs={{0,16},{1,17},{2,18},{3,19},{4,20},{5,21},{6,22},{7,23},{8,0},{9,1... | collective-permute-start | bytes 98312 | tf_op jit(solution)/shard_map/ppermute | solution.py:270
  138.0 15.9 %collective-permute-start.7 = (bf16[128,128]{1,0:T(8,128)(2,1)S(1)}, bf16[128,128]{1,0:T(8,128)(2,1)S(1)}, u32[]{:S(2)}, u32[]{:S(2)}) collective-permute-start(bf16[128,128]{1,0:T(8,128)(2,1)S(1)} %get-tuple-element.32), channel_id=1, source_target_pairs={{16,0},{17,1},{18,2},{19,3},{20,4},{21,5},{22,6},{23,7},{0,8},{1,9... | collective-permute-start | bytes 98312 | tf_op jit(solution)/shard_map/ppermute | solution.py:269
  150.6 7.6 %all-to-all-start.3 = ((bf16[4,40,128]{2,1,0:T(8,128)(2,1)}), bf16[4,40,128]{2,1,0:T(8,128)(2,1)S(1)}, u32[]{:S(2)}, u32[]{:S(2)}) async-start(bf16[4,40,128]{2,1,0:T(8,128)(2,1)} %broadcast_in_dim.86), calls=%async_computation.3 | async-start | bytes 81920 | tf_op jit(solution)/shard_map/all_to_all | solution.py:172

commit v3 on v2

v3 whole, which is shorter than its diff:
```python
import functools
import math

import jax
import jax.numpy as jnp
import numpy as np
from jax import lax
from jax.experimental import pallas as pl
from jax.experimental.pallas import tpu as pltpu
from jax.sharding import PartitionSpec as P

smoothing = 0.1
LANES = 128
RIM = 32
f32, bf16 = jnp.float32, jnp.bfloat16


def dot(a, b, dims=(((1,), (0,)), ((), ()))):
    return lax.dot_general(a, b, dims, preferred_element_type=f32)


def tile(index, count=1):
    return slice(index * LANES, (index + count) * LANES)


def signed(d):
    return d * lax.rsqrt(d * d + smoothing * smoothing)


def prepare_kernel(x_ref, target_ref, flat_ref, east_ref, west_ref, first_ref, last_ref, wide_ref, aim_ref):
    channels, rows, cols = wide_ref.shape
    variables = target_ref.shape[0]
    wide_ref[...] = x_ref[0].astype(f32)
    aim_ref[...] = jnp.zeros(aim_ref.shape, f32)
    for row in range(rows):
        flat_ref[:, tile(row)] = wide_ref[:, row, :].astype(bf16)
        aim_ref[:variables, tile(row)] = target_ref[:, row, :]
    high = aim_ref[...].astype(bf16)
    low = (aim_ref[...] - high.astype(f32)).astype(bf16)
    cell = lax.broadcasted_iota(jnp.int32, (rows * cols, 4 * rows), 0)
    slot = lax.broadcasted_iota(jnp.int32, (rows * cols, 4 * rows), 1)
    column = jnp.where(slot < rows, cols - 1, jnp.where(slot < 2 * rows, cols - 2, jnp.where(slot < 3 * rows, 0, 1)))
    wanted = (slot % rows) * cols + column
    pick = jnp.where(cell == wanted, 1.0, 0.0).astype(bf16)
    edges = dot(flat_ref[...], pick).astype(bf16)
    high_edges = dot(high, pick).astype(bf16)
    low_edges = dot(low, pick).astype(bf16)
    for ref, begin in ((east_ref, 0), (west_ref, 2 * rows)):
        ref[:channels] = edges[:, begin : begin + 2 * rows]
        ref[channels:, :rows] = high_edges[:, begin : begin + rows]
        ref[channels:, rows:] = low_edges[:, begin : begin + rows]
    for ref, near, second in ((first_ref, 0, 1), (last_ref, rows - 1, rows - 2)):
        ref[:channels, :cols] = flat_ref[:, tile(near)]
        ref[:channels, cols:] = flat_ref[:, tile(second)]
        ref[channels:, :cols] = high[:, tile(near)]
        ref[channels:, cols:] = low[:, tile(near)]


def rim_choice(rows):
    width = 2 * LANES + 8
    sources = [np.zeros((size, 3 * LANES), np.float32) for size in (2 * rows, 2 * rows, 2 * rows, 2 * rows, width, width)]
    left, right, east, west, north, south = sources
    for row in range(rows):
        lane = row + 2
        left[row, LANES + lane] = 1
        left[rows + row, lane] = 1
        right[row, LANES + RIM + lane] = 1
        right[rows + row, 2 * LANES + RIM + lane] = 1
        east[row, RIM + lane] = 1
        west[row, 2 * LANES + lane] = 1
    for source, lanes in ((north, (1, 0)), (south, (rows + 2, rows + 3))):
        for second, lane in enumerate(lanes):
            source[2 * LANES + second, LANES + lane] = 1
            source[2 * LANES + 2 + second, lane] = 1
            source[2 * LANES + 4 + second, LANES + RIM + lane] = 1
            source[2 * LANES + 6 + second, 2 * LANES + RIM + lane] = 1
            source[second * LANES + LANES - 1, RIM + lane] = 1
            source[second * LANES, 2 * LANES + lane] = 1
    return [jnp.asarray(source, bf16) for source in sources]


def forward_kernel(rows, pole_ref, x_ref, north_ref, south_ref, left_ref, right_ref, east_ref, west_ref,
                   cl_ref, cr_ref, ce_ref, cw_ref, cn_ref, cs_ref, w_ref, b_ref, ow_ref, ob_ref,
                   out_ref, slope_ref, x3_ref, truth_ref):
    channels = x_ref.shape[0]
    variables = out_ref.shape[0]
    north_pole, south_pole = pole_ref[0], pole_ref[1]
    lane = lax.broadcasted_iota(jnp.int32, (channels, LANES), 1)
    lane3 = lax.broadcasted_iota(jnp.int32, (3 * channels, LANES), 1)
    left = left_ref[:channels].astype(f32)
    right = right_ref[:channels].astype(f32)
    north = north_ref[:channels].astype(f32)
    south = south_ref[:channels].astype(f32)
    weights = w_ref[...].T

    def taps(tap_row):
        return weights[:, tap_row * 3 * channels : (tap_row + 1) * 3 * channels]

    for row in range(rows + 4):
        if row < 2 or row >= rows + 2:
            edge = north if row < 2 else south
            second = 1 - row if row < 2 else row - rows - 2
            block = edge[:, tile(second)]
            before = edge[:, 2 * LANES + second : 2 * LANES + second + 1]
            after = edge[:, 2 * LANES + 4 + second : 2 * LANES + 5 + second]
        else:
            block = x_ref[:, tile(row - 2)].astype(f32)
            before, after = left[:, row - 2 : row - 1], right[:, row - 2 : row - 1]
        x3_ref[:channels, tile(row)] = jnp.where(lane == 0, before, pltpu.roll(block, 1, 1)).astype(bf16)
        x3_ref[channels : 2 * channels, tile(row)] = block.astype(bf16)
        x3_ref[2 * channels :, tile(row)] = jnp.where(
            lane == LANES - 1, after, pltpu.roll(block, LANES - 1, 1)
        ).astype(bf16)

    def finish(pre, place):
        pre = pre + b_ref[...]
        sigmoid = 1.0 / (1.0 + jnp.exp(-pre))
        active = (pre * sigmoid).astype(bf16)
        slope_ref[:, place] = sigmoid * (1.0 + pre * (1.0 - sigmoid))
        out_ref[:, place] = (dot(ow_ref[...], active) + ob_ref[...]).astype(bf16)

    for pair in range(rows // 2):
        begin = 1 + 2 * pair
        pre = dot(taps(0), x3_ref[:, tile(begin, 2)])
        for tap_row in (1, 2):
            pre = pre + dot(taps(tap_row), x3_ref[:, tile(begin + tap_row, 2)])
        finish(pre, tile(begin, 2))
    for q, pole in ((0, north_pole), (rows + 1, south_pole)):
        above, below = x3_ref[:, tile(q)].astype(f32), x3_ref[:, tile(q + 2)].astype(f32)
        turned = lane3 < pole * LANES
        pre = dot(taps(1), x3_ref[:, tile(q + 1)])
        pre = pre + dot(taps(0), jnp.where(turned, below, above).astype(bf16))
        pre = pre + dot(taps(2), jnp.where(turned, above, below).astype(bf16))
        finish(pre, tile(q))
    rim = dot(left_ref[...], cl_ref[...]) + dot(right_ref[...], cr_ref[...])
    rim = rim + dot(east_ref[...], ce_ref[...]) + dot(west_ref[...], cw_ref[...])
    rim = rim + dot(north_ref[...], cn_ref[...]) + dot(south_ref[...], cs_ref[...])
    middle = jnp.concatenate([rim[:channels, tile(k)] for k in range(3)], axis=0)
    above, below = pltpu.roll(middle, 1, 1), pltpu.roll(middle, LANES - 1, 1)
    first = (lane3 == 1) | (lane3 == RIM + 1)
    last = (lane3 == rows + 2) | (lane3 == RIM + rows + 2)
    turned = (first & (lane3 < north_pole * LANES)) | (last & (lane3 < south_pole * LANES))
    pre = dot(taps(1), middle.astype(bf16))
    pre = pre + dot(taps(0), jnp.where(turned, below, above).astype(bf16))
    pre = pre + dot(taps(2), jnp.where(turned, above, below).astype(bf16))
    finish(pre, tile(rows + 2))
    aim = slice(channels, channels + variables)
    for place, ref in ((0, north_ref), (1, south_ref)):
        edge = ref[channels:, tile(0)].astype(f32) + ref[channels:, tile(1)].astype(f32)
        truth_ref[:, tile(place)] = edge[:variables]
    side = lax.broadcasted_iota(jnp.int32, (variables, LANES), 1)
    truth_ref[:, tile(2)] = rim[aim, tile(1)] + jnp.where(side < RIM, rim[aim, tile(0)], rim[aim, tile(2)])


def weight_kernel(rows, shares, members, own_ref, all_ref, target_ref, truth_ref, vw_ref, owt_ref, slope_ref, x3_ref,
                  g_ref, term_ref):
    channels = slope_ref.shape[0]

    def grad(place, truth):
        own = own_ref[:, place].astype(f32)
        total = jnp.zeros_like(own)
        for member in range(members):
            total = total + signed(own - all_ref[member, :, place].astype(f32))
        grad_out = vw_ref[...] * (signed(own - truth) / members - total / (members * (members - 1)))
        grad_act = dot(owt_ref[...], grad_out.astype(bf16))
        g_ref[:, place] = (grad_act * slope_ref[:, place]).astype(bf16)

    for pair in range(rows // 2):
        truth = jnp.concatenate([target_ref[:, 2 * pair, :], target_ref[:, 2 * pair + 1, :]], axis=1)
        grad(tile(1 + 2 * pair, 2), truth)
    for place, q in enumerate((0, rows + 1, rows + 2)):
        grad(tile(q), truth_ref[:, tile(place)])

    grad_pre = g_ref[:, tile(1, rows)]
    terms = []
    for tap_row in range(3):
        terms.append(dot(x3_ref[:, tile(1 + tap_row, rows)], grad_pre, (((1,), (1,)), ((), ()))))
    size = channels // shares
    pieces = []
    for loop_half in range(2):
        for taps in (range(5), range(5, 10)):
            for share in range(loop_half * shares // 2, (loop_half + 1) * shares // 2):
                for tap in taps:
                    if tap < 9:
                        begin = (tap % 3) * channels + share * size
                        pieces.append(terms[tap // 3][begin : begin + size])
                    else:
                        pieces.append(jnp.zeros((size, channels), f32))
    term_ref[...] = jnp.concatenate(pieces, axis=0).astype(bf16)


def feature_kernel(pole_ref, g_ref, w_ref, out_ref, wide_ref):
    channels, rows, cols = wide_ref.shape
    north_pole, south_pole = pole_ref[0], pole_ref[1]
    lane = lax.broadcasted_iota(jnp.int32, (channels, LANES), 1)

    def taps(tap_row):
        return w_ref[tap_row * 3 * channels : (tap_row + 1) * 3 * channels, :]

    def split(value, turned):
        kept = jnp.where(turned, 0.0, value)
        return kept.astype(bf16), (value - kept).astype(bf16)

    north, north_turned = split(g_ref[:, tile(0)].astype(f32), lane < north_pole * LANES)
    south, south_turned = split(g_ref[:, tile(rows + 1)].astype(f32), lane < south_pole * LANES)
    rim = g_ref[:, tile(rows + 2)].astype(f32)
    above, below = pltpu.roll(rim, 1, 1), pltpu.roll(rim, LANES - 1, 1)
    first = (lane == 2) | (lane == RIM + 2)
    last = (lane == rows + 1) | (lane == RIM + rows + 1)
    above, above_turned = split(above, first & (lane < north_pole * LANES))
    below, below_turned = split(below, last & (lane < south_pole * LANES))
    side = dot(taps(1), rim.astype(bf16))
    side = side + dot(taps(2), above) + dot(taps(0), below)
    side = side + dot(taps(0), above_turned) + dot(taps(2), below_turned)
    from_left, from_right = side[2 * channels :], side[:channels]

    for pair in range(rows // 2):
        row = 2 * pair
        upper = g_ref[:, tile(row, 2)]
        lower = g_ref[:, tile(row + 2, 2)]
        if pair == 0:
            upper = jnp.concatenate([north, g_ref[:, tile(1)]], axis=1)
        if pair == rows // 2 - 1:
            lower = jnp.concatenate([g_ref[:, tile(rows)], south], axis=1)
        spread = dot(taps(1), g_ref[:, tile(row + 1, 2)]) + dot(taps(2), upper) + dot(taps(0), lower)
        for part in range(2):
            block = spread[:, tile(part)]
            if row + part == 0:
                block = block + dot(taps(0), north_turned)
            if row + part == rows - 1:
                block = block + dot(taps(2), south_turned)
            spot = row + part + 2
            moved_west = pltpu.roll(block[:channels], LANES - 1, 1)
            moved_east = pltpu.roll(block[2 * channels :], 1, 1)
            total = block[channels : 2 * channels]
            total = total + jnp.where(lane == 0, from_left[:, spot : spot + 1], moved_east)
            total = total + jnp.where(lane == LANES - 1, from_right[:, RIM + spot : RIM + spot + 1], moved_west)
            wide_ref[:, row + part, :] = total
    out_ref[0] = wide_ref[...].astype(bf16)


def ring_pairs(bands, loops):
    half = loops // 2
    pairs = []
    for band in range(bands):
        for loop in range(loops):
            if loop < half:
                goal = (band + 1, loop) if band + 1 < bands else (band, loop + half)
            else:
                goal = (band - 1, loop) if band > 0 else (band, loop - half)
            pairs.append((band * loops + loop, goal[0] * loops + goal[1]))
    return pairs, [(j, i) for i, j in pairs]


def exchange(pieces, groups):
    return lax.all_to_all(
        pieces, ("ens", "lat", "lon"), split_axis=0, concat_axis=0, axis_index_groups=groups, tiled=True
    )


def pallas(kernel, out_shape, scratch=(), scalars=0, operands=0, flops=0, nbytes=0):
    specs = {}
    if scalars:
        vmem = pl.BlockSpec(memory_space=pltpu.VMEM)
        specs["in_specs"] = [pl.BlockSpec(memory_space=pltpu.SMEM)] + [vmem] * operands
    return pl.pallas_call(
        kernel,
        out_shape=out_shape,
        scratch_shapes=list(scratch),
        compiler_params=pltpu.CompilerParams(vmem_limit_bytes=20 * 1024 * 1024),
        cost_estimate=pl.CostEstimate(flops=flops, bytes_accessed=nbytes, transcendentals=0),
        **specs,
    )


def on_device(features, conv_weight, conv_bias, out_weight, out_bias, var_weight, target):
    channels, rows, cols = features.shape[1:]
    variables = out_weight.shape[0]
    members = lax.axis_size("ens")
    bands, loops = lax.axis_size("lat"), lax.axis_size("lon")
    half = loops // 2
    band, loop = lax.axis_index("lat"), lax.axis_index("lon")
    cells = rows * cols
    more = cells + 3 * cols
    halo = -(-(channels + variables) // 16) * 16
    shape = jax.ShapeDtypeStruct
    east_way = [(i, (i + 1) % loops) for i in range(loops)]
    west_way = [(j, i) for i, j in east_way]
    onward, back = ring_pairs(bands, loops)
    near = loop < half
    poles = jnp.stack([band == 0, band == bands - 1]).astype(jnp.int32)

    def place(member, band, spot):
        return (member * bands + band) * loops + spot

    level_groups = [
        [place(e, b, h * half + s) for e in range(members) for s in range(half)] for b in range(bands) for h in range(2)
    ]
    column_groups = [
        [place(e, b, h * half + s) for h in range(2) for b in range(bands)] for e in range(members) for s in range(half)
    ]
    member_groups = [[place(e, b, s) for e in range(members)] for b in range(bands) for s in range(loops)]

    flat, east, west, first, last = pallas(
        prepare_kernel,
        (
            shape((channels, cells), bf16),
            shape((halo, 2 * rows), bf16),
            shape((halo, 2 * rows), bf16),
            shape((halo, 2 * cols), bf16),
            shape((halo, 2 * cols), bf16),
        ),
        scratch=[pltpu.VMEM((channels, rows, cols), f32), pltpu.VMEM((halo - channels, cells), f32)],
    )(features, target)
    left = lax.ppermute(east, "lon", east_way)
    right = lax.ppermute(west, "lon", west_way)

    def with_corners(edge, near, second):
        picks = [side[:, k : k + 1] for side in (left, right) for k in (near, second, rows + near, rows + second)]
        return jnp.concatenate([edge] + picks, axis=1)

    first = with_corners(first, 0, 1)
    last = with_corners(last, rows - 1, rows - 2)
    got_on = lax.ppermute(jnp.where(near, last, first), ("lat", "lon"), onward)
    got_back = lax.ppermute(jnp.where(near, first, last), ("lat", "lon"), back)
    north = jnp.where(near, got_on, got_back)
    south = jnp.where(near, got_back, got_on)

    weights = conv_weight.transpose(1, 0, 2).reshape(9 * channels, channels)

    own, slope, x3, truth = pallas(
        functools.partial(forward_kernel, rows),
        (
            shape((variables, more), bf16),
            shape((channels, more), f32),
            shape((3 * channels, cells + 4 * cols), bf16),
            shape((variables, 3 * cols), f32),
        ),
        scalars=1,
        operands=17,
        flops=2 * cells * channels * (9 * channels + variables),
    )(
        poles, flat, north, south, left, right, east, west, *rim_choice(rows),
        weights, conv_bias[:, None], out_weight, out_bias[:, None],
    )

    everyone = exchange(jnp.broadcast_to(own, (members, variables, more)), member_groups)

    grads, terms = pallas(
        functools.partial(weight_kernel, rows, loops, members),
        (shape((channels, more), bf16), shape((10 * channels, channels), bf16)),
        flops=2 * cells * channels * (9 * channels + variables),
    )(own, everyone, target, truth, var_weight[:, None], out_weight.T, slope, x3)

    size = 5 * channels // loops
    terms = exchange(terms.reshape(members * half, size, channels), level_groups)
    terms = jnp.sum(terms.astype(f32), axis=0).astype(bf16)

    grad_features = pallas(
        feature_kernel,
        shape((1, channels, rows, cols), bf16),
        scratch=[pltpu.VMEM((channels, rows, cols), f32)],
        scalars=1,
        operands=2,
        flops=2 * cells * channels * 9 * channels,
    )(poles, grads, weights)

    terms = exchange(jnp.broadcast_to(terms, (2 * bands, size, channels)), column_groups)
    terms = jnp.sum(terms.astype(f32), axis=0).astype(bf16)
    terms = exchange(jnp.broadcast_to(terms, (members, size, channels)), member_groups)
    share = jnp.where(near, terms[: members // 2], terms[members // 2 :]).reshape(2 * size, channels)
    share = share[: 9 * channels // loops].astype(f32)
    total_cells = members * cells * bands * loops
    grad_weight = (share / math.sqrt(total_cells)).reshape(9, channels // loops, channels).transpose(1, 0, 2)
    return grad_features, grad_weight


def solution(mesh):
    return jax.shard_map(
        on_device,
        mesh=mesh,
        in_specs=(P("ens", None, "lat", "lon"), P(), P(), P(), P(), P(), P(None, "lat", "lon")),
        out_specs=(P("ens", None, "lat", "lon"), P("lon", None, None)),
        check_vma=False,
    )
```

time: 160 us -> 140 us (0.88)
  the two profiles are of different devices: /device:TPU:25 before, /device:TPU:32 now
where the time goes in v3:
time: 140 us; the launch traced here: 139 us
  blocking collectives  45.3 us (32%)
  waiting for transfers between devices  34.4 us (25%)
  starting transfers between devices  33 us (24%)
  Pallas kernels  13.4 us (10%)
  local copies, waits for them, and re-layouts  11.7 us (8%)
    all_to_all x2, blocking collectives, exchange(): lax.all_to_all(pieces, ('ens', 'lat', 'lon'), split_axis=0, concat_axis=0...  45.3 us
    ppermute x1, starting transfers between devices, on_device(): right = lax.ppermute(west, 'lon', west_way)  16.7 us
    all_to_all x2, waiting for transfers between devices, exchange(): lax.all_to_all(pieces, ('ens', 'lat', 'lon'), split_axis=0, concat_axis=0...  14.6 us
    ppermute x1, waiting for transfers between devices, on_device(): left = lax.ppermute(east, 'lon', east_way)  12.9 us
    all_to_all x2, starting transfers between devices, exchange(): lax.all_to_all(pieces, ('ens', 'lat', 'lon'), split_axis=0, concat_axis=0...  7.7 us
    unnamed x33, local copies, waits for them, and re-layouts  7.46 us
    ppermute x1, waiting for transfers between devices, on_device(): got_back = lax.ppermute(jnp.where(near, first, last), ('lat', 'lon'), back)  6.11 us
    pallas_call x1, Pallas kernels, on_device(): pallas(functools.partial(forward_kernel, rows), (shape((variables, more),...  5.17 us
  transfers between devices with their start and end apart: 6, of which 5 were waited for; matrix products, arithmetic and copies ran while one was open for 1% of the time, Pallas kernels for 2%

profile of v3, /device:TPU:32, one launch (start us, length us, event | category | flops | bytes accessed | tf_op | source)
XLA Modules:
  0.0 139.5 jit_solution(17524262738440670972)
XLA Ops:
  0.6 1.0 copy-done
  1.7 1.0 copy-done.6
  2.7 2.3 %shard_map.140 = (bf16[128,2048]{1,0:T(8,128)(2,1)S(1)}, bf16[208,32]{1,0:T(8,128)(2,1)S(1)}, bf16[208,32]{1,0:T(8,128)(2,1)S(1)}, bf16[208,256]{1,0:T(8,128)(2,1)S(1)}, bf16[208,256]{1,0:T(8,128)(2,1)S(1)}) custom-call(bf16[1,128,16,128]{3,2,1,0:T(8,128)(2,1)S(1)} %copy-done.6, f32[69,16,128]{2,1,0:T(8,128)S(1)} %copy-done), custom_call_target="tpu_custom_call" | custom-call | tf_op jit(solution)/shard_map/pallas_call | solution.py:304
  5.0 16.7 %collective-permute-start.1 = (bf16[208,32]{1,0:T(8,128)(2,1)S(1)}, bf16[208,32]{1,0:T(8,128)(2,1)S(1)}, u32[]{:S(2)}, u32[]{:S(2)}) collective-permute-start(bf16[208,32]{1,0:T(8,128)(2,1)S(1)} %get-tuple-element.16.west_ref), channel_id=1, source_target_pairs={{1,0},{2,1},{3,2},{4,3},{5,4},{6,5},{7,6},{8,7},{9,8},{10,9},{11,1... | collective-permute-start | bytes 39944 | tf_op jit(solution)/shard_map/ppermute | solution.py:316
  21.7 1.9 %collective-permute-start = (bf16[208,32]{1,0:T(8,128)(2,1)S(1)}, bf16[208,32]{1,0:T(8,128)(2,1)S(1)}, u32[]{:S(2)}, u32[]{:S(2)}) collective-permute-start(bf16[208,32]{1,0:T(8,128)(2,1)S(1)} %get-tuple-element.15.east_ref), channel_id=1, source_target_pairs={{0,1},{1,2},{2,3},{3,4},{4,5},{5,6},{6,7},{7,8},{8,9},{9,10},{10,1... | collective-permute-start | bytes 39944 | tf_op jit(solution)/shard_map/ppermute | solution.py:315
  23.7 0.8 copy.19.b_ref
  25.3 12.9 %collective-permute-done.left_ref = bf16[208,32]{1,0:T(8,128)(2,1)S(1)} collective-permute-done((bf16[208,32]{1,0:T(8,128)(2,1)S(1)}, bf16[208,32]{1,0:T(8,128)(2,1)S(1)}, u32[]{:S(2)}, u32[]{:S(2)}) %collective-permute-start) | collective-permute-done | bytes 13344 | tf_op jit(solution)/shard_map/ppermute | solution.py:315
  39.0 4.7 %collective-permute-start.2 = (bf16[208,264]{1,0:T(8,128)(2,1)S(1)}, bf16[208,264]{1,0:T(8,128)(2,1)S(1)}, u32[]{:S(2)}, u32[]{:S(2)}) collective-permute-start(bf16[208,264]{1,0:T(8,128)(2,1)S(1)} %get-tuple-element.27), channel_id=1, source_target_pairs={{0,16},{1,17},{2,18},{3,19},{4,20},{5,21},{6,22},{7,23},{8,0},{9,1... | collective-permute-start | bytes 329480 | tf_op jit(solution)/shard_map/ppermute | solution.py:324
  43.7 1.9 %collective-permute-start.3 = (bf16[208,264]{1,0:T(8,128)(2,1)S(1)}, bf16[208,264]{1,0:T(8,128)(2,1)S(1)}, u32[]{:S(2)}, u32[]{:S(2)}) collective-permute-start(bf16[208,264]{1,0:T(8,128)(2,1)S(1)} %get-tuple-element.26), channel_id=1, source_target_pairs={{16,0},{17,1},{18,2},{19,3},{20,4},{21,5},{22,6},{23,7},{0,8},{1,9... | collective-permute-start | bytes 329480 | tf_op jit(solution)/shard_map/ppermute | solution.py:325
  46.5 6.1 %collective-permute-done.3 = bf16[208,264]{1,0:T(8,128)(2,1)S(1)} collective-permute-done((bf16[208,264]{1,0:T(8,128)(2,1)S(1)}, bf16[208,264]{1,0:T(8,128)(2,1)S(1)}, u32[]{:S(2)}, u32[]{:S(2)}) %collective-permute-start.3) | collective-permute-done | bytes 109856 | tf_op jit(solution)/shard_map/ppermute | solution.py:325
  52.7 5.2 %shard_map.141 = (bf16[69,2432]{1,0:T(8,128)(2,1)S(1)}, f32[128,2432]{1,0:T(8,128)S(1)}, bf16[384,2560]{1,0:T(8,128)(2,1)S(1)}, f32[69,384]{1,0:T(8,128)S(1)}) custom-call(s32[2]{0:T(128)S(1)} %add_convert_fusion.pole_ref, bf16[128,2048]{1,0:T(8,128)(2,1)S(1)} %get-tuple-element.13.x_ref, bf16[208,264]{1,0:T(8,128)(2,1)S(1)} %get-tuple-element.25.north_ref, ...), custom_call_target="tpu_custom_call" | custom-call | flops 640155648 | tf_op jit(solution)/shard_map/pallas_call | solution.py:331
  57.9 1.3 copy-done.2
  59.2 1.1 copy-done.4
  60.3 1.2 broadcast_in_dim.20
  61.5 4.4 %all-to-all-start = ((bf16[4,69,2432]{2,1,0:T(8,128)(2,1)}), bf16[4,69,2432]{2,1,0:T(8,128)(2,1)S(1)}, u32[]{:S(2)}, u32[]{:S(2)}) async-start(bf16[4,69,2432]{2,1,0:T(8,128)(2,1)} %broadcast_in_dim.20), calls=%async_computation | async-start | bytes 2801664 | tf_op jit(solution)/shard_map/all_to_all | solution.py:256
  66.1 12.5 %all-to-all-done.all_ref = bf16[4,69,2432]{2,1,0:T(8,128)(2,1)S(1)} async-done(((bf16[4,69,2432]{2,1,0:T(8,128)(2,1)}), bf16[4,69,2432]{2,1,0:T(8,128)(2,1)S(1)}, u32[]{:S(2)}, u32[]{:S(2)}) %all-to-all-start) | async-done | bytes 1342496 | tf_op jit(solution)/shard_map/all_to_all | solution.py:256
  78.7 1.5 %copy-done.3 = bf16[384,2560]{1,0:T(8,128)(2,1)S(1)} copy-done((bf16[384,2560]{1,0:T(8,128)(2,1)S(1)}, bf16[384,2560]{1,0:T(8,128)(2,1)}, u32[]{:S(2)}) %copy-start.3) | copy-done | bytes 1966104
  80.2 1.3 copy-done.5
  81.5 2.6 %shard_map.142 = (bf16[128,2432]{1,0:T(8,128)(2,1)S(1)}, bf16[1280,128]{1,0:T(8,128)(2,1)S(1)}) custom-call(bf16[69,2432]{1,0:T(8,128)(2,1)S(1)} %get-tuple-element.18.own_ref, bf16[4,69,2432]{2,1,0:T(8,128)(2,1)S(1)} %all-to-all-done.all_ref, f32[69,16,128]{2,1,0:T(8,128)S(1)} %copy-done.1, f32[69,384]{1,0:T(8,128)S(1)} %get-tuple-element.19.truth_ref, ...), custom_call_target="tpu_custom_call" | custom-call | flops 640155648 | tf_op jit(solution)/shard_map/pallas_call | solution.py:349
  84.1 12.4 %all_to_all.20 = bf16[32,40,128]{2,1,0:T(8,128)(2,1)S(1)} all-to-all(bf16[32,40,128]{2,1,0:T(8,128)(2,1)S(1)} %bitcast.15), channel_id=1, replica_groups={{0,1,2,3,4,5,6,7,128,129,130,131,132,133,134,135,256,257,258,259,260,26..., dimensions={0} | all-to-all | bytes 655360 | tf_op jit(solution)/shard_map/all_to_all | solution.py:256
  96.6 32.9 %all_to_all.21 = bf16[16,40,128]{2,1,0:T(8,128)(2,1)S(1)} all-to-all(bf16[16,40,128]{2,1,0:T(8,128)(2,1)S(1)} %broadcast_in_dim.22), channel_id=1, replica_groups={{0,16,32,48,64,80,96,112,8,24,40,56,72,88,104,120},{1,17,33,49,65,81,97..., dimensions={0} | all-to-all | bytes 327680 | tf_op jit(solution)/shard_map/all_to_all | solution.py:256
  130.1 3.3 %all-to-all-start.3 = ((bf16[4,40,128]{2,1,0:T(8,128)(2,1)}), bf16[4,40,128]{2,1,0:T(8,128)(2,1)S(1)}, u32[]{:S(2)}, u32[]{:S(2)}) async-start(bf16[4,40,128]{2,1,0:T(8,128)(2,1)} %broadcast_in_dim.23), calls=%async_computation.3 | async-start | bytes 81920 | tf_op jit(solution)/shard_map/all_to_all | solution.py:256
  133.4 3.4 %shard_map.143 = bf16[1,128,16,128]{3,2,1,0:T(8,128)(2,1)} custom-call(s32[2]{0:T(128)S(1)} %add_convert_fusion.pole_ref, bf16[128,2432]{1,0:T(8,128)(2,1)S(1)} %get-tuple-element.22.g_ref, bf16[1152,128]{1,0:T(8,128)(2,1)S(1)} %bitcast.18), custom_call_target="tpu_custom_call" | custom-call | flops 603979776 | tf_op jit(solution)/shard_map/pallas_call | solution.py:359
  136.7 2.1 %all-to-all-done.3 = bf16[4,40,128]{2,1,0:T(8,128)(2,1)S(1)} async-done(((bf16[4,40,128]{2,1,0:T(8,128)(2,1)}), bf16[4,40,128]{2,1,0:T(8,128)(2,1)S(1)}, u32[]{:S(2)}, u32[]{:S(2)}) %all-to-all-start.3) | async-done | bytes 40992 | tf_op jit(solution)/shard_map/all_to_all | solution.py:256
  (46 shorter events, 4.1 us)
Async XLA Ops:
  0.6 1.1 copy-start
  1.7 1.0 copy-start.6
  5.0 20.2 %collective-permute-start.1 = (bf16[208,32]{1,0:T(8,128)(2,1)S(1)}, bf16[208,32]{1,0:T(8,128)(2,1)S(1)}, u32[]{:S(2)}, u32[]{:S(2)}) collective-permute-start(bf16[208,32]{1,0:T(8,128)(2,1)S(1)} %get-tuple-element.16.west_ref), channel_id=1, source_target_pairs={{1,0},{2,1},{3,2},{4,3},{5,4},{6,5},{7,6},{8,7},{9,8},{10,9},{11,1... | collective-permute-start | bytes 39944 | tf_op jit(solution)/shard_map/ppermute | solution.py:316
  21.7 16.4 %collective-permute-start = (bf16[208,32]{1,0:T(8,128)(2,1)S(1)}, bf16[208,32]{1,0:T(8,128)(2,1)S(1)}, u32[]{:S(2)}, u32[]{:S(2)}) collective-permute-start(bf16[208,32]{1,0:T(8,128)(2,1)S(1)} %get-tuple-element.15.east_ref), channel_id=1, source_target_pairs={{0,1},{1,2},{2,3},{3,4},{4,5},{5,6},{6,7},{7,8},{8,9},{9,10},{10,1... | collective-permute-start | bytes 39944 | tf_op jit(solution)/shard_map/ppermute | solution.py:315
  38.4 14.2 %copy-start.7 = (bf16[69,128]{1,0:T(8,128)(2,1)S(1)}, bf16[69,128]{1,0:T(8,128)(2,1)}, u32[]{:S(2)}) copy-start(bf16[69,128]{1,0:T(8,128)(2,1)} %ow_ref.1) | copy-start | bytes 52996
  38.4 14.2 %copy-start.8 = (bf16[128,9,128]{2,0,1:T(8,128)(2,1)S(1)}, bf16[128,9,128]{2,0,1:T(8,128)(2,1)}, u32[]{:S(2)}) copy-start(bf16[128,9,128]{2,0,1:T(8,128)(2,1)} %param.14) | copy-start | bytes 884740
  38.4 14.2 %copy-start.9 = (bf16[264,384]{1,0:T(8,128)(2,1)S(1)}, bf16[264,384]{1,0:T(8,128)(2,1)}, u32[]{:S(2)}) copy-start(bf16[264,384]{1,0:T(8,128)(2,1)} %constant.38.clone.cn_ref) | copy-start | bytes 608260
  38.4 14.2 %copy-start.10 = (bf16[264,384]{1,0:T(8,128)(2,1)S(1)}, bf16[264,384]{1,0:T(8,128)(2,1)}, u32[]{:S(2)}) copy-start(bf16[264,384]{1,0:T(8,128)(2,1)} %constant.39.clone.cs_ref) | copy-start | bytes 608260
  38.4 14.2 %copy-start.11 = (bf16[32,384]{1,0:T(8,128)(2,1)S(1)}, bf16[32,384]{1,0:T(8,128)(2,1)}, u32[]{:S(2)}) copy-start(bf16[32,384]{1,0:T(8,128)(2,1)} %constant.34.clone.cl_ref) | copy-start | bytes 73732
  38.5 14.2 %copy-start.12 = (bf16[32,384]{1,0:T(8,128)(2,1)S(1)}, bf16[32,384]{1,0:T(8,128)(2,1)}, u32[]{:S(2)}) copy-start(bf16[32,384]{1,0:T(8,128)(2,1)} %constant.35.clone.cr_ref) | copy-start | bytes 73732
  38.5 14.2 %copy-start.13 = (bf16[32,384]{1,0:T(8,128)(2,1)S(1)}, bf16[32,384]{1,0:T(8,128)(2,1)}, u32[]{:S(2)}) copy-start(bf16[32,384]{1,0:T(8,128)(2,1)} %constant.36.clone.ce_ref) | copy-start | bytes 73732
  38.5 14.2 %copy-start.14 = (bf16[32,384]{1,0:T(8,128)(2,1)S(1)}, bf16[32,384]{1,0:T(8,128)(2,1)}, u32[]{:S(2)}) copy-start(bf16[32,384]{1,0:T(8,128)(2,1)} %constant.37.clone.cw_ref) | copy-start | bytes 73732
  39.0 7.5 %collective-permute-start.2 = (bf16[208,264]{1,0:T(8,128)(2,1)S(1)}, bf16[208,264]{1,0:T(8,128)(2,1)S(1)}, u32[]{:S(2)}, u32[]{:S(2)}) collective-permute-start(bf16[208,264]{1,0:T(8,128)(2,1)S(1)} %get-tuple-element.27), channel_id=1, source_target_pairs={{0,16},{1,17},{2,18},{3,19},{4,20},{5,21},{6,22},{7,23},{8,0},{9,1... | collective-permute-start | bytes 329480 | tf_op jit(solution)/shard_map/ppermute | solution.py:324
  43.7 8.9 %collective-permute-start.3 = (bf16[208,264]{1,0:T(8,128)(2,1)S(1)}, bf16[208,264]{1,0:T(8,128)(2,1)S(1)}, u32[]{:S(2)}, u32[]{:S(2)}) collective-permute-start(bf16[208,264]{1,0:T(8,128)(2,1)S(1)} %get-tuple-element.26), channel_id=1, source_target_pairs={{16,0},{17,1},{18,2},{19,3},{20,4},{21,5},{22,6},{23,7},{0,8},{1,9... | collective-permute-start | bytes 329480 | tf_op jit(solution)/shard_map/ppermute | solution.py:325
  57.9 1.3 copy-start.2
  59.2 1.1 copy-start.4
  61.5 4.6 %copy-start.15 = (f32[69]{0:T(128)S(1)}, f32[69]{0:T(128)}, u32[]{:S(2)}) copy-start(f32[69]{0:T(128)} %param.18) | copy-start | bytes 832
  61.5 17.2 %copy-start.1 = (f32[69,16,128]{2,1,0:T(8,128)S(1)}, f32[69,16,128]{2,1,0:T(8,128)}, u32[]{:S(2)}) copy-start(f32[69,16,128]{2,1,0:T(8,128)} %target_ref.3) | copy-start | bytes 1695748
  61.5 17.2 %all-to-all-start = ((bf16[4,69,2432]{2,1,0:T(8,128)(2,1)}), bf16[4,69,2432]{2,1,0:T(8,128)(2,1)S(1)}, u32[]{:S(2)}, u32[]{:S(2)}) async-start(bf16[4,69,2432]{2,1,0:T(8,128)(2,1)} %broadcast_in_dim.20), calls=%async_computation | async-start | bytes 2801664 | tf_op jit(solution)/shard_map/all_to_all | solution.py:256
  78.7 1.5 %copy-start.3 = (bf16[384,2560]{1,0:T(8,128)(2,1)S(1)}, bf16[384,2560]{1,0:T(8,128)(2,1)}, u32[]{:S(2)}) copy-start(bf16[384,2560]{1,0:T(8,128)(2,1)} %copy-done.2) | copy-start | bytes 5898244
  80.2 1.3 copy-start.5
  130.1 8.7 %all-to-all-start.3 = ((bf16[4,40,128]{2,1,0:T(8,128)(2,1)}), bf16[4,40,128]{2,1,0:T(8,128)(2,1)S(1)}, u32[]{:S(2)}, u32[]{:S(2)}) async-start(bf16[4,40,128]{2,1,0:T(8,128)(2,1)} %broadcast_in_dim.23), calls=%async_computation.3 | async-start | bytes 81920 | tf_op jit(solution)/shard_map/all_to_all | solution.py:256

commit v4 on v3

v4 whole, which is shorter than its diff:
```python
import functools
import math

import jax
import jax.numpy as jnp
import numpy as np
from jax import lax
from jax.experimental import pallas as pl
from jax.experimental.pallas import tpu as pltpu
from jax.sharding import PartitionSpec as P

smoothing = 0.1
LANES = 128
TAP_QUARTERS = ((0, 1, 2), (3, 4), (5, 6), (7, 8))
VMEM_BYTES = 60 * 2**20
HALO_LANES = 2 * LANES + 16
RIM = 32
f32, bf16 = jnp.float32, jnp.bfloat16


def dot(a, b, dims=(((1,), (0,)), ((), ()))):
    return lax.dot_general(a, b, dims, preferred_element_type=f32)


def tile(index, count=1):
    return slice(index * LANES, (index + count) * LANES)


def signed(d):
    return d * lax.rsqrt(d * d + smoothing * smoothing)


class Copies:
    def __init__(self, sems):
        self.sems, self.made = sems, []

    def start(self, source, goal):
        copy = pltpu.make_async_copy(source, goal, self.sems.at[len(self.made)])
        copy.start()
        self.made.append(copy)
        return copy


def prepare_kernel(odd_ref, x_hbm, target_hbm, flat_hbm, close_hbm, other_hbm, east_hbm, west_hbm, first_hbm, last_hbm,
                   x_ref, target_ref, wide_ref, aim_ref, flat_ref, close_ref, other_ref, east_ref, west_ref, first_ref,
                   last_ref, sems):
    channels, rows, cols = wide_ref.shape
    variables = target_ref.shape[0]
    copies = Copies(sems)
    part = channels // 2
    halves = [slice(k * part, (k + 1) * part) for k in range(2)]
    loads = [copies.start(x_hbm.at[0, here], x_ref.at[here]) for here in halves]
    load_target = copies.start(target_hbm, target_ref)
    cell = lax.broadcasted_iota(jnp.int32, (rows * cols, 4 * rows), 0)
    slot = lax.broadcasted_iota(jnp.int32, (1, 4 * rows), 1)
    column = jnp.where(slot < rows, cols - 1, jnp.where(slot < 2 * rows, cols - 2, jnp.where(slot < 3 * rows, 0, 1)))
    pick = jnp.where(cell == (slot % rows) * cols + column, 1.0, 0.0).astype(bf16)
    aim_ref[variables - variables % 8 :] = jnp.zeros((aim_ref.shape[0] - variables + variables % 8, rows * cols), f32)
    for load, here in zip(loads, halves):
        load.wait()
        wide_ref[here] = x_ref[here].astype(f32)
        for row in range(rows):
            flat_ref[here, tile(row)] = wide_ref[here, row, :].astype(bf16)
    saves = [copies.start(flat_ref, flat_hbm)]
    edges = dot(flat_ref[...], pick)
    load_target.wait()
    for row in range(rows):
        aim_ref[:variables, tile(row)] = target_ref[:, row, :]
    high = aim_ref[...].astype(bf16)
    low = (aim_ref[...] - high.astype(f32)).astype(bf16)
    for ref, near, second in ((first_ref, 0, 1), (last_ref, rows - 1, rows - 2)):
        ref[:channels, :cols] = flat_ref[:, tile(near)]
        ref[:channels, cols:] = flat_ref[:, tile(second)]
        ref[channels:, :cols] = high[:, tile(near)]
        ref[channels:, cols:] = low[:, tile(near)]
    saves += [copies.start(first_ref, first_hbm), copies.start(last_ref, last_hbm)]
    high_edges = dot(high, pick)
    low_edges = dot(low, pick)

    def side(begin):
        aim = jnp.concatenate([high_edges[:, begin : begin + rows], low_edges[:, begin : begin + rows]], axis=1)
        return jnp.concatenate([edges[:, begin : begin + 2 * rows], aim], axis=0)

    east, west = side(0), side(2 * rows)
    lane = lax.broadcasted_iota(jnp.int32, east.shape, 1)
    odd = lane < odd_ref[0] * LANES
    other_ref[...] = jnp.where(odd, east, west).astype(bf16)
    close_ref[...] = jnp.where(odd, west, east).astype(bf16)
    east_ref[...] = east.astype(bf16)
    west_ref[...] = west.astype(bf16)
    for ref, goal in ((other_ref, other_hbm), (close_ref, close_hbm), (east_ref, east_hbm), (west_ref, west_hbm)):
        saves.append(copies.start(ref, goal))
    for save in saves:
        save.wait()


def rim_choice(rows):
    sizes = (2 * rows,) * 4 + (HALO_LANES,) * 2
    sources = [np.zeros((size, 3 * LANES), np.float32) for size in sizes]
    left, right, east, west, north, south = sources
    for row in range(rows):
        lane = row + 2
        left[row, LANES + lane] = 1
        left[rows + row, lane] = 1
        right[row, LANES + RIM + lane] = 1
        right[rows + row, 2 * LANES + RIM + lane] = 1
        east[row, RIM + lane] = 1
        west[row, 2 * LANES + lane] = 1
    for source, lanes in ((north, (1, 0)), (south, (rows + 2, rows + 3))):
        for second, lane in enumerate(lanes):
            source[2 * LANES + second, LANES + lane] = 1
            source[2 * LANES + 2 + second, lane] = 1
            source[2 * LANES + 4 + second, LANES + RIM + lane] = 1
            source[2 * LANES + 6 + second, 2 * LANES + RIM + lane] = 1
            source[second * LANES + LANES - 1, RIM + lane] = 1
            source[second * LANES, 2 * LANES + lane] = 1
    return jnp.asarray(np.concatenate(sources), bf16)


def widen(x3_ref, place, block, before, after):
    channels = block.shape[0]
    lane = lax.broadcasted_iota(jnp.int32, (channels, LANES), 1)
    x3_ref[:channels, place] = jnp.where(lane == 0, before, pltpu.roll(block, 1, 1)).astype(bf16)
    x3_ref[channels : 2 * channels, place] = block.astype(bf16)
    x3_ref[2 * channels :, place] = jnp.where(lane == LANES - 1, after, pltpu.roll(block, LANES - 1, 1)).astype(bf16)


def activate(pre, place, b_ref, ow_ref, ob_ref, slope_ref, out_ref):
    pre = pre + b_ref[...]
    sigmoid = 1.0 / (1.0 + jnp.exp(-pre))
    active = (pre * sigmoid).astype(bf16)
    slope_ref[:, place] = sigmoid * (1.0 + pre * (1.0 - sigmoid))
    out_ref[:, place] = (dot(ow_ref[...], active) + ob_ref[...]).astype(bf16)


def inner_kernel(rows, members, x_hbm, left_hbm, right_hbm, w_hbm, b_hbm, ow_hbm, ob_hbm, all_hbm, slope_hbm, x3_hbm,
                 x_ref, left_ref, right_ref, w_ref, b_ref, ow_ref, ob_ref, out_ref, slope_ref, x3_ref, sems):
    channels = x_ref.shape[0]
    copies = Copies(sems)
    sources = (left_hbm, right_hbm, x_hbm, w_hbm, b_hbm, ow_hbm, ob_hbm)
    goals = (left_ref, right_ref, x_ref, w_ref, b_ref, ow_ref, ob_ref)
    loads = [copies.start(source, goal) for source, goal in zip(sources, goals)]
    for load in loads[:3]:
        load.wait()
    left = left_ref[:channels].astype(f32)
    right = right_ref[:channels].astype(f32)
    for row in range(rows):
        block = x_ref[:, tile(row)].astype(f32)
        widen(x3_ref, tile(row), block, left[:, row : row + 1], right[:, row : row + 1])
    saves = [copies.start(x3_ref, x3_hbm.at[:, tile(1, rows)])]
    for load in loads[3:]:
        load.wait()
    weights = w_ref[...].T
    pairs = rows // 2 - 1
    done = 0
    for stop in ((pairs + 1) // 2, pairs):
        for pair in range(done, stop):
            pre = None
            for tap_row in range(3):
                taps = weights[:, tap_row * 3 * channels : (tap_row + 1) * 3 * channels]
                term = dot(taps, x3_ref[:, tile(2 * pair + tap_row, 2)])
                pre = term if pre is None else pre + term
            activate(pre, tile(2 * pair, 2), b_ref, ow_ref, ob_ref, slope_ref, out_ref)
        lanes = tile(2 * done, 2 * (stop - done))
        goal = tile(2 * done + 2, 2 * (stop - done))
        saves.append(copies.start(slope_ref.at[:, lanes], slope_hbm.at[:, goal]))
        for member in range(members):
            saves.append(copies.start(out_ref.at[:, lanes], all_hbm.at[member, :, goal]))
        done = stop
    for save in saves:
        save.wait()


def outer_kernel(rows, members, north_ref, south_ref, odd_ref, all_in, slope_in, x3_in, other_hbm, close_hbm, left_hbm, right_hbm, east_hbm,
                 west_hbm, choice_hbm, w_hbm, b_hbm, ow_hbm, ob_hbm, all_hbm, slope_hbm, x3_hbm, truth_hbm,
                 other_ref, close_ref, left_ref, right_ref, east_ref, west_ref, choice_ref, w_ref, b_ref, ow_ref, ob_ref,
                 truth_ref, out_ref, slope_ref, near_ref, sems):
    del all_in, slope_in
    channels = slope_ref.shape[0]
    variables = out_ref.shape[0]
    copies = Copies(sems)
    loads = [
        copies.start(close_hbm, close_ref),
        copies.start(other_hbm, other_ref),
        copies.start(x3_in.at[:, tile(1, 2)], near_ref.at[:, tile(2, 2)]),
        copies.start(x3_in.at[:, tile(rows - 1, 2)], near_ref.at[:, tile(4, 2)]),
        copies.start(w_hbm, w_ref),
        copies.start(b_hbm, b_ref),
        copies.start(ow_hbm, ow_ref),
        copies.start(ob_hbm, ob_ref),
        copies.start(left_hbm, left_ref),
        copies.start(right_hbm, right_ref),
        copies.start(east_hbm, east_ref),
        copies.start(west_hbm, west_ref),
        copies.start(choice_hbm, choice_ref),
    ]
    lane3 = lax.broadcasted_iota(jnp.int32, (3 * channels, LANES), 1)
    loads[0].wait()
    loads[1].wait()
    close, other = close_ref[...].astype(f32), other_ref[...].astype(f32)
    odd = lax.broadcasted_iota(jnp.int32, close.shape, 1) < odd_ref[0] * HALO_LANES
    north, south = jnp.where(odd, close, other), jnp.where(odd, other, close)
    poles = north_ref[0], south_ref[0]
    for halo, spots in ((north, (1, 0)), (south, (6, 7))):
        halo = halo[:channels]
        for second, spot in enumerate(spots):
            before = halo[:, 2 * LANES + second : 2 * LANES + second + 1]
            after = halo[:, 2 * LANES + 4 + second : 2 * LANES + 5 + second]
            widen(near_ref, tile(spot), halo[:, tile(second)], before, after)
    for load in loads[2:8]:
        load.wait()
    saves = [
        copies.start(near_ref.at[:, tile(1)], x3_hbm.at[:, tile(0)]),
        copies.start(near_ref.at[:, tile(6)], x3_hbm.at[:, tile(rows + 1)]),
    ]
    weights = w_ref[...].T

    def taps(tap_row):
        return weights[:, tap_row * 3 * channels : (tap_row + 1) * 3 * channels]

    def beyond(above, middle, below, turned):
        pre = dot(taps(1), middle.astype(bf16))
        pre = pre + dot(taps(0), jnp.where(turned, below, above).astype(bf16))
        return pre + dot(taps(2), jnp.where(turned, above, below).astype(bf16))

    def finish(pre, place):
        activate(pre, place, b_ref, ow_ref, ob_ref, slope_ref, out_ref)

    for spot, place in ((2, 1), (5, 2)):
        pre = dot(taps(0), near_ref[:, tile(spot - 1)])
        pre = pre + dot(taps(1), near_ref[:, tile(spot)]) + dot(taps(2), near_ref[:, tile(spot + 1)])
        finish(pre, tile(place))
    for spot, place, pole in ((1, 0, poles[0]), (6, 3, poles[1])):
        above, below = near_ref[:, tile(spot - 1)].astype(f32), near_ref[:, tile(spot + 1)].astype(f32)
        finish(beyond(above, near_ref[:, tile(spot)], below, lane3 < pole * LANES), tile(place))
    for load in loads[8:]:
        load.wait()
    rim, begin = 0.0, 0
    sources = (left_ref[...], right_ref[...], east_ref[...], west_ref[...], north.astype(bf16), south.astype(bf16))
    for source in sources:
        rim = rim + dot(source, choice_ref[begin : begin + source.shape[1]])
        begin += source.shape[1]
    middle = jnp.concatenate([rim[:channels, tile(k)] for k in range(3)], axis=0)
    first = (lane3 == 1) | (lane3 == RIM + 1)
    last = (lane3 == rows + 2) | (lane3 == RIM + rows + 2)
    turned = (first & (lane3 < poles[0] * LANES)) | (last & (lane3 < poles[1] * LANES))
    finish(beyond(pltpu.roll(middle, 1, 1), middle, pltpu.roll(middle, LANES - 1, 1), turned), tile(4))
    for lanes, goal in ((tile(0, 2), tile(0, 2)), (tile(2, 3), tile(rows, 3))):
        for member in range(members):
            saves.append(copies.start(out_ref.at[:, lanes], all_hbm.at[member, :, goal]))
        saves.append(copies.start(slope_ref.at[:, lanes], slope_hbm.at[:, goal]))
    aim = slice(channels, channels + variables)
    for place, halo in ((0, north), (1, south)):
        truth_ref[:, tile(place)] = halo[aim, tile(0)] + halo[aim, tile(1)]
    side = lax.broadcasted_iota(jnp.int32, (variables, LANES), 1)
    truth_ref[:, tile(2)] = rim[aim, tile(1)] + jnp.where(side < RIM, rim[aim, tile(0)], rim[aim, tile(2)])
    saves.append(copies.start(truth_ref, truth_hbm))
    for save in saves:
        save.wait()


def weight_kernel(rows, shares, members, member_ref, all_hbm, target_hbm, truth_hbm, vw_hbm, owt_hbm, slope_hbm, x3_hbm,
                  g_hbm, term_hbm, truth_ref, vw_ref, owt_ref, g_ref, term_ref, all_ref, target_ref, out_grad_ref,
                  slope_ref, x3_ref, sems):
    channels = g_ref.shape[0]
    tiles = rows + 3
    cuts = ((0, 6), (6, 12), (12, tiles))
    copies = Copies(sems)
    first = [copies.start(vw_hbm, vw_ref), copies.start(truth_hbm, truth_ref), copies.start(target_hbm, target_ref)]
    blocks = []
    for start, stop in cuts:
        place = tile(start, stop - start)
        blocks.append(copies.start(all_hbm.at[:, :, place], all_ref.at[:, :, place]))
    later = [copies.start(owt_hbm, owt_ref), copies.start(slope_hbm, slope_ref), copies.start(x3_hbm, x3_ref)]
    for load in first:
        load.wait()

    def truth(q):
        if q == 0:
            return truth_ref[:, tile(0)]
        if q > rows:
            return truth_ref[:, tile(q - rows)]
        return target_ref[:, q - 1, :]

    for number, (start, stop) in enumerate(cuts):
        blocks[number].wait()
        for q in range(start, stop, 2):
            count = min(2, stop - q)
            place = tile(q, count)
            own = all_ref[member_ref[0], :, place].astype(f32)
            total = jnp.zeros_like(own)
            for member in range(members):
                total = total + signed(own - all_ref[member, :, place].astype(f32))
            fit = signed(own - jnp.concatenate([truth(q + n) for n in range(count)], axis=1))
            grad = vw_ref[...] * (fit / members - total / (members * (members - 1)))
            out_grad_ref[:, place] = grad.astype(bf16)
    later[0].wait()
    later[1].wait()
    for q in range(0, tiles, 2):
        place = tile(q, min(2, tiles - q))
        g_ref[:, place] = (dot(owt_ref[...], out_grad_ref[:, place]) * slope_ref[:, place]).astype(bf16)
    save = copies.start(g_ref, g_hbm)
    later[2].wait()
    grad_pre = g_ref[:, tile(1, rows)]
    terms = []
    for tap_row in range(3):
        terms.append(dot(x3_ref[:, tile(tap_row, rows)], grad_pre, (((1,), (1,)), ((), ()))))
    size = channels // shares
    pieces = []
    for quarter in TAP_QUARTERS:
        for spot in range(shares // 2):
            for share in (spot, spot + shares // 2):
                for tap in quarter:
                    begin = (tap % 3) * channels + share * size
                    pieces.append(terms[tap // 3][begin : begin + size])
                for _ in range(3 - len(quarter)):
                    pieces.append(jnp.zeros((size, channels), f32))
    term_ref[...] = jnp.concatenate(pieces, axis=0).astype(bf16)
    copies.start(term_ref, term_hbm).wait()
    save.wait()


def feature_kernel(north_ref, south_ref, g_hbm, w_hbm, out_hbm, g_ref, w_ref, out_ref, wide_ref, sems):
    channels, rows, cols = wide_ref.shape
    copies = Copies(sems)
    for load in (copies.start(g_hbm, g_ref), copies.start(w_hbm, w_ref)):
        load.wait()
    north_pole, south_pole = north_ref[0], south_ref[0]
    lane = lax.broadcasted_iota(jnp.int32, (channels, LANES), 1)

    def taps(tap_row):
        return w_ref[tap_row * 3 * channels : (tap_row + 1) * 3 * channels, :]

    def split(value, turned):
        kept = jnp.where(turned, 0.0, value)
        return kept.astype(bf16), (value - kept).astype(bf16)

    north, north_turned = split(g_ref[:, tile(0)].astype(f32), lane < north_pole * LANES)
    south, south_turned = split(g_ref[:, tile(rows + 1)].astype(f32), lane < south_pole * LANES)
    rim = g_ref[:, tile(rows + 2)].astype(f32)
    above, below = pltpu.roll(rim, 1, 1), pltpu.roll(rim, LANES - 1, 1)
    first = (lane == 2) | (lane == RIM + 2)
    last = (lane == rows + 1) | (lane == RIM + rows + 1)
    above, above_turned = split(above, first & (lane < north_pole * LANES))
    below, below_turned = split(below, last & (lane < south_pole * LANES))
    side = dot(taps(1), rim.astype(bf16))
    side = side + dot(taps(2), above) + dot(taps(0), below)
    side = side + dot(taps(0), above_turned) + dot(taps(2), below_turned)
    from_left, from_right = side[2 * channels :], side[:channels]

    for pair in range(rows // 2):
        row = 2 * pair
        upper = g_ref[:, tile(row, 2)]
        lower = g_ref[:, tile(row + 2, 2)]
        if pair == 0:
            upper = jnp.concatenate([north, g_ref[:, tile(1)]], axis=1)
        if pair == rows // 2 - 1:
            lower = jnp.concatenate([g_ref[:, tile(rows)], south], axis=1)
        spread = dot(taps(1), g_ref[:, tile(row + 1, 2)]) + dot(taps(2), upper) + dot(taps(0), lower)
        for part in range(2):
            block = spread[:, tile(part)]
            if row + part == 0:
                block = block + dot(taps(0), north_turned)
            if row + part == rows - 1:
                block = block + dot(taps(2), south_turned)
            spot = row + part + 2
            moved_west = pltpu.roll(block[:channels], LANES - 1, 1)
            moved_east = pltpu.roll(block[2 * channels :], 1, 1)
            total = block[channels : 2 * channels]
            total = total + jnp.where(lane == 0, from_left[:, spot : spot + 1], moved_east)
            total = total + jnp.where(lane == LANES - 1, from_right[:, RIM + spot : RIM + spot + 1], moved_west)
            wide_ref[:, row + part, :] = total
    out_ref[0] = wide_ref[...].astype(bf16)
    copies.start(out_ref, out_hbm).wait()


def exchange(pieces, groups):
    return lax.all_to_all(
        pieces, ("ens", "lat", "lon"), split_axis=0, concat_axis=0, axis_index_groups=groups, tiled=True
    )


def pallas(kernel, out_shape, flags, operands, scratch, copies, aliases=None, flops=0, nbytes=0):
    hbm = pl.BlockSpec(memory_space=pltpu.HBM)
    return pl.pallas_call(
        kernel,
        out_shape=out_shape,
        in_specs=[pl.BlockSpec(memory_space=pltpu.SMEM)] * len(flags) + [hbm] * len(operands),
        out_specs=(hbm,) * len(out_shape),
        scratch_shapes=[pltpu.VMEM(*spec) for spec in scratch] + [pltpu.SemaphoreType.DMA((copies,))],
        input_output_aliases=aliases or {},
        compiler_params=pltpu.CompilerParams(vmem_limit_bytes=VMEM_BYTES),
        cost_estimate=pl.CostEstimate(flops=flops, bytes_accessed=nbytes, transcendentals=0),
    )(*flags, *operands)


def like(*arrays):
    return [(array.shape, array.dtype) for array in arrays]


def on_device(features, conv_weight, conv_bias, out_weight, out_bias, var_weight, target):
    channels, rows, cols = features.shape[1:]
    variables = out_weight.shape[0]
    members = lax.axis_size("ens")
    bands, loops = lax.axis_size("lat"), lax.axis_size("lon")
    half = loops // 2
    member, band, loop = (lax.axis_index(axis) for axis in ("ens", "lat", "lon"))
    cells = rows * cols
    inner, outer = cells - 2 * cols, 5 * cols
    halo = -(-(channels + variables) // 16) * 16
    shape = jax.ShapeDtypeStruct
    odd_loop, odd_band = loop % 2 == 1, band % 2 == 1
    flags = [flag[None].astype(jnp.int32) for flag in (band == 0, band == bands - 1, odd_band)]

    close_loops = [(i, i ^ 1) for i in range(loops)]
    other_loops = [(i, (i + 1 if i % 2 else i - 1) % loops) for i in range(loops)]
    close_bands = [(b, b ^ 1) for b in range(bands)]
    other_bands = []
    for b in range(bands):
        other = b + 1 if b % 2 else b - 1
        for i in range(loops):
            goal = other * loops + i if 0 <= other < bands else b * loops + (i + half) % loops
            other_bands.append((b * loops + i, goal))

    def place(member, band, spot):
        return (member * bands + band) * loops + spot

    level_groups = [
        [place(e, b, h * half + s) for e in range(members) for s in range(half)] for b in range(bands) for h in range(2)
    ]
    column_groups = [
        [place(e, b, h * half + s) for h in range(2) for b in range(bands)] for e in range(members) for s in range(half)
    ]
    member_groups = [[place(e, b, s) for e in range(members)] for b in range(bands) for s in range(loops)]

    side, edge = shape((halo, 2 * rows), bf16), shape((halo, 2 * cols), bf16)
    prepared = (shape((channels, cells), bf16), side, side, side, side, edge, edge)
    flat, close, other, east, west, first, last = pallas(
        prepare_kernel,
        prepared,
        (odd_loop[None].astype(jnp.int32),),
        (features, target),
        [((channels, rows, cols), bf16), (target.shape, f32), ((channels, rows, cols), f32)]
        + [((halo - channels, cells), f32)] + like(*prepared),
        10,
    )
    got_close = lax.ppermute(close, "lon", close_loops)
    got_other = lax.ppermute(other, "lon", other_loops)
    left = jnp.where(~odd_loop, got_other, got_close)
    right = jnp.where(odd_loop, got_other, got_close)

    def with_corners(edge, near, second):
        picks = [side[:, k : k + 1] for side in (left, right) for k in (near, second, rows + near, rows + second)]
        return jnp.concatenate([edge] + picks + [jnp.zeros((halo, HALO_LANES - 2 * cols - 8), bf16)], axis=1)

    first = with_corners(first, 0, 1)
    last = with_corners(last, rows - 1, rows - 2)
    got_close = lax.ppermute(jnp.where(odd_band, first, last), "lat", close_bands)
    got_other = lax.ppermute(jnp.where(odd_band, last, first), ("lat", "lon"), other_bands)

    weights = conv_weight.transpose(1, 0, 2).reshape(9 * channels, channels)
    bias = (weights, conv_bias[:, None], out_weight, out_bias[:, None])
    whole = (
        shape((members, variables, inner + outer), bf16),
        shape((channels, inner + outer), f32),
        shape((3 * channels, cells + 2 * cols), bf16),
    )
    operands = (flat, left, right, *bias)
    everyone, slope, x3 = pallas(
        functools.partial(inner_kernel, rows, members),
        whole,
        (),
        operands,
        like(*operands) + [((variables, inner), bf16), ((channels, inner), f32), ((3 * channels, cells), bf16)],
        8 + 2 * (members + 1),
        flops=2 * inner * channels * (9 * channels + variables),
        nbytes=8 * 2**20,
    )
    operands = (got_other, got_close, left, right, east, west, rim_choice(rows), *bias)
    beyond = shape((variables, 3 * cols), f32)
    everyone, slope, x3, truth = pallas(
        functools.partial(outer_kernel, rows, members),
        (*whole, beyond),
        flags,
        (everyone, slope, x3, *operands),
        like(*operands, beyond)
        + [((variables, outer), bf16), ((channels, outer), f32), ((3 * channels, 8 * cols), bf16)],
        16 + 2 * (members + 1),
        aliases={3: 0, 4: 1, 5: 2},
        flops=2 * outer * channels * (9 * channels + variables),
    )
    everyone = exchange(everyone, member_groups)

    operands = (truth, var_weight[:, None], out_weight.T)
    results = (shape((channels, inner + outer), bf16), shape((12 * channels, channels), bf16))
    grads, terms = pallas(
        functools.partial(weight_kernel, rows, loops, members),
        results,
        (member[None].astype(jnp.int32),),
        (everyone, target, *operands, slope, x3),
        like(*operands, *results, everyone, target) + [((variables, inner + outer), bf16)] + like(slope, x3),
        11,
        flops=2 * cells * channels * (9 * channels + variables),
    )

    size = 3 * channels // loops
    terms = exchange(terms.reshape(members * half, 2 * size, channels), level_groups)
    terms = jnp.sum(terms.astype(f32), axis=0).astype(bf16)

    results = (shape((1, channels, rows, cols), bf16),)
    (grad_features,) = pallas(
        feature_kernel,
        results,
        flags[:2],
        (grads, weights),
        like(grads, weights, *results) + [((channels, rows, cols), f32)],
        3,
        flops=2 * cells * channels * 9 * channels,
    )

    terms = jnp.broadcast_to(terms.reshape(2, 1, size, channels), (2, bands, size, channels))
    terms = exchange(terms.reshape(2 * bands, size, channels), column_groups)
    terms = jnp.sum(terms.astype(f32), axis=0).astype(bf16)
    grad_features, terms = lax.optimization_barrier((grad_features, terms))
    terms = exchange(jnp.broadcast_to(terms, (members, size, channels)), member_groups)
    share = [terms[k, : len(quarter) * channels // loops] for k, quarter in enumerate(TAP_QUARTERS)]
    share = jnp.concatenate(share, axis=0).astype(f32)
    total_cells = members * cells * bands * loops
    grad_weight = (share / math.sqrt(total_cells)).reshape(9, channels // loops, channels).transpose(1, 0, 2)
    return grad_features, grad_weight


def solution(mesh):
    return jax.shard_map(
        on_device,
        mesh=mesh,
        in_specs=(P("ens", None, "lat", "lon"), P(), P(), P(), P(), P(), P(None, "lat", "lon")),
        out_specs=(P("ens", None, "lat", "lon"), P("lon", None, None)),
        check_vma=False,
    )
```

time: 140 us -> 125 us (0.89)
  blocking collectives: 45.3 us -> 21.8 us
  starting transfers between devices: 33 us -> 49.2 us
  waiting for transfers between devices: 34.4 us -> 22.4 us
  Pallas kernels: 13.4 us -> 23.1 us
  local copies, waits for them, and re-layouts: 11.7 us -> 6.07 us
    all_to_all x2, blocking collectives: 45.3 us -> 21.8 us  [exchange(): lax.all_to_all(pieces, ('ens', 'lat', 'lon'), split_axis=0, concat_axis=0...]
    ppermute x4, waiting for transfers between devices: 19.8 us -> 1.4 us  [the longest x1 1.26 us: on_device(): got_close = lax.ppermute(close, 'lon', close_loops)]
    pallas_call x4 -> x5, Pallas kernels: 13.4 us -> 23.1 us  [pallas(): pl.pallas_call(kernel, out_shape=out_shape, in_specs=[pl.BlockSpec(memory...]
    all_to_all x2, starting transfers between devices: 7.7 us -> 16.3 us  [exchange(): lax.all_to_all(pieces, ('ens', 'lat', 'lon'), split_axis=0, concat_axis=0...]
    ppermute x4, starting transfers between devices: 25.3 us -> 32.9 us  [the longest x1 16.8 us: on_device(): got_other = lax.ppermute(other, 'lon', other_loops)]
    all_to_all x2, waiting for transfers between devices: 14.6 us -> 21 us  [exchange(): lax.all_to_all(pieces, ('ens', 'lat', 'lon'), split_axis=0, concat_axis=0...]
    unnamed x33 -> x23, local copies, waits for them, and re-layouts: 7.46 us -> 2.55 us
    broadcast_in_dim x5 -> x4, local copies, waits for them, and re-layouts: 2.86 us -> 2.83 us  [the longest x2 1.45 us: on_device(): bias = (weights, conv_bias[:, None], out_weight, out_bias[:, None])]
  transfers between devices with their start and end apart: 6 -> 6, of which waited for: 5 -> 4; matrix products, arithmetic and copies ran while one was open for 1% -> 2% of each run, Pallas kernels for 2% -> 7%
where the time goes in v4:
time: 125 us; the launch traced here: 124 us
  starting transfers between devices  49.2 us (39%)
  Pallas kernels  23.1 us (18%)
  waiting for transfers between devices  22.4 us (18%)
  blocking collectives  21.8 us (17%)
  local copies, waits for them, and re-layouts  6.07 us (5%)
    pallas_call x5, Pallas kernels, pallas(): pl.pallas_call(kernel, out_shape=out_shape, in_specs=[pl.BlockSpec(memory...  23.1 us
    all_to_all x2, blocking collectives, exchange(): lax.all_to_all(pieces, ('ens', 'lat', 'lon'), split_axis=0, concat_axis=0...  21.8 us
    all_to_all x2, waiting for transfers between devices, exchange(): lax.all_to_all(pieces, ('ens', 'lat', 'lon'), split_axis=0, concat_axis=0...  21 us
    ppermute x1, starting transfers between devices, on_device(): got_other = lax.ppermute(other, 'lon', other_loops)  16.8 us
    all_to_all x2, starting transfers between devices, exchange(): lax.all_to_all(pieces, ('ens', 'lat', 'lon'), split_axis=0, concat_axis=0...  16.3 us
    ppermute x1, starting transfers between devices, on_device(): lax.ppermute(jnp.where(odd_band, first, last), 'lat', close_bands)  11.2 us
    ppermute x1, starting transfers between devices, on_device(): lax.ppermute(jnp.where(odd_band, last, first), ('lat', 'lon'), other_bands)  2.93 us
    unnamed x23, local copies, waits for them, and re-layouts  2.55 us
  transfers between devices with their start and end apart: 6, of which 4 were waited for; matrix products, arithmetic and copies ran while one was open for 2% of the time, Pallas kernels for 7%

profile of v4, /device:TPU:32, one launch (start us, length us, event | category | flops | bytes accessed | tf_op | source)
XLA Modules:
  0.0 124.3 jit_solution(14327537216285987020)
XLA Ops:
  0.6 4.2 %shard_map.95 = (bf16[128,2048]{1,0:T(8,128)(2,1)}, bf16[208,32]{1,0:T(8,128)(2,1)}, bf16[208,32]{1,0:T(8,128)(2,1)}, bf16[208,32]{1,0:T(8,128)(2,1)}, bf16[208,...) custom-call(s32[1]{0:T(128)} %bitcast.4.odd_ref, bf16[1,128,16,128]{3,2,1,0:T(8,128)(2,1)} %x_hbm.1, ...), custom_call_target="tpu_custom_call" | custom-call | tf_op jit(solution)/shard_map/pallas_call | solution.py:385
  4.8 16.8 %collective-permute-start = (bf16[208,32]{1,0:T(8,128)(2,1)}, bf16[208,32]{1,0:T(8,128)(2,1)S(1)}, u32[]{:S(2)}, u32[]{:S(2)}) collective-permute-start(bf16[208,32]{1,0:T(8,128)(2,1)} %get-tuple-element.21), channel_id=1, source_target_pairs={{0,15},{1,2},{2,1},{3,4},{4,3},{5,6},{6,5},{7,8},{8,7},{9,10},{10,... | collective-permute-start | bytes 39944 | tf_op jit(solution)/shard_map/ppermute | solution.py:448
  21.7 1.9 %collective-permute-start.1 = (bf16[208,32]{1,0:T(8,128)(2,1)}, bf16[208,32]{1,0:T(8,128)(2,1)S(1)}, u32[]{:S(2)}, u32[]{:S(2)}) collective-permute-start(bf16[208,32]{1,0:T(8,128)(2,1)} %get-tuple-element.22), channel_id=1, source_target_pairs={{0,1},{1,0},{2,3},{3,2},{4,5},{5,4},{6,7},{7,6},{8,9},{9,8},{10,11... | collective-permute-start | bytes 39944 | tf_op jit(solution)/shard_map/ppermute | solution.py:447
  23.8 1.3 %collective-permute-done.1 = bf16[208,32]{1,0:T(8,128)(2,1)S(1)} collective-permute-done((bf16[208,32]{1,0:T(8,128)(2,1)}, bf16[208,32]{1,0:T(8,128)(2,1)S(1)}, u32[]{:S(2)}, u32[]{:S(2)}) %collective-permute-start.1) | collective-permute-done | bytes 13344 | tf_op jit(solution)/shard_map/ppermute | solution.py:447
  25.9 2.9 %collective-permute-start.2 = (bf16[208,272]{1,0:T(8,128)(2,1)S(1)}, bf16[208,272]{1,0:T(8,128)(2,1)S(1)}, u32[]{:S(2)}, u32[]{:S(2)}) collective-permute-start(bf16[208,272]{1,0:T(8,128)(2,1)S(1)} %get-tuple-element.39), channel_id=1, source_target_pairs={{0,8},{1,9},{2,10},{3,11},{4,12},{5,13},{6,14},{7,15},{8,0},{9,1},... | collective-permute-start | bytes 339464 | tf_op jit(solution)/shard_map/ppermute | solution.py:459
  28.8 11.2 %collective-permute-start.3 = (bf16[208,272]{1,0:T(8,128)(2,1)S(1)}, bf16[208,272]{1,0:T(8,128)(2,1)S(1)}, u32[]{:S(2)}, u32[]{:S(2)}) collective-permute-start(bf16[208,272]{1,0:T(8,128)(2,1)S(1)} %get-tuple-element.38), channel_id=1, source_target_pairs={{0,16},{16,0},{32,48},{48,32},{64,80},{80,64},{96,112},{112,96},{1... | collective-permute-start | bytes 339464 | tf_op jit(solution)/shard_map/ppermute | solution.py:458
  40.1 0.7 copy.19.b_hbm
  40.8 0.7 copy.20.ob_hbm
  41.5 5.4 %shard_map.96 = (bf16[4,69,2432]{2,1,0:T(8,128)(2,1)}, f32[128,2432]{1,0:T(8,128)}, bf16[384,2304]{1,0:T(8,128)(2,1)}) custom-call(bf16[128,2048]{1,0:T(8,128)(2,1)} %get-tuple-element.20.x_hbm, bf16[208,32]{1,0:T(8,128)(2,1)} %copy-done.2, bf16[208,32]{1,0:T(8,128)(2,1)} %copy-done.1, bf16[1152,128]{1,0:T(8,128)(2,1)} %bitcast.28, f32[128,1]{1,0:T(8,128)} %copy.19.b_hbm, ...), custom_call_target="tpu_custom_call" | custom-call | flops 560136192 | bytes 8388608 | tf_op jit(solution)/shard_map/pallas_call | solution.py:385
  47.0 0.6 copy-done.3
  47.6 4.7 %shard_map.97 = (bf16[4,69,2432]{2,1,0:T(8,128)(2,1)}, f32[128,2432]{1,0:T(8,128)}, bf16[384,2304]{1,0:T(8,128)(2,1)}, f32[69,384]{1,0:T(8,128)}) custom-call(s32[1]{0:T(128)} %bitcast.north_ref, s32[1]{0:T(128)} %bitcast.1.south_ref, s32[1]{0:T(128)} %bitcast.3.odd_ref, ...), custom_call_target="tpu_custom_call", output_to_operand_aliasing={{0}: (3, {}), {1}: (4, {}), {2}: (5, {})} | custom-call | flops 200048640 | tf_op jit(solution)/shard_map/pallas_call | solution.py:385
  52.3 4.7 %all-to-all-start = ((bf16[4,69,2432]{2,1,0:T(8,128)(2,1)}), bf16[4,69,2432]{2,1,0:T(8,128)(2,1)S(1)}, u32[]{:S(2)}, u32[]{:S(2)}) async-start(bf16[4,69,2432]{2,1,0:T(8,128)(2,1)} %get-tuple-element.30), calls=%async_computation | async-start | bytes 2801664 | tf_op jit(solution)/shard_map/all_to_all | solution.py:378
  57.0 0.7 copy.23
  57.8 0.7 copy.24.vw_hbm
  58.5 11.3 %all-to-all-done.all_hbm = bf16[4,69,2432]{2,1,0:T(8,128)(2,1)S(1)} async-done(((bf16[4,69,2432]{2,1,0:T(8,128)(2,1)}), bf16[4,69,2432]{2,1,0:T(8,128)(2,1)S(1)}, u32[]{:S(2)}, u32[]{:S(2)}) %all-to-all-start) | async-done | bytes 1342496 | tf_op jit(solution)/shard_map/all_to_all | solution.py:378
  69.8 1.1 copy-done
  70.9 4.9 %shard_map.98 = (bf16[128,2432]{1,0:T(8,128)(2,1)}, bf16[1536,128]{1,0:T(8,128)(2,1)}) custom-call(s32[1]{0:T(128)} %bitcast.2.member_ref, bf16[4,69,2432]{2,1,0:T(8,128)(2,1)} %copy-done, f32[69,16,128]{2,1,0:T(8,128)} %target_hbm.3, f32[69,384]{1,0:T(8,128)} %get-tuple-element.31.truth_hbm, f32[69,1]{1,0:T(8,128)} %copy.24.vw_hbm, ...), custom_call_target="tpu_custom_call" | custom-call | flops 640155648 | tf_op jit(solution)/shard_map/pallas_call | solution.py:385
  75.8 13.8 %all_to_all.20 = bf16[32,48,128]{2,1,0:T(8,128)(2,1)S(1)} all-to-all(bf16[32,48,128]{2,1,0:T(8,128)(2,1)} %bitcast.27), channel_id=1, replica_groups={{0,1,2,3,4,5,6,7,128,129,130,131,132,133,134,135,256,257,258,259,260,26..., dimensions={0} | all-to-all | bytes 786432 | tf_op jit(solution)/shard_map/all_to_all | solution.py:378
  89.8 0.7 broadcast_in_dim.31
  90.4 11.6 %all-to-all-start.2 = ((bf16[16,24,128]{2,1,0:T(8,128)(2,1)}), bf16[16,24,128]{2,1,0:T(8,128)(2,1)S(1)}, u32[]{:S(2)}, u32[]{:S(2)}) async-start(bf16[16,24,128]{2,1,0:T(8,128)(2,1)} %bitcast.13), calls=%async_computation.2 | async-start | bytes 196608 | tf_op jit(solution)/shard_map/all_to_all | solution.py:378
  102.0 4.0 %shard_map.99 = bf16[1,128,16,128]{3,2,1,0:T(8,128)(2,1)} custom-call(s32[1]{0:T(128)} %bitcast.north_ref, s32[1]{0:T(128)} %bitcast.1.south_ref, bf16[128,2432]{1,0:T(8,128)(2,1)} %get-tuple-element.34.g_hbm, bf16[1152,128]{1,0:T(8,128)(2,1)} %bitcast.30), custom_call_target="tpu_custom_call" | custom-call | flops 603979776 | tf_op jit(solution)/shard_map/pallas_call | solution.py:385
  106.0 9.7 %all-to-all-done.2 = bf16[16,24,128]{2,1,0:T(8,128)(2,1)S(1)} async-done(((bf16[16,24,128]{2,1,0:T(8,128)(2,1)}), bf16[16,24,128]{2,1,0:T(8,128)(2,1)S(1)}, u32[]{:S(2)}, u32[]{:S(2)}) %all-to-all-start.2) | async-done | bytes 98336 | tf_op jit(solution)/shard_map/all_to_all | solution.py:378
  115.7 7.9 %all_to_all.21 = bf16[4,24,128]{2,1,0:T(8,128)(2,1)S(1)} all-to-all(bf16[4,24,128]{2,1,0:T(8,128)(2,1)S(1)} %broadcast_in_dim.32), channel_id=1, replica_groups={{0,128,256,384},{1,129,257,385},{2,130,258,386},{3,131,259,387},{4,132,..., dimensions={0} | all-to-all | bytes 49152 | tf_op jit(solution)/shard_map/all_to_all | solution.py:378
  123.7 0.6 multiply_bitcast_fusion
  (35 shorter events, 1.1 us)
Async XLA Ops:
  4.8 20.6 %copy-start.6 = (bf16[208,256]{1,0:T(8,128)(2,1)S(1)}, bf16[208,256]{1,0:T(8,128)(2,1)}, u32[]{:S(2)}) copy-start(bf16[208,256]{1,0:T(8,128)(2,1)} %get-tuple-element.27) | copy-start | bytes 319492
  4.8 20.8 %copy-start.5 = (bf16[208,256]{1,0:T(8,128)(2,1)S(1)}, bf16[208,256]{1,0:T(8,128)(2,1)}, u32[]{:S(2)}) copy-start(bf16[208,256]{1,0:T(8,128)(2,1)} %get-tuple-element.26) | copy-start | bytes 319492
  4.8 18.9 %collective-permute-start = (bf16[208,32]{1,0:T(8,128)(2,1)}, bf16[208,32]{1,0:T(8,128)(2,1)S(1)}, u32[]{:S(2)}, u32[]{:S(2)}) collective-permute-start(bf16[208,32]{1,0:T(8,128)(2,1)} %get-tuple-element.21), channel_id=1, source_target_pairs={{0,15},{1,2},{2,1},{3,4},{4,3},{5,6},{6,5},{7,8},{8,7},{9,10},{10,... | collective-permute-start | bytes 39944 | tf_op jit(solution)/shard_map/ppermute | solution.py:448
  21.7 3.3 %collective-permute-start.1 = (bf16[208,32]{1,0:T(8,128)(2,1)}, bf16[208,32]{1,0:T(8,128)(2,1)S(1)}, u32[]{:S(2)}, u32[]{:S(2)}) collective-permute-start(bf16[208,32]{1,0:T(8,128)(2,1)} %get-tuple-element.22), channel_id=1, source_target_pairs={{0,1},{1,0},{2,3},{3,2},{4,5},{5,4},{6,7},{7,6},{8,9},{9,8},{10,11... | collective-permute-start | bytes 39944 | tf_op jit(solution)/shard_map/ppermute | solution.py:447
  25.0 0.8 copy-start.1
  25.1 0.8 copy-start.2
  25.3 14.8 %copy-start.8 = (f32[128]{0:T(128)S(1)}, f32[128]{0:T(128)}, u32[]{:S(2)}) copy-start(f32[128]{0:T(128)} %param.10) | copy-start | bytes 1540
  25.3 15.6 %copy-start.9 = (f32[69]{0:T(128)S(1)}, f32[69]{0:T(128)}, u32[]{:S(2)}) copy-start(f32[69]{0:T(128)} %param.12) | copy-start | bytes 832
  25.9 21.0 %collective-permute-start.2 = (bf16[208,272]{1,0:T(8,128)(2,1)S(1)}, bf16[208,272]{1,0:T(8,128)(2,1)S(1)}, u32[]{:S(2)}, u32[]{:S(2)}) collective-permute-start(bf16[208,272]{1,0:T(8,128)(2,1)S(1)} %get-tuple-element.39), channel_id=1, source_target_pairs={{0,8},{1,9},{2,10},{3,11},{4,12},{5,13},{6,14},{7,15},{8,0},{9,1},... | collective-permute-start | bytes 339464 | tf_op jit(solution)/shard_map/ppermute | solution.py:459
  28.8 18.1 %collective-permute-start.3 = (bf16[208,272]{1,0:T(8,128)(2,1)S(1)}, bf16[208,272]{1,0:T(8,128)(2,1)S(1)}, u32[]{:S(2)}, u32[]{:S(2)}) collective-permute-start(bf16[208,272]{1,0:T(8,128)(2,1)S(1)} %get-tuple-element.38), channel_id=1, source_target_pairs={{0,16},{16,0},{32,48},{48,32},{64,80},{80,64},{96,112},{112,96},{1... | collective-permute-start | bytes 339464 | tf_op jit(solution)/shard_map/ppermute | solution.py:458
  46.9 0.7 copy-start.3
  46.9 0.7 copy-start.4
  52.3 4.7 %copy-start.7 = (bf16[69,128]{1,0:T(8,128)(2,1)S(1)}, bf16[69,128]{1,0:T(8,128)(2,1)}, u32[]{:S(2)}) copy-start(bf16[69,128]{1,0:T(8,128)(2,1)} %ow_hbm.3) | copy-start | bytes 52996
  52.3 5.4 %copy-start.10 = (f32[69]{0:T(128)S(1)}, f32[69]{0:T(128)}, u32[]{:S(2)}) copy-start(f32[69]{0:T(128)} %param.13) | copy-start | bytes 832
  52.3 17.5 %all-to-all-start = ((bf16[4,69,2432]{2,1,0:T(8,128)(2,1)}), bf16[4,69,2432]{2,1,0:T(8,128)(2,1)S(1)}, u32[]{:S(2)}, u32[]{:S(2)}) async-start(bf16[4,69,2432]{2,1,0:T(8,128)(2,1)} %get-tuple-element.30), calls=%async_computation | async-start | bytes 2801664 | tf_op jit(solution)/shard_map/all_to_all | solution.py:378
  69.8 1.1 copy-start
  90.4 25.3 %all-to-all-start.2 = ((bf16[16,24,128]{2,1,0:T(8,128)(2,1)}), bf16[16,24,128]{2,1,0:T(8,128)(2,1)S(1)}, u32[]{:S(2)}, u32[]{:S(2)}) async-start(bf16[16,24,128]{2,1,0:T(8,128)(2,1)} %bitcast.13), calls=%async_computation.2 | async-start | bytes 196608 | tf_op jit(solution)/shard_map/all_to_all | solution.py:378

commit v5 on v4

v5 whole, which is shorter than its diff:
```python
import functools
import math

import jax
import jax.numpy as jnp
import numpy as np
from jax import lax
from jax.experimental import pallas as pl
from jax.experimental.pallas import tpu as pltpu
from jax.sharding import PartitionSpec as P

smoothing = 0.1
LANES = 128
TAP_QUARTERS = ((0, 1, 2), (3, 4), (5, 6), (7, 8))
VMEM_BYTES = 60 * 2**20
ROOMY = 50 * 10**6
FAR = 138 * 10**5
HALO_LANES = 2 * LANES + 16
RIM = 32
f32, bf16 = jnp.float32, jnp.bfloat16


def dot(a, b, dims=(((1,), (0,)), ((), ()))):
    return lax.dot_general(a, b, dims, preferred_element_type=f32)


def tile(index, count=1):
    return slice(index * LANES, (index + count) * LANES)


def signed(d):
    return d * lax.rsqrt(d * d + smoothing * smoothing)


class Copies:
    def __init__(self, sems):
        self.sems, self.made = sems, []

    def start(self, source, goal):
        copy = pltpu.make_async_copy(source, goal, self.sems.at[len(self.made)])
        copy.start()
        self.made.append(copy)
        return copy


class Plan:
    def __init__(self, channels, variables, rows):
        halo = channels + -(-variables // 16) * 16
        tall = -(-variables // 16) * 16
        self.x3 = (slice(0, 3 * channels), tile(0, rows + 2))
        top = 3 * channels
        self.flat = (slice(top, top + channels), tile(0, rows))
        top += channels
        sources = 4 * rows + LANES + 2 * HALO_LANES
        self.weights = (slice(top, top + channels), tile(0, 9))
        self.choice = (slice(top, top + sources), tile(9, 3))
        self.first = (slice(top, top + halo), tile(12, 2))
        self.last = (slice(top, top + halo), tile(14, 2))
        self.mix = (slice(top, top + tall), tile(16))
        self.mix_turned = (slice(top, top + channels), tile(17))
        self.sides = (slice(top + halo, top + 2 * halo), tile(12))
        self.rows16 = top + max(sources, 2 * halo)
        self.slope = (slice(0, channels), tile(0, rows + 3))
        self.truth = (slice(channels, channels + -(-variables // 8) * 8), tile(0, 3))
        top = channels + tall
        self.bias = (slice(top, top + LANES), tile(0))
        self.out_bias = (slice(top, top + LANES), tile(1))
        self.var_weight = (slice(top, top + LANES), tile(2))
        top += LANES
        self.aim = (slice(top, top + tall), tile(0, rows))
        self.rows32 = top + tall


def prepare_kernel(plan, odd_ref, x_hbm, target_hbm, far16, far32, close_hbm, other_hbm,
                   x_ref, target_ref, wide_ref, aim_ref, flat_ref, close_ref, other_ref, sides_ref, first_ref,
                   last_ref, sems):
    channels, rows, cols = wide_ref.shape
    variables = target_ref.shape[0]
    copies = Copies(sems)
    part = channels // 2
    halves = [slice(k * part, (k + 1) * part) for k in range(2)]
    loads = [copies.start(x_hbm.at[0, here], x_ref.at[here]) for here in halves]
    load_target = copies.start(target_hbm, target_ref)
    cell = lax.broadcasted_iota(jnp.int32, (rows * cols, 4 * rows), 0)
    slot = lax.broadcasted_iota(jnp.int32, (1, 4 * rows), 1)
    column = jnp.where(slot < rows, cols - 1, jnp.where(slot < 2 * rows, cols - 2, jnp.where(slot < 3 * rows, 0, 1)))
    pick = jnp.where(cell == (slot % rows) * cols + column, 1.0, 0.0).astype(bf16)
    aim_ref[variables - variables % 8 :] = jnp.zeros((aim_ref.shape[0] - variables + variables % 8, rows * cols), f32)
    for load, here in zip(loads, halves):
        load.wait()
        wide_ref[here] = x_ref[here].astype(f32)
        for row in range(rows):
            flat_ref[here, tile(row)] = wide_ref[here, row, :].astype(bf16)
    saves = [copies.start(flat_ref, far16.at[*plan.flat])]
    edges = dot(flat_ref[...], pick)
    load_target.wait()
    for row in range(rows):
        aim_ref[:variables, tile(row)] = target_ref[:, row, :]
    saves.append(copies.start(aim_ref, far32.at[*plan.aim]))
    high = aim_ref[...].astype(bf16)
    low = (aim_ref[...] - high.astype(f32)).astype(bf16)
    for ref, near, second in ((first_ref, 0, 1), (last_ref, rows - 1, rows - 2)):
        ref[:channels, :cols] = flat_ref[:, tile(near)]
        ref[:channels, cols:] = flat_ref[:, tile(second)]
        ref[channels:, :cols] = high[:, tile(near)]
        ref[channels:, cols:] = low[:, tile(near)]
    saves += [copies.start(first_ref, far16.at[*plan.first]), copies.start(last_ref, far16.at[*plan.last])]
    high_edges = dot(high, pick)
    low_edges = dot(low, pick)

    def side(begin):
        aim = jnp.concatenate([high_edges[:, begin : begin + rows], low_edges[:, begin : begin + rows]], axis=1)
        return jnp.concatenate([edges[:, begin : begin + 2 * rows], aim], axis=0)

    east, west = side(0), side(2 * rows)
    lane = lax.broadcasted_iota(jnp.int32, east.shape, 1)
    odd = lane < odd_ref[0] * LANES
    other_ref[...] = jnp.where(odd, east, west).astype(bf16)
    close_ref[...] = jnp.where(odd, west, east).astype(bf16)
    sides_ref[...] = jnp.zeros(sides_ref.shape, bf16)
    sides_ref[:, : 4 * rows] = jnp.concatenate([east, west], axis=1).astype(bf16)
    for ref, goal in ((other_ref, other_hbm), (close_ref, close_hbm), (sides_ref, far16.at[*plan.sides])):
        saves.append(copies.start(ref, goal))
    for save in saves:
        save.wait()


def pack_kernel(plan, far16_in, far32_in, w_hbm, choice_hbm, mix_ref, b_ref, ob_ref, vw_ref, far16, far32,
                w_ref, choice_ref, w_turned_ref, tall_ref, mix16_ref, turned_ref, row_ref, columns_ref, sems):
    del far16_in, far32_in
    variables = mix_ref.shape[0]
    copies = Copies(sems)
    load_w, load_choice = copies.start(w_hbm, w_ref), copies.start(choice_hbm, choice_ref)
    saves = []
    tall_ref[...] = jnp.zeros(tall_ref.shape, f32)
    tall_ref[:variables] = mix_ref[...].astype(f32)
    mix16_ref[...] = tall_ref[: mix16_ref.shape[0]].astype(bf16)
    turned_ref[...] = tall_ref[...].T.astype(bf16)
    saves.append(copies.start(mix16_ref, far16.at[*plan.mix]))
    saves.append(copies.start(turned_ref, far16.at[*plan.mix_turned]))
    row_ref[...] = jnp.zeros(row_ref.shape, f32)
    for number, (ref, goal) in enumerate(((b_ref, plan.bias), (ob_ref, plan.out_bias), (vw_ref, plan.var_weight))):
        row_ref[:1, : ref.shape[1]] = ref[...]
        columns_ref[number] = jnp.broadcast_to(row_ref[:1], (LANES, LANES)).T
        saves.append(copies.start(columns_ref.at[number], far32.at[*goal]))
    load_choice.wait()
    saves.append(copies.start(choice_ref, far16.at[*plan.choice]))
    load_w.wait()
    w_turned_ref[...] = w_ref[...].T
    saves.append(copies.start(w_turned_ref, far16.at[*plan.weights]))
    for save in saves:
        save.wait()


def fetch_kernel(places16, places32, far16, far32, *refs):
    copies = Copies(refs[-1])
    sources = [far16.at[*place] for place in places16] + [far32.at[*place] for place in places32]
    for load in [copies.start(source, ref) for source, ref in zip(sources, refs)]:
        load.wait()


def corner_kernel(rows, odd_loop_ref, odd_band_ref, other_ref, close_ref, first_ref, last_ref,
                  left_ref, right_ref, send_other_ref, send_close_ref):
    other, close = other_ref[...].astype(f32), close_ref[...].astype(f32)
    odd = lax.broadcasted_iota(jnp.int32, other.shape, 1) < odd_loop_ref[0] * LANES
    left = jnp.where(odd, close, other).astype(bf16)
    right = jnp.where(odd, other, close).astype(bf16)
    left_ref[...] = left
    right_ref[...] = right
    source = lax.broadcasted_iota(jnp.int32, (2 * rows, 32), 0)
    goal = lax.broadcasted_iota(jnp.int32, (2 * rows, 32), 1)
    nth, spot = goal % 4, goal % 16
    wanted = jnp.where(goal < 16, nth % 2, rows - 1 - nth % 2) + (nth // 2) * rows
    hit = source == wanted
    from_left = jnp.where(hit & (spot < 4), 1.0, 0.0).astype(bf16)
    from_right = jnp.where(hit & (spot >= 4) & (spot < 8), 1.0, 0.0).astype(bf16)
    corners = dot(left, from_left) + dot(right, from_right)
    first, last = first_ref[...].astype(f32), last_ref[...].astype(f32)
    odd_band = odd_band_ref[0] * HALO_LANES
    odd = lax.broadcasted_iota(jnp.int32, first.shape, 1) < odd_band
    send_other_ref[:, : 2 * LANES] = jnp.where(odd, last, first).astype(bf16)
    send_close_ref[:, : 2 * LANES] = jnp.where(odd, first, last).astype(bf16)
    odd = lax.broadcasted_iota(jnp.int32, (first.shape[0], 16), 1) < odd_band
    send_other_ref[:, 2 * LANES :] = jnp.where(odd, corners[:, 16:], corners[:, :16]).astype(bf16)
    send_close_ref[:, 2 * LANES :] = jnp.where(odd, corners[:, :16], corners[:, 16:]).astype(bf16)


def rim_choice(rows):
    sizes = (2 * rows,) * 2 + (LANES,) + (HALO_LANES,) * 2
    sources = [np.zeros((size, 3 * LANES), np.float32) for size in sizes]
    left, right, sides, north, south = sources
    for row in range(rows):
        lane = row + 2
        left[row, LANES + lane] = 1
        left[rows + row, lane] = 1
        right[row, LANES + RIM + lane] = 1
        right[rows + row, 2 * LANES + RIM + lane] = 1
        sides[row, RIM + lane] = 1
        sides[2 * rows + row, 2 * LANES + lane] = 1
    for source, lanes in ((north, (1, 0)), (south, (rows + 2, rows + 3))):
        for second, lane in enumerate(lanes):
            source[2 * LANES + second, LANES + lane] = 1
            source[2 * LANES + 2 + second, lane] = 1
            source[2 * LANES + 4 + second, LANES + RIM + lane] = 1
            source[2 * LANES + 6 + second, 2 * LANES + RIM + lane] = 1
            source[second * LANES + LANES - 1, RIM + lane] = 1
            source[second * LANES, 2 * LANES + lane] = 1
    return jnp.asarray(np.concatenate(sources), bf16)


def widen(x3_ref, place, block, before, after):
    channels = block.shape[0]
    lane = lax.broadcasted_iota(jnp.int32, (channels, LANES), 1)
    x3_ref[:channels, place] = jnp.where(lane == 0, before, pltpu.roll(block, 1, 1)).astype(bf16)
    x3_ref[channels : 2 * channels, place] = block.astype(bf16)
    x3_ref[2 * channels :, place] = jnp.where(lane == LANES - 1, after, pltpu.roll(block, LANES - 1, 1)).astype(bf16)


def activate(pre, place, bias, mix, out_bias, slope_ref, out_ref):
    pre = pre + bias
    sigmoid = 1.0 / (1.0 + jnp.exp(-pre))
    active = (pre * sigmoid).astype(bf16)
    slope_ref[:, place] = sigmoid * (1.0 + pre * (1.0 - sigmoid))
    out = dot(mix, active) + out_bias[: mix.shape[0]]
    out_ref[:, place] = out[: out_ref.shape[0]].astype(bf16)


def inner_kernel(rows, left_ref, right_ref, x_ref, w_ref, mix_ref, b_ref, ob_ref, out_ref, slope_ref, x3_ref):
    channels = x_ref.shape[0]
    left = left_ref[:channels].astype(f32)
    right = right_ref[:channels].astype(f32)
    for row in range(rows):
        block = x_ref[:, tile(row)].astype(f32)
        widen(x3_ref, tile(row), block, left[:, row : row + 1], right[:, row : row + 1])
    bias, out_bias = b_ref[:, :1], ob_ref[:, :1]
    for pair in range(rows // 2 - 1):
        pre = None
        for tap_row in range(3):
            taps = w_ref[:, tap_row * 3 * channels : (tap_row + 1) * 3 * channels]
            term = dot(taps, x3_ref[:, tile(2 * pair + tap_row, 2)])
            pre = term if pre is None else pre + term
        activate(pre, tile(2 * pair, 2), bias, mix_ref[...], out_bias, slope_ref, out_ref)


def outer_kernel(plan, rows, members, north_ref, south_ref, odd_ref, other_ref, close_ref, in_out_ref, in_slope_ref,
                 in_x3_ref, left_ref, right_ref, w_ref, mix_ref, choice_ref, sides_ref, b_ref, ob_ref, far16_in, far32_in,
                 all_hbm, far16, far32, truth_ref, out_ref, slope_ref, near_ref, sems):
    channels = slope_ref.shape[0]
    variables = out_ref.shape[0]
    copies = Copies(sems)
    del far16_in, far32_in
    slope_hbm, x3_hbm = far32.at[*plan.slope], far16.at[*plan.x3]
    saves = [copies.start(in_out_ref, all_hbm.at[member, :, tile(2, rows - 2)]) for member in range(members)]
    saves.append(copies.start(in_slope_ref, slope_hbm.at[:, tile(2, rows - 2)]))
    saves.append(copies.start(in_x3_ref, x3_hbm.at[:, tile(1, rows)]))
    near_ref[:, tile(2, 2)] = in_x3_ref[:, tile(0, 2)]
    near_ref[:, tile(4, 2)] = in_x3_ref[:, tile(rows - 2, 2)]
    lane3 = lax.broadcasted_iota(jnp.int32, (3 * channels, LANES), 1)
    close, other = close_ref[...].astype(f32), other_ref[...].astype(f32)
    odd = lax.broadcasted_iota(jnp.int32, close.shape, 1) < odd_ref[0] * HALO_LANES
    north, south = jnp.where(odd, close, other), jnp.where(odd, other, close)
    poles = north_ref[0], south_ref[0]
    for halo, spots in ((north, (1, 0)), (south, (6, 7))):
        halo = halo[:channels]
        for second, spot in enumerate(spots):
            before = halo[:, 2 * LANES + second : 2 * LANES + second + 1]
            after = halo[:, 2 * LANES + 4 + second : 2 * LANES + 5 + second]
            widen(near_ref, tile(spot), halo[:, tile(second)], before, after)
    saves += [
        copies.start(near_ref.at[:, tile(1)], x3_hbm.at[:, tile(0)]),
        copies.start(near_ref.at[:, tile(6)], x3_hbm.at[:, tile(rows + 1)]),
    ]
    bias, out_bias = b_ref[:, :1], ob_ref[:, :1]

    def taps(tap_row):
        return w_ref[:, tap_row * 3 * channels : (tap_row + 1) * 3 * channels]

    def beyond(above, middle, below, turned):
        pre = dot(taps(1), middle.astype(bf16))
        pre = pre + dot(taps(0), jnp.where(turned, below, above).astype(bf16))
        return pre + dot(taps(2), jnp.where(turned, above, below).astype(bf16))

    def finish(pre, place):
        activate(pre, place, bias, mix_ref[...], out_bias, slope_ref, out_ref)

    for spot, place in ((2, 1), (5, 2)):
        pre = dot(taps(0), near_ref[:, tile(spot - 1)])
        pre = pre + dot(taps(1), near_ref[:, tile(spot)]) + dot(taps(2), near_ref[:, tile(spot + 1)])
        finish(pre, tile(place))
    for spot, place, pole in ((1, 0, poles[0]), (6, 3, poles[1])):
        above, below = near_ref[:, tile(spot - 1)].astype(f32), near_ref[:, tile(spot + 1)].astype(f32)
        finish(beyond(above, near_ref[:, tile(spot)], below, lane3 < pole * LANES), tile(place))
    rim, begin = 0.0, 0
    sources = (left_ref[...], right_ref[...], sides_ref[...], north.astype(bf16), south.astype(bf16))
    for source in sources:
        rim = rim + dot(source, choice_ref[begin : begin + source.shape[1]])
        begin += source.shape[1]
    middle = jnp.concatenate([rim[:channels, tile(k)] for k in range(3)], axis=0)
    first = (lane3 == 1) | (lane3 == RIM + 1)
    last = (lane3 == rows + 2) | (lane3 == RIM + rows + 2)
    turned = (first & (lane3 < poles[0] * LANES)) | (last & (lane3 < poles[1] * LANES))
    finish(beyond(pltpu.roll(middle, 1, 1), middle, pltpu.roll(middle, LANES - 1, 1), turned), tile(4))
    for lanes, goal in ((tile(0, 2), tile(0, 2)), (tile(2, 3), tile(rows, 3))):
        for member in range(members):
            saves.append(copies.start(out_ref.at[:, lanes], all_hbm.at[member, :, goal]))
        saves.append(copies.start(slope_ref.at[:, lanes], slope_hbm.at[:, goal]))
    aim = slice(channels, channels + truth_ref.shape[0])
    for place, halo in ((0, north), (1, south)):
        truth_ref[:, tile(place)] = halo[aim, tile(0)] + halo[aim, tile(1)]
    side = lax.broadcasted_iota(jnp.int32, (truth_ref.shape[0], LANES), 1)
    truth_ref[:, tile(2)] = rim[aim, tile(1)] + jnp.where(side < RIM, rim[aim, tile(0)], rim[aim, tile(2)])
    saves.append(copies.start(truth_ref, far32.at[*plan.truth]))
    for save in saves:
        save.wait()


def weight_kernel(plan, rows, shares, members, member_ref, all_ref, far16, far32, g_hbm, term_hbm,
                  truth_ref, vw_ref, owt_ref, g_ref, term_ref, target_ref, out_grad_ref, slope_ref, x3_ref, sems):
    channels = g_ref.shape[0]
    variables = out_grad_ref.shape[0]
    tiles = rows + 3
    copies = Copies(sems)
    first = [
        copies.start(far32.at[*plan.var_weight], vw_ref),
        copies.start(far32.at[*plan.truth], truth_ref),
        copies.start(far32.at[*plan.aim], target_ref),
    ]
    later = [
        copies.start(far16.at[*plan.mix_turned], owt_ref),
        copies.start(far32.at[*plan.slope], slope_ref),
        copies.start(far16.at[*plan.x3], x3_ref),
    ]
    for load in first:
        load.wait()
    scale = vw_ref[:variables, :1]

    def truth(q):
        if q == 0:
            return truth_ref[:variables, tile(0)]
        if q > rows:
            return truth_ref[:variables, tile(q - rows)]
        return target_ref[:variables, tile(q - 1)]

    for q in range(0, tiles, 2):
        count = min(2, tiles - q)
        place = tile(q, count)
        own = all_ref[member_ref[0], :, place].astype(f32)
        total = jnp.zeros_like(own)
        for member in range(members):
            total = total + signed(own - all_ref[member, :, place].astype(f32))
        fit = signed(own - jnp.concatenate([truth(q + n) for n in range(count)], axis=1))
        grad = scale * (fit / members - total / (members * (members - 1)))
        out_grad_ref[:, place] = grad.astype(bf16)
    later[0].wait()
    later[1].wait()
    for q in range(0, tiles, 2):
        place = tile(q, min(2, tiles - q))
        g_ref[:, place] = (dot(owt_ref[:, :variables], out_grad_ref[:, place]) * slope_ref[:, place]).astype(bf16)
    save = copies.start(g_ref, g_hbm.at[:channels])
    later[2].wait()
    grad_pre = g_ref[:, tile(1, rows)]
    terms = []
    for tap_row in range(3):
        terms.append(dot(x3_ref[:, tile(tap_row, rows)], grad_pre, (((1,), (1,)), ((), ()))))
    size = channels // shares
    pieces = []
    for quarter in TAP_QUARTERS:
        for spot in range(shares // 2):
            for share in (spot, spot + shares // 2):
                for tap in quarter:
                    begin = (tap % 3) * channels + share * size
                    pieces.append(terms[tap // 3][begin : begin + size])
                for _ in range(3 - len(quarter)):
                    pieces.append(jnp.zeros((size, channels), f32))
    term_ref[...] = jnp.concatenate(pieces, axis=0).astype(bf16)
    copies.start(term_ref, term_hbm).wait()
    save.wait()


def feature_kernel(north_ref, south_ref, g_hbm, w_hbm, out_hbm, g_ref, w_ref, out_ref, wide_ref, sems):
    channels, rows, cols = wide_ref.shape
    copies = Copies(sems)
    for load in (copies.start(g_hbm.at[: g_ref.shape[0]], g_ref), copies.start(w_hbm, w_ref)):
        load.wait()
    north_pole, south_pole = north_ref[0], south_ref[0]
    lane = lax.broadcasted_iota(jnp.int32, (channels, LANES), 1)

    def taps(tap_row):
        return w_ref[tap_row * 3 * channels : (tap_row + 1) * 3 * channels, :]

    def split(value, turned):
        kept = jnp.where(turned, 0.0, value)
        return kept.astype(bf16), (value - kept).astype(bf16)

    north, north_turned = split(g_ref[:, tile(0)].astype(f32), lane < north_pole * LANES)
    south, south_turned = split(g_ref[:, tile(rows + 1)].astype(f32), lane < south_pole * LANES)
    rim = g_ref[:, tile(rows + 2)].astype(f32)
    above, below = pltpu.roll(rim, 1, 1), pltpu.roll(rim, LANES - 1, 1)
    first = (lane == 2) | (lane == RIM + 2)
    last = (lane == rows + 1) | (lane == RIM + rows + 1)
    above, above_turned = split(above, first & (lane < north_pole * LANES))
    below, below_turned = split(below, last & (lane < south_pole * LANES))
    side = dot(taps(1), rim.astype(bf16))
    side = side + dot(taps(2), above) + dot(taps(0), below)
    side = side + dot(taps(0), above_turned) + dot(taps(2), below_turned)
    from_left, from_right = side[2 * channels :], side[:channels]

    for pair in range(rows // 2):
        row = 2 * pair
        upper = g_ref[:, tile(row, 2)]
        lower = g_ref[:, tile(row + 2, 2)]
        if pair == 0:
            upper = jnp.concatenate([north, g_ref[:, tile(1)]], axis=1)
        if pair == rows // 2 - 1:
            lower = jnp.concatenate([g_ref[:, tile(rows)], south], axis=1)
        spread = dot(taps(1), g_ref[:, tile(row + 1, 2)]) + dot(taps(2), upper) + dot(taps(0), lower)
        for part in range(2):
            block = spread[:, tile(part)]
            if row + part == 0:
                block = block + dot(taps(0), north_turned)
            if row + part == rows - 1:
                block = block + dot(taps(2), south_turned)
            spot = row + part + 2
            moved_west = pltpu.roll(block[:channels], LANES - 1, 1)
            moved_east = pltpu.roll(block[2 * channels :], 1, 1)
            total = block[channels : 2 * channels]
            total = total + jnp.where(lane == 0, from_left[:, spot : spot + 1], moved_east)
            total = total + jnp.where(lane == LANES - 1, from_right[:, RIM + spot : RIM + spot + 1], moved_west)
            wide_ref[:, row + part, :] = total
    out_ref[0] = wide_ref[...].astype(bf16)
    copies.start(out_ref, out_hbm).wait()


def exchange(pieces, groups):
    return lax.all_to_all(
        pieces, ("ens", "lat", "lon"), split_axis=0, concat_axis=0, axis_index_groups=groups, tiled=True
    )


def pallas(kernel, out_shape, flags, operands, scratch, copies, outs="", vmem=VMEM_BYTES, near=(), aliases=None, flops=0, nbytes=0):
    hbm, vmem_spec = (pl.BlockSpec(memory_space=space) for space in (pltpu.HBM, pltpu.VMEM))
    return pl.pallas_call(
        kernel,
        out_shape=out_shape,
        in_specs=[pl.BlockSpec(memory_space=pltpu.SMEM)] * len(flags)
        + [vmem_spec if number in near else hbm for number in range(len(operands))],
        out_specs=tuple(vmem_spec if place == "v" else hbm for place in (outs or "h" * len(out_shape))),
        scratch_shapes=[pltpu.VMEM(*spec) for spec in scratch] + [pltpu.SemaphoreType.DMA((copies,))] * (copies > 0),
        input_output_aliases=aliases or {},
        compiler_params=pltpu.CompilerParams(vmem_limit_bytes=vmem),
        cost_estimate=pl.CostEstimate(flops=flops, bytes_accessed=nbytes, transcendentals=0),
    )(*flags, *operands)


def like(*arrays):
    return [(array.shape, array.dtype) for array in arrays]


def on_device(features, conv_weight, conv_bias, out_weight, out_bias, var_weight, target):
    channels, rows, cols = features.shape[1:]
    variables = out_weight.shape[0]
    members = lax.axis_size("ens")
    bands, loops = lax.axis_size("lat"), lax.axis_size("lon")
    half = loops // 2
    member, band, loop = (lax.axis_index(axis) for axis in ("ens", "lat", "lon"))
    cells = rows * cols
    inner, outer = cells - 2 * cols, 5 * cols
    halo = -(-(channels + variables) // 16) * 16
    shape = jax.ShapeDtypeStruct
    odd_loop, odd_band = loop % 2 == 1, band % 2 == 1
    flags = [flag[None].astype(jnp.int32) for flag in (band == 0, band == bands - 1, odd_band)]

    close_loops = [(i, i ^ 1) for i in range(loops)]
    other_loops = [(i, (i + 1 if i % 2 else i - 1) % loops) for i in range(loops)]
    close_bands = [(b, b ^ 1) for b in range(bands)]
    other_bands = []
    for b in range(bands):
        other = b + 1 if b % 2 else b - 1
        for i in range(loops):
            goal = other * loops + i if 0 <= other < bands else b * loops + (i + half) % loops
            other_bands.append((b * loops + i, goal))

    def place(member, band, spot):
        return (member * bands + band) * loops + spot

    level_groups = [
        [place(e, b, h * half + s) for e in range(members) for s in range(half)] for b in range(bands) for h in range(2)
    ]
    column_groups = [
        [place(e, b, h * half + s) for h in range(2) for b in range(bands)] for e in range(members) for s in range(half)
    ]
    member_groups = [[place(e, b, s) for e in range(members)] for b in range(bands) for s in range(loops)]

    plan = Plan(channels, variables, rows)

    def far(least, width, dtype):
        count = -(-FAR // (width * jnp.dtype(dtype).itemsize))
        return shape((-(-max(count, least) // 16) * 16, width), dtype)

    side, edge = shape((halo, 2 * rows), bf16), shape((halo, 2 * cols), bf16)
    aim = shape((halo - channels, cells), f32)
    wholes = (far(plan.rows16, cells + 2 * cols, bf16), far(plan.rows32, inner + outer, f32))
    far16, far32, close, other = pallas(
        functools.partial(prepare_kernel, plan),
        (*wholes, side, side),
        (odd_loop[None].astype(jnp.int32),),
        (features, target),
        [((channels, rows, cols), bf16), (target.shape, f32), ((channels, rows, cols), f32)]
        + like(aim) + [((channels, cells), bf16)] + like(side, side) + [((halo, LANES), bf16)] + like(edge, edge),
        10,
    )
    got_other = lax.ppermute(other, "lon", other_loops)
    got_close = lax.ppermute(close, "lon", close_loops)

    tall = halo - channels
    choice_rows = 4 * rows + LANES + 2 * HALO_LANES
    weights = conv_weight.transpose(1, 0, 2).reshape(9 * channels, channels)
    far16, far32 = pallas(
        functools.partial(pack_kernel, plan),
        wholes,
        (),
        (far16, far32, weights, rim_choice(rows), out_weight, conv_bias[None], out_bias[None], var_weight[None]),
        [(weights.shape, bf16), ((choice_rows, 3 * LANES), bf16), (weights.shape[::-1], bf16)]
        + [((LANES, LANES), f32), ((tall, LANES), bf16), ((LANES, LANES), bf16), ((8, LANES), f32)]
        + [((3, LANES, LANES), f32)],
        9,
        near=(4, 5, 6, 7),
        aliases={0: 0, 1: 1},
        nbytes=4 * 2**20,
    )
    places16 = (plan.flat, plan.weights, plan.mix, plan.choice, plan.sides, plan.first, plan.last)
    places32 = (plan.bias, plan.out_bias)
    fetched = [
        shape((place[0].stop - place[0].start, place[1].stop - place[1].start), dtype)
        for places, dtype in ((places16, bf16), (places32, f32))
        for place in places
    ]
    flat, turned, mix, choice, sides, first, last, bias, out_bias = pallas(
        functools.partial(fetch_kernel, places16, places32),
        fetched,
        (),
        (far16, far32),
        (),
        len(fetched),
        outs="v" * len(fetched),
        vmem=ROOMY,
        nbytes=4 * 2**20,
    )
    left, right, other, close = pallas(
        functools.partial(corner_kernel, rows),
        (side, side, shape((halo, HALO_LANES), bf16), shape((halo, HALO_LANES), bf16)),
        (odd_loop[None].astype(jnp.int32), flags[2]),
        (got_other, got_close, first, last),
        (),
        0,
        outs="vvvv",
        vmem=ROOMY,
        near=range(4),
    )
    got_other = lax.ppermute(other, ("lat", "lon"), other_bands)
    got_close = lax.ppermute(close, "lat", close_bands)

    inner_out, inner_slope, inner_x3 = pallas(
        functools.partial(inner_kernel, rows),
        (shape((variables, inner), bf16), shape((channels, inner), f32), shape((3 * channels, cells), bf16)),
        (),
        (left, right, flat, turned, mix, bias, out_bias),
        (),
        0,
        outs="vvv",
        vmem=ROOMY,
        near=range(7),
        flops=2 * inner * channels * (9 * channels + variables),
        nbytes=8 * 2**20,
    )
    beyond = ((-(-variables // 8) * 8, 3 * cols), f32)
    everyone, far16, far32 = pallas(
        functools.partial(outer_kernel, plan, rows, members),
        (shape((members, variables, inner + outer), bf16), *wholes),
        flags,
        (
            got_other, got_close, inner_out, inner_slope, inner_x3, left, right,
            turned, mix, choice, sides, bias, out_bias, far16, far32,
        ),
        [beyond, ((variables, outer), bf16), ((channels, outer), f32), ((3 * channels, 8 * cols), bf16)],
        5 + 4 + 2 * (members + 1),
        vmem=ROOMY,
        near=range(13),
        aliases={16: 1, 17: 2},
        flops=2 * outer * channels * (9 * channels + variables),
    )
    everyone = exchange(everyone, member_groups)

    results = (far(channels, inner + outer, bf16), shape((12 * channels, channels), bf16))
    grads_spec = ((channels, inner + outer), bf16)
    grads, terms = pallas(
        functools.partial(weight_kernel, plan, rows, loops, members),
        results,
        (member[None].astype(jnp.int32),),
        (everyone, far16, far32),
        [beyond, ((LANES, LANES), f32), ((channels, LANES), bf16), grads_spec] + like(results[1], aim)
        + [((variables, inner + outer), bf16), ((channels, inner + outer), f32)]
        + [((3 * channels, cells + 2 * cols), bf16)],
        8,
        vmem=ROOMY,
        near=(0,),
        flops=2 * cells * channels * (9 * channels + variables),
    )

    size = 3 * channels // loops
    terms = exchange(terms.reshape(members * half, 2 * size, channels), level_groups)
    terms = jnp.sum(terms.astype(f32), axis=0).astype(bf16)

    results = (shape((1, channels, rows, cols), bf16),)
    (grad_features,) = pallas(
        feature_kernel,
        results,
        flags[:2],
        (grads, weights),
        [grads_spec] + like(weights, *results) + [((channels, rows, cols), f32)],
        3,
        flops=2 * cells * channels * 9 * channels,
    )

    terms = jnp.broadcast_to(terms.reshape(2, 1, size, channels), (2, bands, size, channels))
    terms = exchange(terms.reshape(2 * bands, size, channels), column_groups)
    terms = jnp.sum(terms.astype(f32), axis=0).astype(bf16)
    grad_features, terms = lax.optimization_barrier((grad_features, terms))
    terms = exchange(jnp.broadcast_to(terms, (members, size, channels)), member_groups)
    share = [terms[k, : len(quarter) * channels // loops] for k, quarter in enumerate(TAP_QUARTERS)]
    share = jnp.concatenate(share, axis=0).astype(f32)
    total_cells = members * cells * bands * loops
    grad_weight = (share / math.sqrt(total_cells)).reshape(9, channels // loops, channels).transpose(1, 0, 2)
    return grad_features, grad_weight


def solution(mesh):
    return jax.shard_map(
        on_device,
        mesh=mesh,
        in_specs=(P("ens", None, "lat", "lon"), P(), P(), P(), P(), P(), P(None, "lat", "lon")),
        out_specs=(P("ens", None, "lat", "lon"), P("lon", None, None)),
        check_vma=False,
    )
```

time: 125 us -> 122 us (0.976)
  local copies, waits for them, and re-layouts: 6.07 us -> 0.66 us
  blocking collectives: 21.8 us -> 24.7 us
  starting transfers between devices: 49.2 us -> 47.4 us
  waiting for transfers between devices: 22.4 us -> 24.2 us
    ppermute x2, starting transfers between devices: 14.2 us -> 11 us  [the longest x1 8.12 us: on_device(): got_close = lax.ppermute(close, 'lat', close_bands)]
    all_to_all x2, blocking collectives: 21.8 us -> 24.7 us  [exchange(): lax.all_to_all(pieces, ('ens', 'lat', 'lon'), split_axis=0, concat_axis=0...]
    unnamed x23 -> x0, local copies, waits for them, and re-layouts: 2.55 us -> none
    broadcast_in_dim x3 -> x0, local copies, waits for them, and re-layouts: 2.17 us -> none  [the longest x2 1.45 us: on_device(): bias = (weights, conv_bias[:, None], out_weight, out_bias[:, None])]
    ppermute x2, waiting for transfers between devices: 0.01 us -> 1.67 us  [the longest x1 1.67 us: on_device(): got_close = lax.ppermute(close, 'lat', close_bands)]
    all_to_all x2, waiting for transfers between devices: 21 us -> 22.5 us  [exchange(): lax.all_to_all(pieces, ('ens', 'lat', 'lon'), split_axis=0, concat_axis=0...]
    all_to_all x2, starting transfers between devices: 16.3 us -> 17.7 us  [exchange(): lax.all_to_all(pieces, ('ens', 'lat', 'lon'), split_axis=0, concat_axis=0...]
    ppermute x1, waiting for transfers between devices: 1.26 us -> 0.01 us  [on_device(): got_close = lax.ppermute(close, 'lon', close_loops)]
  transfers between devices with their start and end apart: 6 -> 6, of which waited for: 4 -> 3; matrix products, arithmetic and copies ran while one was open for 2% -> 0% of each run, Pallas kernels for 7% -> 9%
where the time goes in v5:
time: 122 us
  starting transfers between devices  47.4 us (39%)
  blocking collectives  24.7 us (20%)
  waiting for transfers between devices  24.2 us (20%)
  Pallas kernels  23.2 us (19%)
    all_to_all x2, blocking collectives, exchange(): lax.all_to_all(pieces, ('ens', 'lat', 'lon'), split_axis=0, concat_axis=0...  24.7 us
    pallas_call x8, Pallas kernels, pallas(): pl.pallas_call(kernel, out_shape=out_shape, in_specs=[pl.BlockSpec(memory...  23.2 us
    all_to_all x2, waiting for transfers between devices, exchange(): lax.all_to_all(pieces, ('ens', 'lat', 'lon'), split_axis=0, concat_axis=0...  22.5 us
    all_to_all x2, starting transfers between devices, exchange(): lax.all_to_all(pieces, ('ens', 'lat', 'lon'), split_axis=0, concat_axis=0...  17.7 us
    ppermute x1, starting transfers between devices, on_device(): got_other = lax.ppermute(other, 'lon', other_loops)  16.7 us
    ppermute x1, starting transfers between devices, on_device(): got_close = lax.ppermute(close, 'lat', close_bands)  8.12 us
    ppermute x1, starting transfers between devices, on_device(): got_other = lax.ppermute(other, ('lat', 'lon'), other_bands)  2.92 us
  transfers between devices with their start and end apart: 6, of which 3 were waited for; matrix products, arithmetic and copies ran while one was open for 0% of the time, Pallas kernels for 9%

profile of v5, /device:TPU:32, one launch (start us, length us, event | category | flops | bytes accessed | tf_op | source)
XLA Modules:
  0.0 121.6 jit_solution(17332809140080469096)
XLA Ops:
  0.6 4.2 %shard_map.95 = (bf16[3008,2304]{1,0:T(8,128)(2,1)}, f32[1424,2432]{1,0:T(8,128)}, bf16[208,32]{1,0:T(8,128)(2,1)}, bf16[208,32]{1,0:T(8,128)(2,1)}) custom-call(s32[1]{0:T(128)} %bitcast.4.odd_ref.odd_loop_ref, bf16[1,128,16,128]{3,2,1,0:T(8,128)(2,1)} %x_hbm.1, f32[69,16,128]{2,1,0:T(8,128)} %target_hbm.1), custom_call_target="tpu_custom_call" | custom-call | tf_op jit(solution)/shard_map/pallas_call | solution.py:442
  4.8 16.7 %collective-permute-start = (bf16[208,32]{1,0:T(8,128)(2,1)}, bf16[208,32]{1,0:T(8,128)(2,1)S(1)}, u32[]{:S(2)}, u32[]{:S(2)}) collective-permute-start(bf16[208,32]{1,0:T(8,128)(2,1)} %get-tuple-element.31), channel_id=1, source_target_pairs={{0,15},{1,2},{2,1},{3,4},{4,3},{5,6},{6,5},{7,8},{8,7},{9,10},{10,... | collective-permute-start | bytes 39944 | tf_op jit(solution)/shard_map/ppermute | solution.py:512
  21.5 1.9 %collective-permute-start.1 = (bf16[208,32]{1,0:T(8,128)(2,1)}, bf16[208,32]{1,0:T(8,128)(2,1)S(1)}, u32[]{:S(2)}, u32[]{:S(2)}) collective-permute-start(bf16[208,32]{1,0:T(8,128)(2,1)} %get-tuple-element.32), channel_id=1, source_target_pairs={{0,1},{1,0},{2,3},{3,2},{4,5},{5,4},{6,7},{7,6},{8,9},{9,8},{10,11... | collective-permute-start | bytes 39944 | tf_op jit(solution)/shard_map/ppermute | solution.py:513
  23.5 3.0 %shard_map.96 = (bf16[3008,2304]{1,0:T(8,128)(2,1)}, f32[1424,2432]{1,0:T(8,128)}) custom-call(bf16[3008,2304]{1,0:T(8,128)(2,1)} %get-tuple-element.33.far16_in, f32[1424,2432]{1,0:T(8,128)} %get-tuple-element.34.far32_in, bf16[1152,128]{1,0:T(8,128)(2,1)} %bitcast.27, ...), custom_call_target="tpu_custom_call", output_to_operand_aliasing={{0}: (0, {}), {1}: (1, {})} | custom-call | bytes 4194304 | tf_op jit(solution)/shard_map/pallas_call | solution.py:442
  26.5 1.5 %shard_map.97 = (bf16[128,2048]{1,0:T(8,128)(2,1)S(1)}, bf16[128,1152]{1,0:T(8,128)(2,1)S(1)}, bf16[80,128]{1,0:T(8,128)(2,1)S(1)}, bf16[736,384]{1,0:T(8,128)(2...) custom-call(bf16[3008,2304]{1,0:T(8,128)(2,1)} %get-tuple-element.35, ...), custom_call_target="tpu_custom_call" | custom-call | bytes 4194304 | tf_op jit(solution)/shard_map/pallas_call | solution.py:442
  28.0 0.0 collective-permute-done.other_ref
  28.0 0.0 collective-permute-done.1.close_ref
  28.0 0.3 shard_map.98
  28.3 2.9 %collective-permute-start.2 = (bf16[208,272]{1,0:T(8,128)(2,1)S(1)}, bf16[208,272]{1,0:T(8,128)(2,1)S(1)}, u32[]{:S(2)}, u32[]{:S(2)}) collective-permute-start(bf16[208,272]{1,0:T(8,128)(2,1)S(1)} %get-tuple-element.39), channel_id=1, source_target_pairs={{0,8},{1,9},{2,10},{3,11},{4,12},{5,13},{6,14},{7,15},{8,0},{9,1},... | collective-permute-start | bytes 339464 | tf_op jit(solution)/shard_map/ppermute | solution.py:560
  31.2 8.1 %collective-permute-start.3 = (bf16[208,272]{1,0:T(8,128)(2,1)S(1)}, bf16[208,272]{1,0:T(8,128)(2,1)S(1)}, u32[]{:S(2)}, u32[]{:S(2)}) collective-permute-start(bf16[208,272]{1,0:T(8,128)(2,1)S(1)} %get-tuple-element.40), channel_id=1, source_target_pairs={{0,16},{16,0},{32,48},{48,32},{64,80},{80,64},{96,112},{112,96},{1... | collective-permute-start | bytes 339464 | tf_op jit(solution)/shard_map/ppermute | solution.py:561
  39.3 2.7 %shard_map.99 = (bf16[69,1792]{1,0:T(8,128)(2,1)S(1)}, f32[128,1792]{1,0:T(8,128)S(1)}, bf16[384,2048]{1,0:T(8,128)(2,1)S(1)}) custom-call(bf16[208,32]{1,0:T(8,128)(2,1)S(1)} %get-tuple-element.41.left_ref, bf16[208,32]{1,0:T(8,128)(2,1)S(1)} %get-tuple-element.42.right_ref, bf16[128,2048]{1,0:T(8,128)(2,1)S(1)} %get-tuple-element.43.x_ref, ...), custom_call_target="tpu_custom_call" | custom-call | flops 560136192 | bytes 8388608 | tf_op jit(solution)/shard_map/pallas_call | solution.py:442
  42.1 1.7 %collective-permute-done.3.close_ref = bf16[208,272]{1,0:T(8,128)(2,1)S(1)} collective-permute-done((bf16[208,272]{1,0:T(8,128)(2,1)S(1)}, bf16[208,272]{1,0:T(8,128)(2,1)S(1)}, u32[]{:S(2)}, u32[]{:S(2)}) %collective-permute-start.3) | collective-permute-done | bytes 113184 | tf_op jit(solution)/shard_map/ppermute | solution.py:561
  43.7 3.6 %shard_map.100 = (bf16[4,69,2432]{2,1,0:T(8,128)(2,1)}, bf16[3008,2304]{1,0:T(8,128)(2,1)}, f32[1424,2432]{1,0:T(8,128)}) custom-call(s32[1]{0:T(128)} %bitcast.north_ref, s32[1]{0:T(128)} %bitcast.1.south_ref, s32[1]{0:T(128)} %bitcast.3.odd_band_ref.odd_ref, ...), custom_call_target="tpu_custom_call", output_to_operand_aliasing={{1}: (16, {}), {2}: (17, {})} | custom-call | flops 200048640 | tf_op jit(solution)/shard_map/pallas_call | solution.py:442
  47.4 4.5 %all-to-all-start = ((bf16[4,69,2432]{2,1,0:T(8,128)(2,1)}), bf16[4,69,2432]{2,1,0:T(8,128)(2,1)S(1)}, u32[]{:S(2)}, u32[]{:S(2)}) async-start(bf16[4,69,2432]{2,1,0:T(8,128)(2,1)} %get-tuple-element.53), calls=%async_computation | async-start | bytes 2801664 | tf_op jit(solution)/shard_map/all_to_all | solution.py:435
  51.9 12.8 %all-to-all-done.all_ref = bf16[4,69,2432]{2,1,0:T(8,128)(2,1)S(1)} async-done(((bf16[4,69,2432]{2,1,0:T(8,128)(2,1)}), bf16[4,69,2432]{2,1,0:T(8,128)(2,1)S(1)}, u32[]{:S(2)}, u32[]{:S(2)}) %all-to-all-start) | async-done | bytes 1342496 | tf_op jit(solution)/shard_map/all_to_all | solution.py:435
  64.7 4.0 %shard_map.101 = (bf16[2848,2432]{1,0:T(8,128)(2,1)}, bf16[1536,128]{1,0:T(8,128)(2,1)S(1)}) custom-call(s32[1]{0:T(128)} %bitcast.2.member_ref, bf16[4,69,2432]{2,1,0:T(8,128)(2,1)S(1)} %all-to-all-done.all_ref, bf16[3008,2304]{1,0:T(8,128)(2,1)} %get-tuple-element.54.far16, f32[1424,2432]{1,0:T(8,128)} %get-tuple-element.55.far32), custom_call_target="tpu_custom_call" | custom-call | flops 640155648 | tf_op jit(solution)/shard_map/pallas_call | solution.py:442
  68.7 16.7 %all_to_all.20 = bf16[32,48,128]{2,1,0:T(8,128)(2,1)S(1)} all-to-all(bf16[32,48,128]{2,1,0:T(8,128)(2,1)S(1)} %bitcast.26), channel_id=1, replica_groups={{0,1,2,3,4,5,6,7,128,129,130,131,132,133,134,135,256,257,258,259,260,26..., dimensions={0} | all-to-all | bytes 786432 | tf_op jit(solution)/shard_map/all_to_all | solution.py:435
  85.4 0.1 reduce_sum.24
  85.5 0.7 broadcast_in_dim.32
  86.2 13.2 %all-to-all-start.2 = ((bf16[16,24,128]{2,1,0:T(8,128)(2,1)}), bf16[16,24,128]{2,1,0:T(8,128)(2,1)S(1)}, u32[]{:S(2)}, u32[]{:S(2)}) async-start(bf16[16,24,128]{2,1,0:T(8,128)(2,1)} %bitcast.12), calls=%async_computation.2 | async-start | bytes 196608 | tf_op jit(solution)/shard_map/all_to_all | solution.py:435
  99.4 3.9 %shard_map.102 = bf16[1,128,16,128]{3,2,1,0:T(8,128)(2,1)} custom-call(s32[1]{0:T(128)} %bitcast.north_ref, s32[1]{0:T(128)} %bitcast.1.south_ref, bf16[2848,2432]{1,0:T(8,128)(2,1)} %get-tuple-element.56.g_hbm, bf16[1152,128]{1,0:T(8,128)(2,1)} %bitcast.28), custom_call_target="tpu_custom_call" | custom-call | flops 603979776 | tf_op jit(solution)/shard_map/pallas_call | solution.py:442
  103.3 9.7 %all-to-all-done.2 = bf16[16,24,128]{2,1,0:T(8,128)(2,1)S(1)} async-done(((bf16[16,24,128]{2,1,0:T(8,128)(2,1)}), bf16[16,24,128]{2,1,0:T(8,128)(2,1)S(1)}, u32[]{:S(2)}, u32[]{:S(2)}) %all-to-all-start.2) | async-done | bytes 98336 | tf_op jit(solution)/shard_map/all_to_all | solution.py:435
  113.1 7.9 %all_to_all.21 = bf16[4,24,128]{2,1,0:T(8,128)(2,1)S(1)} all-to-all(bf16[4,24,128]{2,1,0:T(8,128)(2,1)S(1)} %broadcast_in_dim.33), channel_id=1, replica_groups={{0,128,256,384},{1,129,257,385},{2,130,258,386},{3,131,259,387},{4,132,..., dimensions={0} | all-to-all | bytes 49152 | tf_op jit(solution)/shard_map/all_to_all | solution.py:435
  121.0 0.6 multiply_bitcast_fusion
  (5 shorter events, 0.0 us)
Async XLA Ops:
  4.8 23.2 %collective-permute-start = (bf16[208,32]{1,0:T(8,128)(2,1)}, bf16[208,32]{1,0:T(8,128)(2,1)S(1)}, u32[]{:S(2)}, u32[]{:S(2)}) collective-permute-start(bf16[208,32]{1,0:T(8,128)(2,1)} %get-tuple-element.31), channel_id=1, source_target_pairs={{0,15},{1,2},{2,1},{3,4},{4,3},{5,6},{6,5},{7,8},{8,7},{9,10},{10,... | collective-permute-start | bytes 39944 | tf_op jit(solution)/shard_map/ppermute | solution.py:512
  21.5 6.5 %collective-permute-start.1 = (bf16[208,32]{1,0:T(8,128)(2,1)}, bf16[208,32]{1,0:T(8,128)(2,1)S(1)}, u32[]{:S(2)}, u32[]{:S(2)}) collective-permute-start(bf16[208,32]{1,0:T(8,128)(2,1)} %get-tuple-element.32), channel_id=1, source_target_pairs={{0,1},{1,0},{2,3},{3,2},{4,5},{5,4},{6,7},{7,6},{8,9},{9,8},{10,11... | collective-permute-start | bytes 39944 | tf_op jit(solution)/shard_map/ppermute | solution.py:513
  28.3 13.8 %collective-permute-start.2 = (bf16[208,272]{1,0:T(8,128)(2,1)S(1)}, bf16[208,272]{1,0:T(8,128)(2,1)S(1)}, u32[]{:S(2)}, u32[]{:S(2)}) collective-permute-start(bf16[208,272]{1,0:T(8,128)(2,1)S(1)} %get-tuple-element.39), channel_id=1, source_target_pairs={{0,8},{1,9},{2,10},{3,11},{4,12},{5,13},{6,14},{7,15},{8,0},{9,1},... | collective-permute-start | bytes 339464 | tf_op jit(solution)/shard_map/ppermute | solution.py:560
  31.2 12.5 %collective-permute-start.3 = (bf16[208,272]{1,0:T(8,128)(2,1)S(1)}, bf16[208,272]{1,0:T(8,128)(2,1)S(1)}, u32[]{:S(2)}, u32[]{:S(2)}) collective-permute-start(bf16[208,272]{1,0:T(8,128)(2,1)S(1)} %get-tuple-element.40), channel_id=1, source_target_pairs={{0,16},{16,0},{32,48},{48,32},{64,80},{80,64},{96,112},{112,96},{1... | collective-permute-start | bytes 339464 | tf_op jit(solution)/shard_map/ppermute | solution.py:561
  47.4 17.3 %all-to-all-start = ((bf16[4,69,2432]{2,1,0:T(8,128)(2,1)}), bf16[4,69,2432]{2,1,0:T(8,128)(2,1)S(1)}, u32[]{:S(2)}, u32[]{:S(2)}) async-start(bf16[4,69,2432]{2,1,0:T(8,128)(2,1)} %get-tuple-element.53), calls=%async_computation | async-start | bytes 2801664 | tf_op jit(solution)/shard_map/all_to_all | solution.py:435
  86.2 26.9 %all-to-all-start.2 = ((bf16[16,24,128]{2,1,0:T(8,128)(2,1)}), bf16[16,24,128]{2,1,0:T(8,128)(2,1)S(1)}, u32[]{:S(2)}, u32[]{:S(2)}) async-start(bf16[16,24,128]{2,1,0:T(8,128)(2,1)} %bitcast.12), calls=%async_computation.2 | async-start | bytes 196608 | tf_op jit(solution)/shard_map/all_to_all | solution.py:435

commit v6 on v5

--- a/solution.py
+++ b/solution.py
@@ -15,7 +15,10 @@
 VMEM_BYTES = 60 * 2**20
 ROOMY = 50 * 10**6
 FAR = 138 * 10**5
-HALO_LANES = 2 * LANES + 16
+HALO_LANES = 2 * LANES
+CORNERS = 8
+ACROSS = (((1,), (1,)), ((), ()))
+DOWN = (((0,), (0,)), ((), ()))
 RIM = 32
 f32, bf16 = jnp.float32, jnp.bfloat16
 
@@ -45,21 +48,21 @@
 
 class Plan:
     def __init__(self, channels, variables, rows):
-        halo = channels + -(-variables // 16) * 16
-        tall = -(-variables // 16) * 16
+        tall = -(-(variables + CORNERS) // 16) * 16
+        halo = channels + tall
         self.x3 = (slice(0, 3 * channels), tile(0, rows + 2))
         top = 3 * channels
         self.flat = (slice(top, top + channels), tile(0, rows))
         top += channels
-        sources = 4 * rows + LANES + 2 * HALO_LANES
+        sources = 4 * rows + 2 * LANES + 2 * HALO_LANES
         self.weights = (slice(top, top + channels), tile(0, 9))
         self.choice = (slice(top, top + sources), tile(9, 3))
         self.first = (slice(top, top + halo), tile(12, 2))
         self.last = (slice(top, top + halo), tile(14, 2))
         self.mix = (slice(top, top + tall), tile(16))
         self.mix_turned = (slice(top, top + channels), tile(17))
-        self.sides = (slice(top + halo, top + 2 * halo), tile(12))
-        self.rows16 = top + max(sources, 2 * halo)
+        self.sides = (slice(top + halo, top + halo + LANES), tile(12, 2))
+        self.rows16 = top + max(sources, halo + LANES)
         self.slope = (slice(0, channels), tile(0, rows + 3))
         self.truth = (slice(channels, channels + -(-variables // 8) * 8), tile(0, 3))
         top = channels + tall
@@ -81,8 +84,8 @@
     halves = [slice(k * part, (k + 1) * part) for k in range(2)]
     loads = [copies.start(x_hbm.at[0, here], x_ref.at[here]) for here in halves]
     load_target = copies.start(target_hbm, target_ref)
-    cell = lax.broadcasted_iota(jnp.int32, (rows * cols, 4 * rows), 0)
-    slot = lax.broadcasted_iota(jnp.int32, (1, 4 * rows), 1)
+    cell = lax.broadcasted_iota(jnp.int32, (4 * rows, rows * cols), 1)
+    slot = lax.broadcasted_iota(jnp.int32, (4 * rows, 1), 0)
     column = jnp.where(slot < rows, cols - 1, jnp.where(slot < 2 * rows, cols - 2, jnp.where(slot < 3 * rows, 0, 1)))
     pick = jnp.where(cell == (slot % rows) * cols + column, 1.0, 0.0).astype(bf16)
     aim_ref[variables - variables % 8 :] = jnp.zeros((aim_ref.shape[0] - variables + variables % 8, rows * cols), f32)
@@ -92,7 +95,7 @@
         for row in range(rows):
             flat_ref[here, tile(row)] = wide_ref[here, row, :].astype(bf16)
     saves = [copies.start(flat_ref, far16.at[*plan.flat])]
-    edges = dot(flat_ref[...], pick)
+    edges = dot(pick, flat_ref[...], ACROSS)
     load_target.wait()
     for row in range(rows):
         aim_ref[:variables, tile(row)] = target_ref[:, row, :]
@@ -105,20 +108,21 @@
         ref[channels:, :cols] = high[:, tile(near)]
         ref[channels:, cols:] = low[:, tile(near)]
     saves += [copies.start(first_ref, far16.at[*plan.first]), copies.start(last_ref, far16.at[*plan.last])]
-    high_edges = dot(high, pick)
-    low_edges = dot(low, pick)
-
-    def side(begin):
-        aim = jnp.concatenate([high_edges[:, begin : begin + rows], low_edges[:, begin : begin + rows]], axis=1)
-        return jnp.concatenate([edges[:, begin : begin + 2 * rows], aim], axis=0)
-
-    east, west = side(0), side(2 * rows)
-    lane = lax.broadcasted_iota(jnp.int32, east.shape, 1)
-    odd = lane < odd_ref[0] * LANES
-    other_ref[...] = jnp.where(odd, east, west).astype(bf16)
-    close_ref[...] = jnp.where(odd, west, east).astype(bf16)
-    sides_ref[...] = jnp.zeros(sides_ref.shape, bf16)
-    sides_ref[:, : 4 * rows] = jnp.concatenate([east, west], axis=1).astype(bf16)
+    high_edges = dot(pick, high, ACROSS)
+    low_edges = dot(pick, low, ACROSS)
+    part = 2 * rows
+    aims = [jnp.concatenate([high_edges[k : k + rows], low_edges[k : k + rows]], axis=0) for k in (0, part)]
+    for ref in (other_ref, close_ref, sides_ref):
+        ref[...] = jnp.zeros(ref.shape, bf16)
+    for place, (east, west) in (
+        (slice(0, channels), (edges[:part], edges[part:])),
+        (slice(channels, channels + aim_ref.shape[0]), aims),
+    ):
+        odd = lax.broadcasted_iota(jnp.int32, east.shape, 1) < odd_ref[0] * 2 * LANES
+        other_ref[:, place] = jnp.where(odd, east, west).astype(bf16)
+        close_ref[:, place] = jnp.where(odd, west, east).astype(bf16)
+        sides_ref[:part, place] = east.astype(bf16)
+        sides_ref[part : 2 * part, place] = west.astype(bf16)
     for ref, goal in ((other_ref, other_hbm), (close_ref, close_hbm), (sides_ref, far16.at[*plan.sides])):
         saves.append(copies.start(ref, goal))
     for save in saves:
@@ -161,34 +165,34 @@
 
 def corner_kernel(rows, odd_loop_ref, odd_band_ref, other_ref, close_ref, first_ref, last_ref,
                   left_ref, right_ref, send_other_ref, send_close_ref):
+    halo = first_ref.shape[0]
     other, close = other_ref[...].astype(f32), close_ref[...].astype(f32)
-    odd = lax.broadcasted_iota(jnp.int32, other.shape, 1) < odd_loop_ref[0] * LANES
-    left = jnp.where(odd, close, other).astype(bf16)
-    right = jnp.where(odd, other, close).astype(bf16)
-    left_ref[...] = left
-    right_ref[...] = right
-    source = lax.broadcasted_iota(jnp.int32, (2 * rows, 32), 0)
-    goal = lax.broadcasted_iota(jnp.int32, (2 * rows, 32), 1)
+    odd = lax.broadcasted_iota(jnp.int32, other.shape, 1) < odd_loop_ref[0] * 2 * LANES
+    left, right = jnp.where(odd, close, other), jnp.where(odd, other, close)
+    fill = jnp.zeros((LANES - 4 * rows, other.shape[1]), f32)
+    turned = jnp.concatenate([left, right, fill], axis=0).T
+    left_ref[...] = turned[:halo, : 2 * rows].astype(bf16)
+    right_ref[...] = turned[:halo, 2 * rows : 4 * rows].astype(bf16)
+    source = lax.broadcasted_iota(jnp.int32, (2 * rows, 4 * CORNERS), 0)
+    goal = lax.broadcasted_iota(jnp.int32, (2 * rows, 4 * CORNERS), 1)
     nth, spot = goal % 4, goal % 16
     wanted = jnp.where(goal < 16, nth % 2, rows - 1 - nth % 2) + (nth // 2) * rows
     hit = source == wanted
     from_left = jnp.where(hit & (spot < 4), 1.0, 0.0).astype(bf16)
     from_right = jnp.where(hit & (spot >= 4) & (spot < 8), 1.0, 0.0).astype(bf16)
-    corners = dot(left, from_left) + dot(right, from_right)
-    first, last = first_ref[...].astype(f32), last_ref[...].astype(f32)
-    odd_band = odd_band_ref[0] * HALO_LANES
-    odd = lax.broadcasted_iota(jnp.int32, first.shape, 1) < odd_band
-    send_other_ref[:, : 2 * LANES] = jnp.where(odd, last, first).astype(bf16)
-    send_close_ref[:, : 2 * LANES] = jnp.where(odd, first, last).astype(bf16)
-    odd = lax.broadcasted_iota(jnp.int32, (first.shape[0], 16), 1) < odd_band
-    send_other_ref[:, 2 * LANES :] = jnp.where(odd, corners[:, 16:], corners[:, :16]).astype(bf16)
-    send_close_ref[:, 2 * LANES :] = jnp.where(odd, corners[:, :16], corners[:, 16:]).astype(bf16)
+    corners = dot(from_left, left.astype(bf16), DOWN) + dot(from_right, right.astype(bf16), DOWN)
+    of_first, of_last = corners[:CORNERS], corners[16 : 16 + CORNERS]
+    first = jnp.concatenate([first_ref[...].astype(f32)[: halo - CORNERS], of_first], axis=0)
+    last = jnp.concatenate([last_ref[...].astype(f32)[: halo - CORNERS], of_last], axis=0)
+    odd = lax.broadcasted_iota(jnp.int32, first.shape, 1) < odd_band_ref[0] * HALO_LANES
+    send_other_ref[...] = jnp.where(odd, last, first).astype(bf16)
+    send_close_ref[...] = jnp.where(odd, first, last).astype(bf16)
 
 
 def rim_choice(rows):
-    sizes = (2 * rows,) * 2 + (LANES,) + (HALO_LANES,) * 2
+    sizes = (2 * rows,) * 2 + (LANES,) * 2 + (HALO_LANES,) * 2
     sources = [np.zeros((size, 3 * LANES), np.float32) for size in sizes]
-    left, right, sides, north, south = sources
+    left, right, sides, corners, north, south = sources
     for row in range(rows):
         lane = row + 2
         left[row, LANES + lane] = 1
@@ -197,12 +201,12 @@
         right[rows + row, 2 * LANES + RIM + lane] = 1
         sides[row, RIM + lane] = 1
         sides[2 * rows + row, 2 * LANES + lane] = 1
-    for source, lanes in ((north, (1, 0)), (south, (rows + 2, rows + 3))):
+    for base, source, lanes in ((0, north, (1, 0)), (CORNERS, south, (rows + 2, rows + 3))):
         for second, lane in enumerate(lanes):
-            source[2 * LANES + second, LANES + lane] = 1
-            source[2 * LANES + 2 + second, lane] = 1
-            source[2 * LANES + 4 + second, LANES + RIM + lane] = 1
-            source[2 * LANES + 6 + second, 2 * LANES + RIM + lane] = 1
+            corners[base + second, LANES + lane] = 1
+            corners[base + 2 + second, lane] = 1
+            corners[base + 4 + second, LANES + RIM + lane] = 1
+            corners[base + 6 + second, 2 * LANES + RIM + lane] = 1
             source[second * LANES + LANES - 1, RIM + lane] = 1
             source[second * LANES, 2 * LANES + lane] = 1
     return jnp.asarray(np.concatenate(sources), bf16)
@@ -260,12 +264,14 @@
     odd = lax.broadcasted_iota(jnp.int32, close.shape, 1) < odd_ref[0] * HALO_LANES
     north, south = jnp.where(odd, close, other), jnp.where(odd, other, close)
     poles = north_ref[0], south_ref[0]
-    for halo, spots in ((north, (1, 0)), (south, (6, 7))):
-        halo = halo[:channels]
+    height = north.shape[0]
+    fill = jnp.zeros((LANES - 2 * CORNERS, HALO_LANES), f32)
+    corners = jnp.concatenate([north[height - CORNERS :], south[height - CORNERS :], fill], axis=0).T[:height]
+    for base, halo, spots in ((0, north, (1, 0)), (CORNERS, south, (6, 7))):
         for second, spot in enumerate(spots):
-            before = halo[:, 2 * LANES + second : 2 * LANES + second + 1]
-            after = halo[:, 2 * LANES + 4 + second : 2 * LANES + 5 + second]
-            widen(near_ref, tile(spot), halo[:, tile(second)], before, after)
+            before = corners[:channels, base + second : base + second + 1]
+            after = corners[:channels, base + 4 + second : base + 5 + second]
+            widen(near_ref, tile(spot), halo[:channels, tile(second)], before, after)
     saves += [
         copies.start(near_ref.at[:, tile(1)], x3_hbm.at[:, tile(0)]),
         copies.start(near_ref.at[:, tile(6)], x3_hbm.at[:, tile(rows + 1)]),
@@ -290,10 +296,12 @@
     for spot, place, pole in ((1, 0, poles[0]), (6, 3, poles[1])):
         above, below = near_ref[:, tile(spot - 1)].astype(f32), near_ref[:, tile(spot + 1)].astype(f32)
         finish(beyond(above, near_ref[:, tile(spot)], below, lane3 < pole * LANES), tile(place))
-    rim, begin = 0.0, 0
-    sources = (left_ref[...], right_ref[...], sides_ref[...], north.astype(bf16), south.astype(bf16))
-    for source in sources:
-        rim = rim + dot(source, choice_ref[begin : begin + source.shape[1]])
+    begin = 4 * rows
+    rim = dot(left_ref[...], choice_ref[: 2 * rows]) + dot(right_ref[...], choice_ref[2 * rows : begin])
+    rim = rim + dot(sides_ref[...], choice_ref[begin : begin + LANES], DOWN)[:height]
+    begin += LANES
+    for source in (corners, north, south):
+        rim = rim + dot(source.astype(bf16), choice_ref[begin : begin + source.shape[1]])
         begin += source.shape[1]
     middle = jnp.concatenate([rim[:channels, tile(k)] for k in range(3)], axis=0)
     first = (lane3 == 1) | (lane3 == RIM + 1)
@@ -315,7 +323,7 @@
 
 
 def weight_kernel(plan, rows, shares, members, member_ref, all_ref, far16, far32, g_hbm, term_hbm,
-                  truth_ref, vw_ref, owt_ref, g_ref, term_ref, target_ref, out_grad_ref, slope_ref, x3_ref, sems):
+                  truth_ref, vw_ref, owt_ref, g_ref, term_ref, target_ref, out_grad_ref, pair_ref, slope_ref, x3_ref, sems):
     channels = g_ref.shape[0]
     variables = out_grad_ref.shape[0]
     tiles = rows + 3
@@ -330,10 +338,6 @@
         copies.start(far32.at[*plan.slope], slope_ref),
         copies.start(far16.at[*plan.x3], x3_ref),
     ]
-    for load in first:
-        load.wait()
-    scale = vw_ref[:variables, :1]
-
     def truth(q):
         if q == 0:
             return truth_ref[:variables, tile(0)]
@@ -341,16 +345,22 @@
             return truth_ref[:variables, tile(q - rows)]
         return target_ref[:variables, tile(q - 1)]
 
-    for q in range(0, tiles, 2):
-        count = min(2, tiles - q)
+    blocks = [(q, min(2, tiles - q)) for q in range(0, tiles, 2)]
+    for q, count in blocks:
         place = tile(q, count)
         own = all_ref[member_ref[0], :, place].astype(f32)
         total = jnp.zeros_like(own)
         for member in range(members):
             total = total + signed(own - all_ref[member, :, place].astype(f32))
+        pair_ref[:, place] = total / (members * (members - 1))
+    for load in first:
+        load.wait()
+    scale = vw_ref[:variables, :1]
+    for q, count in blocks:
+        place = tile(q, count)
+        own = all_ref[member_ref[0], :, place].astype(f32)
         fit = signed(own - jnp.concatenate([truth(q + n) for n in range(count)], axis=1))
-        grad = scale * (fit / members - total / (members * (members - 1)))
-        out_grad_ref[:, place] = grad.astype(bf16)
+        out_grad_ref[:, place] = (scale * (fit / members - pair_ref[:, place])).astype(bf16)
     later[0].wait()
     later[1].wait()
     for q in range(0, tiles, 2):
@@ -465,7 +475,7 @@
     member, band, loop = (lax.axis_index(axis) for axis in ("ens", "lat", "lon"))
     cells = rows * cols
     inner, outer = cells - 2 * cols, 5 * cols
-    halo = -(-(channels + variables) // 16) * 16
+    halo = channels + -(-(variables + CORNERS) // 16) * 16
     shape = jax.ShapeDtypeStruct
     odd_loop, odd_band = loop % 2 == 1, band % 2 == 1
     flags = [flag[None].astype(jnp.int32) for flag in (band == 0, band == bands - 1, odd_band)]
@@ -497,23 +507,24 @@
         count = -(-FAR // (width * jnp.dtype(dtype).itemsize))
         return shape((-(-max(count, least) // 16) * 16, width), dtype)
 
-    side, edge = shape((halo, 2 * rows), bf16), shape((halo, 2 * cols), bf16)
+    side, turned_side = shape((halo, 2 * rows), bf16), shape((2 * rows, 2 * LANES), bf16)
+    edge, sides = shape((halo, 2 * cols), bf16), shape((LANES, 2 * LANES), bf16)
     aim = shape((halo - channels, cells), f32)
     wholes = (far(plan.rows16, cells + 2 * cols, bf16), far(plan.rows32, inner + outer, f32))
     far16, far32, close, other = pallas(
         functools.partial(prepare_kernel, plan),
-        (*wholes, side, side),
+        (*wholes, turned_side, turned_side),
         (odd_loop[None].astype(jnp.int32),),
         (features, target),
         [((channels, rows, cols), bf16), (target.shape, f32), ((channels, rows, cols), f32)]
-        + like(aim) + [((channels, cells), bf16)] + like(side, side) + [((halo, LANES), bf16)] + like(edge, edge),
+        + like(aim) + [((channels, cells), bf16)] + like(turned_side, turned_side, sides, edge, edge),
         10,
     )
     got_other = lax.ppermute(other, "lon", other_loops)
     got_close = lax.ppermute(close, "lon", close_loops)
 
     tall = halo - channels
-    choice_rows = 4 * rows + LANES + 2 * HALO_LANES
+    choice_rows = 4 * rows + 2 * LANES + 2 * HALO_LANES
     weights = conv_weight.transpose(1, 0, 2).reshape(9 * channels, channels)
     far16, far32 = pallas(
         functools.partial(pack_kernel, plan),
@@ -599,7 +610,7 @@
         (member[None].astype(jnp.int32),),
         (everyone, far16, far32),
         [beyond, ((LANES, LANES), f32), ((channels, LANES), bf16), grads_spec] + like(results[1], aim)
-        + [((variables, inner + outer), bf16), ((channels, inner + outer), f32)]
+        + [((variables, inner + outer), bf16), ((variables, inner + outer), f32), ((channels, inner + outer), f32)]
         + [((3 * channels, cells + 2 * cols), bf16)],
         8,
         vmem=ROOMY,

time: 122 us -> 120 us (0.984)
  blocking collectives: 24.7 us -> 23.2 us
    all_to_all x2, blocking collectives: 24.7 us -> 23.2 us  [exchange(): lax.all_to_all(pieces, ('ens', 'lat', 'lon'), split_axis=0, concat_axis=0...]
where the time goes in v6:
time: 120 us; the launch traced here: 119 us
  starting transfers between devices  46.7 us (39%)
  waiting for transfers between devices  24 us (20%)
  blocking collectives  23.2 us (19%)
  Pallas kernels  23.1 us (19%)
    all_to_all x2, waiting for transfers between devices, exchange(): lax.all_to_all(pieces, ('ens', 'lat', 'lon'), split_axis=0, concat_axis=0...  23.5 us
    all_to_all x2, blocking collectives, exchange(): lax.all_to_all(pieces, ('ens', 'lat', 'lon'), split_axis=0, concat_axis=0...  23.2 us
    pallas_call x8, Pallas kernels, pallas(): pl.pallas_call(kernel, out_shape=out_shape, in_specs=[pl.BlockSpec(memory...  23.1 us
    all_to_all x2, starting transfers between devices, exchange(): lax.all_to_all(pieces, ('ens', 'lat', 'lon'), split_axis=0, concat_axis=0...  17.5 us
    ppermute x1, starting transfers between devices, on_device(): got_other = lax.ppermute(other, 'lon', other_loops)  16.7 us
    ppermute x1, starting transfers between devices, on_device(): got_close = lax.ppermute(close, 'lat', close_bands)  7.65 us
    ppermute x1, starting transfers between devices, on_device(): got_other = lax.ppermute(other, ('lat', 'lon'), other_bands)  2.93 us
  transfers between devices with their start and end apart: 6, of which 3 were waited for; matrix products, arithmetic and copies ran while one was open for 0% of the time, Pallas kernels for 9%

profile of v6, /device:TPU:32, one launch (start us, length us, event | category | flops | bytes accessed | tf_op | source)
XLA Modules:
  0.0 119.2 jit_solution(7322861279265230241)
XLA Ops:
  0.6 3.9 %shard_map.95 = (bf16[3008,2304]{1,0:T(8,128)(2,1)}, f32[1424,2432]{1,0:T(8,128)}, bf16[32,256]{1,0:T(8,128)(2,1)}, bf16[32,256]{1,0:T(8,128)(2,1)}) custom-call(s32[1]{0:T(128)} %bitcast.4.odd_ref.odd_loop_ref, bf16[1,128,16,128]{3,2,1,0:T(8,128)(2,1)} %x_hbm.1, f32[69,16,128]{2,1,0:T(8,128)} %target_hbm.1), custom_call_target="tpu_custom_call" | custom-call | tf_op jit(solution)/shard_map/pallas_call | solution.py:452
  4.5 16.7 %collective-permute-start = (bf16[32,256]{1,0:T(8,128)(2,1)}, bf16[32,256]{1,0:T(8,128)(2,1)S(1)}, u32[]{:S(2)}, u32[]{:S(2)}) collective-permute-start(bf16[32,256]{1,0:T(8,128)(2,1)} %get-tuple-element.31), channel_id=1, source_target_pairs={{0,15},{1,2},{2,1},{3,4},{4,3},{5,6},{6,5},{7,8},{8,7},{9,10},{10,... | collective-permute-start | bytes 49160 | tf_op jit(solution)/shard_map/ppermute | solution.py:523
  21.3 1.9 %collective-permute-start.1 = (bf16[32,256]{1,0:T(8,128)(2,1)}, bf16[32,256]{1,0:T(8,128)(2,1)S(1)}, u32[]{:S(2)}, u32[]{:S(2)}) collective-permute-start(bf16[32,256]{1,0:T(8,128)(2,1)} %get-tuple-element.32), channel_id=1, source_target_pairs={{0,1},{1,0},{2,3},{3,2},{4,5},{5,4},{6,7},{7,6},{8,9},{9,8},{10,11... | collective-permute-start | bytes 49160 | tf_op jit(solution)/shard_map/ppermute | solution.py:524
  23.2 3.1 %shard_map.96 = (bf16[3008,2304]{1,0:T(8,128)(2,1)}, f32[1424,2432]{1,0:T(8,128)}) custom-call(bf16[3008,2304]{1,0:T(8,128)(2,1)} %get-tuple-element.33.far16_in, f32[1424,2432]{1,0:T(8,128)} %get-tuple-element.34.far32_in, bf16[1152,128]{1,0:T(8,128)(2,1)} %bitcast.27, ...), custom_call_target="tpu_custom_call", output_to_operand_aliasing={{0}: (0, {}), {1}: (1, {})} | custom-call | bytes 4194304 | tf_op jit(solution)/shard_map/pallas_call | solution.py:452
  26.3 1.5 %shard_map.97 = (bf16[128,2048]{1,0:T(8,128)(2,1)S(1)}, bf16[128,1152]{1,0:T(8,128)(2,1)S(1)}, bf16[80,128]{1,0:T(8,128)(2,1)S(1)}, bf16[832,384]{1,0:T(8,128)(2...) custom-call(bf16[3008,2304]{1,0:T(8,128)(2,1)} %get-tuple-element.35, ...), custom_call_target="tpu_custom_call" | custom-call | bytes 4194304 | tf_op jit(solution)/shard_map/pallas_call | solution.py:452
  27.8 0.0 collective-permute-done.other_ref
  27.8 0.2 shard_map.98
  28.0 2.9 %collective-permute-start.2 = (bf16[208,256]{1,0:T(8,128)(2,1)S(1)}, bf16[208,256]{1,0:T(8,128)(2,1)S(1)}, u32[]{:S(2)}, u32[]{:S(2)}) collective-permute-start(bf16[208,256]{1,0:T(8,128)(2,1)S(1)} %get-tuple-element.39), channel_id=1, source_target_pairs={{0,8},{1,9},{2,10},{3,11},{4,12},{5,13},{6,14},{7,15},{8,0},{9,1},... | collective-permute-start | bytes 319496 | tf_op jit(solution)/shard_map/ppermute | solution.py:571
  30.9 7.6 %collective-permute-start.3 = (bf16[208,256]{1,0:T(8,128)(2,1)S(1)}, bf16[208,256]{1,0:T(8,128)(2,1)S(1)}, u32[]{:S(2)}, u32[]{:S(2)}) collective-permute-start(bf16[208,256]{1,0:T(8,128)(2,1)S(1)} %get-tuple-element.40), channel_id=1, source_target_pairs={{0,16},{16,0},{32,48},{48,32},{64,80},{80,64},{96,112},{112,96},{1... | collective-permute-start | bytes 319496 | tf_op jit(solution)/shard_map/ppermute | solution.py:572
  38.6 2.7 %shard_map.99 = (bf16[69,1792]{1,0:T(8,128)(2,1)S(1)}, f32[128,1792]{1,0:T(8,128)S(1)}, bf16[384,2048]{1,0:T(8,128)(2,1)S(1)}) custom-call(bf16[208,32]{1,0:T(8,128)(2,1)S(1)} %get-tuple-element.41.left_ref, bf16[208,32]{1,0:T(8,128)(2,1)S(1)} %get-tuple-element.42.right_ref, bf16[128,2048]{1,0:T(8,128)(2,1)S(1)} %get-tuple-element.43.x_ref, ...), custom_call_target="tpu_custom_call" | custom-call | flops 560136192 | bytes 8388608 | tf_op jit(solution)/shard_map/pallas_call | solution.py:452
  41.3 0.0 collective-permute-done.2.other_ref
  41.3 0.5 collective-permute-done.3.close_ref
  41.9 4.0 %shard_map.100 = (bf16[4,69,2432]{2,1,0:T(8,128)(2,1)}, bf16[3008,2304]{1,0:T(8,128)(2,1)}, f32[1424,2432]{1,0:T(8,128)}) custom-call(s32[1]{0:T(128)} %bitcast.north_ref, s32[1]{0:T(128)} %bitcast.1.south_ref, s32[1]{0:T(128)} %bitcast.3.odd_band_ref.odd_ref, ...), custom_call_target="tpu_custom_call", output_to_operand_aliasing={{1}: (16, {}), {2}: (17, {})} | custom-call | flops 200048640 | tf_op jit(solution)/shard_map/pallas_call | solution.py:452
  45.8 4.3 %all-to-all-start = ((bf16[4,69,2432]{2,1,0:T(8,128)(2,1)}), bf16[4,69,2432]{2,1,0:T(8,128)(2,1)S(1)}, u32[]{:S(2)}, u32[]{:S(2)}) async-start(bf16[4,69,2432]{2,1,0:T(8,128)(2,1)} %get-tuple-element.53), calls=%async_computation | async-start | bytes 2801664 | tf_op jit(solution)/shard_map/all_to_all | solution.py:445
  50.1 13.8 %all-to-all-done.all_ref = bf16[4,69,2432]{2,1,0:T(8,128)(2,1)S(1)} async-done(((bf16[4,69,2432]{2,1,0:T(8,128)(2,1)}), bf16[4,69,2432]{2,1,0:T(8,128)(2,1)S(1)}, u32[]{:S(2)}, u32[]{:S(2)}) %all-to-all-start) | async-done | bytes 1342496 | tf_op jit(solution)/shard_map/all_to_all | solution.py:445
  63.9 3.8 %shard_map.101 = (bf16[2848,2432]{1,0:T(8,128)(2,1)}, bf16[1536,128]{1,0:T(8,128)(2,1)S(1)}) custom-call(s32[1]{0:T(128)} %bitcast.2.member_ref, bf16[4,69,2432]{2,1,0:T(8,128)(2,1)S(1)} %all-to-all-done.all_ref, bf16[3008,2304]{1,0:T(8,128)(2,1)} %get-tuple-element.54.far16, f32[1424,2432]{1,0:T(8,128)} %get-tuple-element.55.far32), custom_call_target="tpu_custom_call" | custom-call | flops 640155648 | tf_op jit(solution)/shard_map/pallas_call | solution.py:452
  67.7 15.3 %all_to_all.20 = bf16[32,48,128]{2,1,0:T(8,128)(2,1)S(1)} all-to-all(bf16[32,48,128]{2,1,0:T(8,128)(2,1)S(1)} %bitcast.26), channel_id=1, replica_groups={{0,1,2,3,4,5,6,7,128,129,130,131,132,133,134,135,256,257,258,259,260,26..., dimensions={0} | all-to-all | bytes 786432 | tf_op jit(solution)/shard_map/all_to_all | solution.py:445
  83.0 0.1 reduce_sum.24
  83.1 0.7 broadcast_in_dim.32
  83.7 13.2 %all-to-all-start.2 = ((bf16[16,24,128]{2,1,0:T(8,128)(2,1)}), bf16[16,24,128]{2,1,0:T(8,128)(2,1)S(1)}, u32[]{:S(2)}, u32[]{:S(2)}) async-start(bf16[16,24,128]{2,1,0:T(8,128)(2,1)} %bitcast.12), calls=%async_computation.2 | async-start | bytes 196608 | tf_op jit(solution)/shard_map/all_to_all | solution.py:445
  96.9 4.0 %shard_map.102 = bf16[1,128,16,128]{3,2,1,0:T(8,128)(2,1)} custom-call(s32[1]{0:T(128)} %bitcast.north_ref, s32[1]{0:T(128)} %bitcast.1.south_ref, bf16[2848,2432]{1,0:T(8,128)(2,1)} %get-tuple-element.56.g_hbm, bf16[1152,128]{1,0:T(8,128)(2,1)} %bitcast.28), custom_call_target="tpu_custom_call" | custom-call | flops 603979776 | tf_op jit(solution)/shard_map/pallas_call | solution.py:452
  100.9 9.7 %all-to-all-done.2 = bf16[16,24,128]{2,1,0:T(8,128)(2,1)S(1)} async-done(((bf16[16,24,128]{2,1,0:T(8,128)(2,1)}), bf16[16,24,128]{2,1,0:T(8,128)(2,1)S(1)}, u32[]{:S(2)}, u32[]{:S(2)}) %all-to-all-start.2) | async-done | bytes 98336 | tf_op jit(solution)/shard_map/all_to_all | solution.py:445
  110.6 7.9 %all_to_all.21 = bf16[4,24,128]{2,1,0:T(8,128)(2,1)S(1)} all-to-all(bf16[4,24,128]{2,1,0:T(8,128)(2,1)S(1)} %broadcast_in_dim.33), channel_id=1, replica_groups={{0,128,256,384},{1,129,257,385},{2,130,258,386},{3,131,259,387},{4,132,..., dimensions={0} | all-to-all | bytes 49152 | tf_op jit(solution)/shard_map/all_to_all | solution.py:445
  118.5 0.6 multiply_bitcast_fusion
  (5 shorter events, 0.0 us)
Async XLA Ops:
  4.5 23.2 %collective-permute-start = (bf16[32,256]{1,0:T(8,128)(2,1)}, bf16[32,256]{1,0:T(8,128)(2,1)S(1)}, u32[]{:S(2)}, u32[]{:S(2)}) collective-permute-start(bf16[32,256]{1,0:T(8,128)(2,1)} %get-tuple-element.31), channel_id=1, source_target_pairs={{0,15},{1,2},{2,1},{3,4},{4,3},{5,6},{6,5},{7,8},{8,7},{9,10},{10,... | collective-permute-start | bytes 49160 | tf_op jit(solution)/shard_map/ppermute | solution.py:523
  21.3 6.5 %collective-permute-start.1 = (bf16[32,256]{1,0:T(8,128)(2,1)}, bf16[32,256]{1,0:T(8,128)(2,1)S(1)}, u32[]{:S(2)}, u32[]{:S(2)}) collective-permute-start(bf16[32,256]{1,0:T(8,128)(2,1)} %get-tuple-element.32), channel_id=1, source_target_pairs={{0,1},{1,0},{2,3},{3,2},{4,5},{5,4},{6,7},{7,6},{8,9},{9,8},{10,11... | collective-permute-start | bytes 49160 | tf_op jit(solution)/shard_map/ppermute | solution.py:524
  28.0 13.3 %collective-permute-start.2 = (bf16[208,256]{1,0:T(8,128)(2,1)S(1)}, bf16[208,256]{1,0:T(8,128)(2,1)S(1)}, u32[]{:S(2)}, u32[]{:S(2)}) collective-permute-start(bf16[208,256]{1,0:T(8,128)(2,1)S(1)} %get-tuple-element.39), channel_id=1, source_target_pairs={{0,8},{1,9},{2,10},{3,11},{4,12},{5,13},{6,14},{7,15},{8,0},{9,1},... | collective-permute-start | bytes 319496 | tf_op jit(solution)/shard_map/ppermute | solution.py:571
  30.9 10.9 %collective-permute-start.3 = (bf16[208,256]{1,0:T(8,128)(2,1)S(1)}, bf16[208,256]{1,0:T(8,128)(2,1)S(1)}, u32[]{:S(2)}, u32[]{:S(2)}) collective-permute-start(bf16[208,256]{1,0:T(8,128)(2,1)S(1)} %get-tuple-element.40), channel_id=1, source_target_pairs={{0,16},{16,0},{32,48},{48,32},{64,80},{80,64},{96,112},{112,96},{1... | collective-permute-start | bytes 319496 | tf_op jit(solution)/shard_map/ppermute | solution.py:572
  45.8 18.1 %all-to-all-start = ((bf16[4,69,2432]{2,1,0:T(8,128)(2,1)}), bf16[4,69,2432]{2,1,0:T(8,128)(2,1)S(1)}, u32[]{:S(2)}, u32[]{:S(2)}) async-start(bf16[4,69,2432]{2,1,0:T(8,128)(2,1)} %get-tuple-element.53), calls=%async_computation | async-start | bytes 2801664 | tf_op jit(solution)/shard_map/all_to_all | solution.py:445
  83.7 26.9 %all-to-all-start.2 = ((bf16[16,24,128]{2,1,0:T(8,128)(2,1)}), bf16[16,24,128]{2,1,0:T(8,128)(2,1)S(1)}, u32[]{:S(2)}, u32[]{:S(2)}) async-start(bf16[16,24,128]{2,1,0:T(8,128)(2,1)} %bitcast.12), calls=%async_computation.2 | async-start | bytes 196608 | tf_op jit(solution)/shard_map/all_to_all | solution.py:445
